TPU v7x, 128 devices: a whole 4x4x4 slice. The times are simulated.
128 devices in a mesh: section: 2 (over core), expert: 16 (over z, y), mp: 4 (over x).
Axes of the slice: x: 4, y: 4, z: 4, core: 2. Of those that a mesh axis runs over, the one named last changes fastest.
Arguments:
- block_input: bfloat16 [2, 16, 128, 768], P(None, 'expert'), may hold values from -6 to 6
- segments: int32 [2, 16, 128], P(None, 'expert'), may hold values from 0 to 3, never falling along the last dimension, each value on 1 to 64 neighbouring positions
- routes: int32 [2, 16, 128, 2], P(None, 'expert'), may hold values from 0 to 15, all different within a row; in each aligned block of 128 rows (0 to 127, 128 to 255, ..., all dimensions but the last counted through in order) at most 32 rows name the same one
- cotangent: bfloat16 [2, 16, 128, 768], P(None, 'expert'), may hold values from -6 to 6
- attn_gain: float32 [2, 768], P('section'), may hold values from 0.1 to 1.9
- query_weight: bfloat16 [2, 768, 768], P('section', None, 'mp'), may hold values from -0.21875 to 0.21875
- key_weight: bfloat16 [2, 768, 768], P('section', None, 'mp'), may hold values from -0.21875 to 0.21875
- value_weight: bfloat16 [2, 768, 768], P('section', None, 'mp'), may hold values from -0.21875 to 0.21875
- out_weight: bfloat16 [2, 768, 768], P('section', 'mp'), may hold values from -0.875 to 0.875
- pos_bias: float32 [2, 32, 12], P('section', None, 'mp'), may hold values from -3 to 3
- ffn_gain: float32 [2, 768], P('section'), may hold values from 0.1 to 1.9
- dense_gate: bfloat16 [768, 3072], P(None, ('section', 'mp')), may hold values from -0.21875 to 0.21875
- dense_up: bfloat16 [768, 3072], P(None, ('section', 'mp')), may hold values from -0.21875 to 0.21875
- dense_down: bfloat16 [3072, 768], P(('section', 'mp')), may hold values from -0.109375 to 0.109375
- router: bfloat16 [768, 16], replicated, may hold values from -0.15625 to 0.15625
- expert_gate: bfloat16 [16, 768, 3072], P('expert', None, ('section', 'mp')), may hold values from -0.21875 to 0.21875
- expert_up: bfloat16 [16, 768, 3072], P('expert', None, ('section', 'mp')), may hold values from -0.21875 to 0.21875
- expert_down: bfloat16 [16, 3072, 768], P('expert', ('section', 'mp')), may hold values from -0.109375 to 0.109375
Outputs:
- block_output: float32 [2, 16, 128, 768], P(None, 'expert')
- input_grad: float32 [2, 16, 128, 768], P(None, 'expert')
- grad_attn_gain: float32 [2, 768], P('section')
- grad_query: float32 [2, 768, 768], P('section', None, 'mp')
- grad_key: float32 [2, 768, 768], P('section', None, 'mp')
- grad_value: float32 [2, 768, 768], P('section', None, 'mp')
- grad_out: float32 [2, 768, 768], P('section', 'mp')
- grad_bias: float32 [2, 32, 12], P('section', None, 'mp')
- grad_ffn_gain: float32 [2, 768], P('section')
- grad_dense_gate: float32 [768, 3072], P(None, ('section', 'mp'))
- grad_dense_up: float32 [768, 3072], P(None, ('section', 'mp'))
- grad_dense_down: float32 [3072, 768], P(('section', 'mp'))
- grad_router: float32 [768, 16], replicated
- grad_expert_gate: float32 [16, 768, 3072], P('expert', None, ('section', 'mp'))
- grad_expert_up: float32 [16, 768, 3072], P('expert', None, ('section', 'mp'))
- grad_expert_down: float32 [16, 3072, 768], P('expert', ('section', 'mp'))
Inputs may be any that keep to these rules, and one draw needn't show every extreme that they name: `routes`: each token names two different experts. In the rows of one sequence of one micro-batch (aligned blocks of 128 tokens) no expert is named more than 32 times, a bound that some block reaches. `segments`: within a sequence the numbers never fall; each document (run of equal numbers) has 1 to 64 tokens, and some has exactly 64.
All inputs are finite; a program needn't handle non-finite values.
Results may differ from a plain program's by a relative error of at most 0.025.
Values may be sent and summed in bfloat16 or wider, within the bound.
A program may use at most 128 MiB of HBM per device.

v0:
```python
import jax
import jax.numpy as jnp
import numpy as np
from jax import lax
from jax.sharding import PartitionSpec as P

EPSILON = 1e-06
NEGATIVE = -1e30


def copy_for_each(shard, axis):
    devices = lax.axis_size(axis)
    return lax.all_to_all(
        jnp.broadcast_to(shard[None], (devices, *shard.shape)), axis, 0, 0, tiled=True
    )


def of_everyone(shard, axis):
    everything = copy_for_each(shard, axis)
    return jnp.sum(everything, axis=0)


def partner_2(block, axis, stride):
    count = lax.axis_size(axis)
    route = []
    for low in range(count):
        high = low | 1 << stride
        if high != low and high < count:
            route += [(low, high), (high, low)]
    return lax.ppermute(block, axis, route)


def total_of_pieces(shard, axis):
    return lax.all_gather(shard, axis).sum(0)


def of_everyone_2(shard, axis):
    return copy_for_each(shard, axis).astype(jnp.float32).sum(axis=0)


def for_sending(shard):
    return jax.tree.map(lambda a: a.astype(jnp.bfloat16) if a.dtype == jnp.float32 else a, shard)


def bucket_limits(count):
    exact = count // 2
    limits = []
    for level in range(1, count):
        if level < exact:
            limits.append(level)
        else:
            distance = exact
            while (
                min(
                    count - 1,
                    exact + int(np.floor(np.log(distance / exact) / np.log(128.0 / exact) * exact)),
                )
                < level
            ):
                distance += 1
            limits.append(distance)
    return limits


def bucket_hot(length, count):
    rows = lax.broadcasted_iota(jnp.int32, (length, length), 0)
    cols = lax.broadcasted_iota(jnp.int32, (length, length), 1)
    distance = rows - cols
    bucket = jnp.zeros((length, length), jnp.int32)
    for limit in bucket_limits(count):
        bucket = bucket + (distance >= limit).astype(jnp.int32)
    levels = lax.broadcasted_iota(jnp.int32, (length, length, count), 2)
    return (bucket[:, :, None] == levels).astype(jnp.float32)


def rms_norm(values_in, gain_row):
    return (
        values_in
        * lax.rsqrt(jnp.mean(values_in * values_in, axis=-1, keepdims=True) + EPSILON)
        * gain_row
    )


def gated_hidden(gate_in, up_in):
    return jax.nn.gelu(gate_in, approximate=True) * up_in


def matrix_product(left, right):
    return jnp.dot(left, right, preferred_element_type=jnp.float32)


def document_mask(doc_ids):
    length = doc_ids.shape[0]
    rows = lax.broadcasted_iota(jnp.int32, (length, length), 0)
    cols = lax.broadcasted_iota(jnp.int32, (length, length), 1)
    return (cols <= rows) & (doc_ids[:, None] == doc_ids[None, :])


def score_block(query_heads, key_heads, doc_mask, position_bias, score_scale):
    raw = (
        jnp.einsum("qhe,khe->hqk", query_heads, key_heads, preferred_element_type=jnp.float32)
        * score_scale
        + position_bias
    )
    return jnp.where(doc_mask[None], raw, NEGATIVE)


def route_slots(route_now, capacity, expert_ids):
    flat_ids = route_now.reshape(-1)
    flat_hot = (flat_ids[:, None] == expert_ids).astype(jnp.int32)
    ranks = (jnp.cumsum(flat_hot, axis=0) - 1) * flat_hot
    return flat_ids * capacity + jnp.sum(ranks, axis=1)


def shards(
    block_input,
    segments,
    routes,
    cotangent,
    attn_gain,
    query_weight,
    key_weight,
    value_weight,
    out_weight,
    pos_bias,
    ffn_gain,
    dense_gate,
    dense_up,
    dense_down,
    router,
    expert_gate,
    expert_up,
    expert_down,
):
    section_index = lax.axis_index("section")
    leader = lax.axis_index("mp") == 0
    micro_count = block_input.shape[0]
    length = block_input.shape[2]
    model_width = block_input.shape[3]
    expert_count = router.shape[1]
    capacity = 4 * length // expert_count
    head_count = pos_bias.shape[2]
    local_width = query_weight.shape[2]
    head_size = local_width // head_count
    score_scale = head_size ** (-0.5)
    own_query, own_key, own_value, own_out = (
        query_weight[0],
        key_weight[0],
        value_weight[0],
        out_weight[0],
    )
    gain_attn, gain_ffn = (attn_gain[0], ffn_gain[0])
    local_gate_weight, local_up_weight, own_down = (expert_gate[0], expert_up[0], expert_down[0])
    position_hot = bucket_hot(length, pos_bias.shape[1])
    position_bias = jnp.einsum(
        "qkb,bh->hqk", position_hot, pos_bias[0], precision=lax.Precision.HIGHEST
    )
    slot_pick = (jnp.arange(2, dtype=jnp.int32) == section_index).astype(jnp.float32)
    expert_ids = jnp.arange(expert_count, dtype=jnp.int32)
    zero_rows = jnp.zeros((length, model_width), jnp.float32)
    carried = zero_rows
    outputs = []
    stored = []
    for time_step in range(micro_count + 1):
        fresh_rows = block_input[min(time_step, micro_count - 1), 0].astype(jnp.float32) * (
            1.0 if time_step < micro_count else 0.0
        )
        inputs = jnp.where(section_index == 0, fresh_rows, carried)
        doc_ids = jnp.where(
            section_index == 0,
            segments[min(time_step, micro_count - 1), 0],
            segments[max(time_step - 1, 0), 0],
        )
        doc_mask = document_mask(doc_ids)
        normed = rms_norm(inputs, gain_attn).astype(jnp.bfloat16)
        query_heads = (
            matrix_product(normed, own_query)
            .astype(jnp.bfloat16)
            .reshape(length, head_count, head_size)
        )
        key_heads = (
            matrix_product(normed, own_key)
            .astype(jnp.bfloat16)
            .reshape(length, head_count, head_size)
        )
        value_heads = (
            matrix_product(normed, own_value)
            .astype(jnp.bfloat16)
            .reshape(length, head_count, head_size)
        )
        scores = score_block(query_heads, key_heads, doc_mask, position_bias, score_scale)
        peak = jnp.max(scores, axis=-1, keepdims=True)
        log_total = peak + jnp.log(jnp.sum(jnp.exp(scores - peak), axis=-1, keepdims=True))
        attn_probs = jnp.exp(scores - log_total).astype(jnp.bfloat16)
        head_mix = jnp.einsum(
            "hqk,khe->qhe", attn_probs, value_heads, preferred_element_type=jnp.float32
        )
        head_mix = head_mix.astype(jnp.bfloat16).reshape(length, local_width)
        branch = of_everyone(matrix_product(head_mix, own_out), "mp")
        hidden_in = inputs + branch
        normed_ffn = rms_norm(hidden_in, gain_ffn).astype(jnp.bfloat16)
        partner = partner_2(normed_ffn, "section", 0)
        dense_rows = jnp.where(section_index == 0, normed_ffn, partner)
        moe_rows = jnp.where(section_index == 0, partner, normed_ffn)
        gate_pre = matrix_product(dense_rows, dense_gate)
        up_pre = matrix_product(dense_rows, dense_up)
        dense_hid = gated_hidden(gate_pre, up_pre).astype(jnp.bfloat16)
        dense_part = matrix_product(dense_hid, dense_down)
        route_now = routes[max(time_step - 1, 0), 0]
        route_hot = (route_now[:, :, None] == expert_ids).astype(jnp.float32)
        logits = matrix_product(moe_rows, router)
        chosen = jnp.sum(route_hot * logits[:, None, :], axis=-1)
        gate_probs = jax.nn.softmax(chosen, axis=-1)
        slot_ids = route_slots(route_now, capacity, expert_ids)
        send_rows = jnp.zeros((expert_count * capacity, model_width), jnp.bfloat16)
        send_rows = (
            send_rows.at[slot_ids]
            .set(jnp.repeat(moe_rows, 2, axis=0))
            .reshape(expert_count, capacity, model_width)
        )
        received_rows = lax.all_to_all(
            send_rows, "expert", split_axis=0, concat_axis=0, tiled=True
        ).reshape(-1, model_width)
        expert_gate_preact = matrix_product(received_rows, local_gate_weight)
        expert_up_preact = matrix_product(received_rows, local_up_weight)
        expert_hidden_rows = gated_hidden(expert_gate_preact, expert_up_preact).astype(jnp.bfloat16)
        expert_terms = matrix_product(expert_hidden_rows, own_down).reshape(
            expert_count, capacity, model_width
        )
        returned = (
            lax.all_to_all(
                expert_terms.astype(jnp.bfloat16), "expert", split_axis=0, concat_axis=0, tiled=True
            )
            .astype(expert_terms.dtype)
            .reshape(-1, model_width)
        )
        picked = returned[slot_ids].reshape(length, 2, model_width)
        moe_part = jnp.sum(gate_probs[:, :, None] * picked, axis=1)
        stacked = (
            jnp.stack([dense_part, moe_part])
            + slot_pick[:, None, None] * jnp.where(leader, hidden_in, 0.0)[None]
        )
        layer_sums = total_of_pieces(stacked, ("section", "mp"))
        carried = layer_sums[0]
        if time_step >= 1:
            outputs.append(layer_sums[1])
        expert_saved_state = (
            received_rows,
            expert_gate_preact,
            expert_up_preact,
            expert_hidden_rows,
        )
        stored.append(
            (
                inputs,
                doc_mask,
                normed,
                query_heads,
                key_heads,
                value_heads,
                log_total,
                head_mix,
                hidden_in,
                dense_rows,
                gate_pre,
                up_pre,
                dense_hid,
                moe_rows,
                route_hot,
                gate_probs,
                slot_ids,
                picked,
                expert_saved_state,
            )
        )
    carried_grad = zero_rows
    input_grads = [zero_rows] * micro_count
    weight_grads = None
    expert_grads = None
    for back_step in range(micro_count + 1):
        time_step = micro_count - back_step
        (
            inputs,
            doc_mask,
            normed,
            query_heads,
            key_heads,
            value_heads,
            log_total,
            head_mix,
            hidden_in,
            dense_rows,
            gate_pre,
            up_pre,
            dense_hid,
            moe_rows,
            route_hot,
            gate_probs,
            slot_ids,
            picked,
            expert_saved_state,
        ) = stored[time_step]
        grad_dense = carried_grad
        if back_step < micro_count:
            grad_moe = cotangent[micro_count - 1 - back_step, 0].astype(jnp.float32)
        else:
            grad_moe = zero_rows
        dense_out_grad = grad_dense.astype(jnp.bfloat16)
        hid_grad = matrix_product(dense_out_grad, dense_down.T)
        step_down = matrix_product(dense_hid.T, dense_out_grad)
        unused_value, gated_back = jax.vjp(gated_hidden, gate_pre, up_pre)
        gate_grad, up_grad = gated_back(hid_grad)
        gate_grad = gate_grad.astype(jnp.bfloat16)
        up_grad = up_grad.astype(jnp.bfloat16)
        step_gate = matrix_product(dense_rows.T, gate_grad)
        step_up = matrix_product(dense_rows.T, up_grad)
        dense_rows_grad = matrix_product(gate_grad, dense_gate.T) + matrix_product(
            up_grad, dense_up.T
        )
        gate_terms = jnp.sum(grad_moe[:, None, :] * picked, axis=-1)
        out_grad = (
            (gate_probs[:, :, None] * grad_moe[:, None, :])
            .astype(jnp.bfloat16)
            .reshape(-1, model_width)
        )
        grad_send = jnp.zeros((expert_count * capacity, model_width), jnp.bfloat16)
        grad_send = (
            grad_send.at[slot_ids].set(out_grad).reshape(expert_count, capacity, model_width)
        )
        received_rows, expert_gate_preact, expert_up_preact, expert_hidden_rows = expert_saved_state
        grad_arrived = lax.all_to_all(
            grad_send, "expert", split_axis=0, concat_axis=0, tiled=True
        ).reshape(-1, model_width)
        expert_hidden_gradient = matrix_product(grad_arrived, own_down.T)
        current_expert_down = matrix_product(expert_hidden_rows.T, grad_arrived)
        unused_value, expert_backward_pass = jax.vjp(
            gated_hidden, expert_gate_preact, expert_up_preact
        )
        expert_gate_gradient, expert_up_gradient = expert_backward_pass(expert_hidden_gradient)
        expert_gate_gradient = expert_gate_gradient.astype(jnp.bfloat16)
        expert_up_gradient = expert_up_gradient.astype(jnp.bfloat16)
        current_expert_gate = matrix_product(received_rows.T, expert_gate_gradient)
        current_expert_up = matrix_product(received_rows.T, expert_up_gradient)
        received_gradient = (
            matrix_product(expert_gate_gradient, local_gate_weight.T)
            + matrix_product(expert_up_gradient, local_up_weight.T)
        ).reshape(expert_count, capacity, model_width)
        returned_grad = (
            lax.all_to_all(
                received_gradient.astype(jnp.bfloat16),
                "expert",
                split_axis=0,
                concat_axis=0,
                tiled=True,
            )
            .astype(received_gradient.dtype)
            .reshape(-1, model_width)
        )
        moe_rows_grad = jnp.sum(returned_grad[slot_ids].reshape(length, 2, model_width), axis=1)
        summed, gate_total = (
            of_everyone_2(
                jnp.stack([dense_rows_grad, moe_rows_grad]).astype(jnp.bfloat16), ("section", "mp")
            ).astype(jnp.float32),
            of_everyone_2(gate_terms.astype(jnp.bfloat16), ("section", "mp")).astype(jnp.float32),
        )
        choice_grad = gate_probs * (
            gate_total - jnp.sum(gate_probs * gate_total, axis=-1, keepdims=True)
        )
        logit_grad = jnp.sum(choice_grad[:, :, None] * route_hot, axis=1)
        step_router = jnp.dot(
            moe_rows.astype(jnp.float32).T, logit_grad, precision=lax.Precision.HIGHEST
        )
        moe_total = summed[1] + jnp.dot(
            logit_grad, router.astype(jnp.float32).T, precision=lax.Precision.HIGHEST
        )
        own_grad = jnp.where(section_index == 0, summed[0], moe_total)
        out_grad_own = jnp.where(section_index == 0, grad_dense, grad_moe)
        unused_value, norm_back = jax.vjp(rms_norm, hidden_in, gain_ffn)
        hidden_grad, step_ffn_gain = norm_back(own_grad)
        hidden_grad = hidden_grad + out_grad_own
        hidden_low = hidden_grad.astype(jnp.bfloat16)
        step_wout = matrix_product(head_mix.T, hidden_low)
        mix_grad = (
            matrix_product(hidden_low, own_out.T)
            .astype(jnp.bfloat16)
            .reshape(length, head_count, head_size)
        )
        scores = score_block(query_heads, key_heads, doc_mask, position_bias, score_scale)
        prob_full = jnp.exp(scores - log_total)
        attn_probs = prob_full.astype(jnp.bfloat16)
        value_grad = jnp.einsum(
            "hqk,qhe->khe", attn_probs, mix_grad, preferred_element_type=jnp.float32
        ).astype(jnp.bfloat16)
        prob_grad = jnp.einsum(
            "qhe,khe->hqk", mix_grad, value_heads, preferred_element_type=jnp.float32
        )
        score_grad = (
            prob_full * (prob_grad - jnp.sum(prob_grad * prob_full, axis=-1, keepdims=True))
        ).astype(jnp.bfloat16)
        step_table = jnp.einsum(
            "hqk,qkb->bh",
            score_grad.astype(jnp.float32),
            position_hot,
            precision=lax.Precision.HIGHEST,
        )
        query_grad = (
            (
                jnp.einsum(
                    "hqk,khe->qhe", score_grad, key_heads, preferred_element_type=jnp.float32
                )
                * score_scale
            )
            .astype(jnp.bfloat16)
            .reshape(length, local_width)
        )
        key_grad = (
            (
                jnp.einsum(
                    "hqk,qhe->khe", score_grad, query_heads, preferred_element_type=jnp.float32
                )
                * score_scale
            )
            .astype(jnp.bfloat16)
            .reshape(length, local_width)
        )
        value_grad = value_grad.reshape(length, local_width)
        step_wquery = matrix_product(normed.T, query_grad)
        step_wkey = matrix_product(normed.T, key_grad)
        step_wvalue = matrix_product(normed.T, value_grad)
        normed_grad = (
            matrix_product(query_grad, own_query.T)
            + matrix_product(key_grad, own_key.T)
            + matrix_product(value_grad, own_value.T)
        )
        unused_value, attn_back = jax.vjp(rms_norm, inputs, gain_attn)
        input_part, gain_part = attn_back(normed_grad)
        input_part = input_part + jnp.where(leader, hidden_grad, 0.0)
        both_inputs, gain_both = (
            of_everyone_2(
                (slot_pick[:, None, None] * input_part[None]).astype(jnp.bfloat16),
                ("section", "mp"),
            ).astype(jnp.float32),
            of_everyone_2(
                (slot_pick[:, None] * gain_part[None]).astype(jnp.bfloat16), ("section", "mp")
            ).astype(jnp.float32),
        )
        carried_grad = both_inputs[1]
        if back_step >= 1:
            input_grads[time_step] = both_inputs[0]
        step_attn_gain = jnp.sum(slot_pick[:, None] * gain_both, axis=0)
        step_grads = (
            step_attn_gain,
            step_wquery,
            step_wkey,
            step_wvalue,
            step_wout,
            step_table,
            step_ffn_gain,
            step_gate,
            step_up,
            step_down,
            step_router,
        )
        current_expert_weights = (current_expert_gate, current_expert_up, current_expert_down)
        if weight_grads is None:
            weight_grads = step_grads
            expert_grads = current_expert_weights
        else:
            weight_grads = jax.tree.map(jnp.add, weight_grads, step_grads)
            expert_grads = jax.tree.map(jnp.add, expert_grads, current_expert_weights)
    weight_grads = jax.tree.map(
        lambda part: part.astype(jnp.float32), lax.psum(for_sending(weight_grads), "expert")
    )
    block_output = jnp.stack(outputs)[:, None]
    input_grad = jnp.stack(input_grads)[:, None]
    return (
        block_output,
        input_grad,
        weight_grads[0][None],
        weight_grads[1][None],
        weight_grads[2][None],
        weight_grads[3][None],
        weight_grads[4][None],
        weight_grads[5][None],
        weight_grads[6][None],
        weight_grads[7],
        weight_grads[8],
        weight_grads[9],
        weight_grads[10],
        expert_grads[0][None],
        expert_grads[1][None],
        expert_grads[2][None],
    )


def solution(mesh):
    placed = (
        P(None, "expert", None, None),
        P(None, "expert", None),
        P(None, "expert", None, None),
        P(None, "expert", None, None),
        P("section", None),
        P("section", None, "mp"),
        P("section", None, "mp"),
        P("section", None, "mp"),
        P("section", "mp", None),
        P("section", None, "mp"),
        P("section", None),
        P(None, ("section", "mp")),
        P(None, ("section", "mp")),
        P(("section", "mp"), None),
        P(),
        P("expert", None, ("section", "mp")),
        P("expert", None, ("section", "mp")),
        P("expert", ("section", "mp"), None),
    )
    return jax.shard_map(
        shards,
        mesh=mesh,
        in_specs=placed,
        out_specs=(
            P(None, "expert", None, None),
            P(None, "expert", None, None),
            P("section", None),
            P("section", None, "mp"),
            P("section", None, "mp"),
            P("section", None, "mp"),
            P("section", "mp", None),
            P("section", None, "mp"),
            P("section", None),
            P(None, ("section", "mp")),
            P(None, ("section", "mp")),
            P(("section", "mp"), None),
            P(),
            P("expert", None, ("section", "mp")),
            P("expert", None, ("section", "mp")),
            P("expert", ("section", "mp"), None),
        ),
        check_vma=False,
    )
```

profile of v0, /device:TPU:0, one launch (start us, length us, event | category | flops | bytes accessed | tf_op | source)
XLA Modules:
  0.0 903.7 jit_solution(17281873312852533071)
XLA Ops:
  16.3 4.5 all-to-all-start
  23.0 18.5 %all-to-all-done = f32[4,128,768]{2,1,0:T(8,128)S(1)} async-done(((f32[4,128,768]{2,1,0:T(8,128)}), f32[4,128,768]{2,1,0:T(8,128)S(1)}, u32[]{:S(2)}, u32[]{:S(2)}) %all-to-all-start) | async-done | bytes 1572896 | tf_op jit(solution)/shard_map/all_to_all | solution.py:13
  47.4 8.0 all-to-all-start.1
  58.7 11.4 %all-to-all-done.1 = bf16[16,32,768]{2,1,0:T(8,128)(2,1)S(1)} async-done(((bf16[16,32,768]{2,1,0:T(8,128)(2,1)}), bf16[16,32,768]{2,1,0:T(8,128)(2,1)S(1)}, u32[]{:S(2)}, u32[]{:S(2)}) %all-to-all-start.1) | async-done | bytes 786464 | tf_op jit(solution)/shard_map/all_to_all | solution.py:221
  70.1 4.4 all-to-all-start.19
  77.5 10.6 %all-to-all-done.19 = bf16[16,32,768]{2,1,0:T(8,128)(2,1)} async-done(((bf16[16,32,768]{2,1,0:T(8,128)(2,1)}), bf16[16,32,768]{2,1,0:T(8,128)(2,1)}, u32[]{:S(2)}, u32[]{:S(2)}) %all-to-all-start.19) | async-done | bytes 786464 | tf_op jit(solution)/shard_map/all_to_all | solution.py:331
  88.1 3.5 multiply_convert_fusion.1
  93.9 4.4 all-to-all-start.2
  101.2 9.8 %all-to-all-done.2 = bf16[16,32,768]{2,1,0:T(8,128)(2,1)} async-done(((bf16[16,32,768]{2,1,0:T(8,128)(2,1)}), bf16[16,32,768]{2,1,0:T(8,128)(2,1)}, u32[]{:S(2)}, u32[]{:S(2)}) %all-to-all-start.2) | async-done | bytes 786464 | tf_op jit(solution)/shard_map/all_to_all | solution.py:231
  119.0 36.6 %all-gather.4.cloned.1.call-done = f32[8,2,128,768]{3,2,1,0:T(8,128)} async-done(((f32[1,2,128,768]{3,2,1,0:T(8,128)}), f32[8,2,128,768]{3,2,1,0:T(8,128)}) %all-gather.4.cloned.1.call-update) | async-done | bytes 6291472 | tf_op jit(solution)/shard_map/all_gather | solution.py:34
  155.6 4.1 reduce_sum.705
  164.6 24.6 %all_to_all.135 = f32[4,128,768]{2,1,0:T(8,128)} all-to-all(f32[4,128,768]{2,1,0:T(8,128)S(1)} %broadcast_in_dim.141), channel_id=1, replica_groups=mesh['section'=2,'expert'=16,'mp'=4] {'mp'}, dimensions={0} | all-to-all | bytes 3145728 | tf_op jit(solution)/shard_map/all_to_all | solution.py:13
  193.9 3.0 scatter_custom_fusion.1
  197.0 7.0 all-to-all-start.4
  211.1 3.2 scatter_custom_fusion.4
  214.3 4.3 all-to-all-done.4
  218.6 4.6 all-to-all-start.14
  226.1 10.7 %all-to-all-done.14 = bf16[16,32,768]{2,1,0:T(8,128)(2,1)} async-done(((bf16[16,32,768]{2,1,0:T(8,128)(2,1)}), bf16[16,32,768]{2,1,0:T(8,128)(2,1)}, u32[]{:S(2)}, u32[]{:S(2)}) %all-to-all-start.14) | async-done | bytes 786464 | tf_op jit(solution)/shard_map/all_to_all | solution.py:331
  236.8 3.5 multiply_convert_fusion.3
  242.5 4.4 all-to-all-start.5
  251.2 8.4 all-to-all-done.5
  267.8 36.7 %all-gather.6.cloned.1.call-done = f32[8,2,128,768]{3,2,1,0:T(8,128)} async-done(((f32[1,2,128,768]{3,2,1,0:T(8,128)}), f32[8,2,128,768]{3,2,1,0:T(8,128)}) %all-gather.6.cloned.1.call-update) | async-done | bytes 6291472 | tf_op jit(solution)/shard_map/all_gather | solution.py:34
  304.5 4.1 reduce_sum.714
  315.2 3.6 all-to-all-start.6
  330.4 9.8 %all-to-all-done.6 = f32[4,128,768]{2,1,0:T(8,128)S(1)} async-done(((f32[4,128,768]{2,1,0:T(8,128)}), f32[4,128,768]{2,1,0:T(8,128)S(1)}, u32[]{:S(2)}, u32[]{:S(2)}) %all-to-all-start.6) | async-done | bytes 1572896 | tf_op jit(solution)/shard_map/all_to_all | solution.py:13
  346.4 3.0 scatter_custom_fusion.2
  349.4 7.2 all-to-all-start.7
  361.4 3.3 scatter_custom_fusion.3
  364.7 6.5 all-to-all-done.7
  371.3 4.3 all-to-all-start.9
  379.1 10.1 %all-to-all-done.9 = bf16[16,32,768]{2,1,0:T(8,128)(2,1)} async-done(((bf16[16,32,768]{2,1,0:T(8,128)(2,1)}), bf16[16,32,768]{2,1,0:T(8,128)(2,1)}, u32[]{:S(2)}, u32[]{:S(2)}) %all-to-all-start.9) | async-done | bytes 786464 | tf_op jit(solution)/shard_map/all_to_all | solution.py:331
  389.1 3.4 multiply_convert_fusion.6
  394.9 4.4 all-to-all-start.10
  402.1 9.9 %all-to-all-done.10 = bf16[16,32,768]{2,1,0:T(8,128)(2,1)} async-done(((bf16[16,32,768]{2,1,0:T(8,128)(2,1)}), bf16[16,32,768]{2,1,0:T(8,128)(2,1)}, u32[]{:S(2)}, u32[]{:S(2)}) %all-to-all-start.10) | async-done | bytes 786464 | tf_op jit(solution)/shard_map/all_to_all | solution.py:349
  412.0 4.7 all-to-all-start.8
  433.6 3.0 multiply_reduce_fusion.2
  438.0 3.3 all-to-all-start.12
  441.4 5.0 all-to-all-done.12
  448.4 4.6 all-to-all-start.11
  455.5 35.3 %all-to-all-done.11 = bf16[8,2,128,768]{3,2,1,0:T(8,128)(2,1)} async-done(((bf16[8,2,128,768]{3,2,1,0:T(8,128)(2,1)}), bf16[8,2,128,768]{3,2,1,0:T(8,128)(2,1)}, u32[]{:S(2)}, u32[]{:S(2)}) %all-to-all-start.11) | async-done | bytes 3145760 | tf_op jit(solution)/shard_map/all_to_all | solution.py:13
  490.8 4.8 all-to-all-start.15
  503.0 7.2 all-to-all-done.15
  512.2 4.7 all-to-all-start.13
  527.6 27.3 %all-to-all-done.13 = bf16[8,2,128,768]{3,2,1,0:T(8,128)(2,1)} async-done(((bf16[8,2,128,768]{3,2,1,0:T(8,128)(2,1)}), bf16[8,2,128,768]{3,2,1,0:T(8,128)(2,1)}, u32[]{:S(2)}, u32[]{:S(2)}) %all-to-all-start.13) | async-done | bytes 3145760 | tf_op jit(solution)/shard_map/all_to_all | solution.py:13
  554.9 3.6 all-to-all-start.20
  563.8 9.6 %all-to-all-done.20 = bf16[16,32,768]{2,1,0:T(8,128)(2,1)S(1)} async-done(((bf16[16,32,768]{2,1,0:T(8,128)(2,1)}), bf16[16,32,768]{2,1,0:T(8,128)(2,1)S(1)}, u32[]{:S(2)}, u32[]{:S(2)}) %all-to-all-start.20) | async-done | bytes 786464 | tf_op jit(solution)/shard_map/all_to_all | solution.py:349
  574.6 3.8 all-to-all-start.22
  580.5 3.1 all-to-all-done.22
  584.9 3.3 all-to-all-start.17
  589.3 4.0 all-to-all-done.17
  595.2 4.4 all-to-all-start.16
  623.2 14.3 %all-to-all-done.16 = bf16[8,2,128,768]{3,2,1,0:T(8,128)(2,1)} async-done(((bf16[8,2,128,768]{3,2,1,0:T(8,128)(2,1)}), bf16[8,2,128,768]{3,2,1,0:T(8,128)(2,1)}, u32[]{:S(2)}, u32[]{:S(2)}) %all-to-all-start.16) | async-done | bytes 3145760 | tf_op jit(solution)/shard_map/all_to_all | solution.py:13
  646.8 4.6 all-to-all-start.18
  668.4 41.1 %all-to-all-done.18 = bf16[8,2,128,768]{3,2,1,0:T(8,128)(2,1)} async-done(((bf16[8,2,128,768]{3,2,1,0:T(8,128)(2,1)}), bf16[8,2,128,768]{3,2,1,0:T(8,128)(2,1)}, u32[]{:S(2)}, u32[]{:S(2)}) %all-to-all-start.18) | async-done | bytes 3145760 | tf_op jit(solution)/shard_map/all_to_all | solution.py:13
  715.5 5.8 all-to-all-start.21
  731.8 27.4 %all-to-all-done.21 = bf16[8,2,128,768]{3,2,1,0:T(8,128)(2,1)} async-done(((bf16[8,2,128,768]{3,2,1,0:T(8,128)(2,1)}), bf16[8,2,128,768]{3,2,1,0:T(8,128)(2,1)}, u32[]{:S(2)}, u32[]{:S(2)}) %all-to-all-start.21) | async-done | bytes 3145760 | tf_op jit(solution)/shard_map/all_to_all | solution.py:13
  765.8 3.3 all-to-all-start.26
  775.0 3.3 all-to-all-start.25
  779.4 4.2 all-to-all-done.25
  784.2 3.3 all-to-all-start.24
  788.6 4.2 all-to-all-done.24
  794.8 4.9 all-to-all-start.23
  808.0 3.4 reduce_sum.725
  813.1 69.9 %all-reduce = (bf16[1,32,3]{1,2,0:T(4,128)(2,1)S(1)}, bf16[1,768]{1,0:T(2,128)(2,1)S(1)}, bf16[1,768]{1,0:T(2,128)(2,1)S(1)}, bf16[768,16]{0,1:T(8,128)(2,1)S(1)}) all-reduce(bf16[1,32,3]{1,2,0:T(4,128)(2,1)S(1)} %fusion.49, bf16[1,768]{1,0:T(2,128)(2,1)S(1)} %broadcast_in_dim.166, ...), channel_id=1, replica_groups=mesh['section'=2,'expert'=16,'mp'=4] {'expert'}, use_global_device_ids=true, to_apply=%region_86.87 | all-reduce | flops 13920 | bytes 55680 | tf_op jit(solution)/shard_map/psum | solution.py:472
  (918 shorter events, 268.2 us)
Async XLA Ops:
  7.2 80.9 %copy-start = (bf16[1,384,768]{2,1,0:T(8,128)(2,1)S(1)}, bf16[1,384,768]{2,1,0:T(8,128)(2,1)}, u32[]{:S(2)}) copy-start(bf16[1,384,768]{2,1,0:T(8,128)(2,1)} %param.35) | copy-start | bytes 1769476
  16.3 25.2 %all-to-all-start = ((f32[4,128,768]{2,1,0:T(8,128)}), f32[4,128,768]{2,1,0:T(8,128)S(1)}, u32[]{:S(2)}, u32[]{:S(2)}) async-start(f32[4,128,768]{2,1,0:T(8,128)} %broadcast_in_dim.138), calls=%async_computation | async-start | bytes 3145728 | tf_op jit(solution)/shard_map/all_to_all | solution.py:13
  21.4 188.2 %copy-start.244 = (s32[128,2]{0,1:T(2,128)}, s32[128,2]{0,1:T(2,128)S(1)}, u32[]{:S(2)}) copy-start(s32[128,2]{0,1:T(2,128)S(1)} %get-tuple-element.199) | copy-start | bytes 3076
  42.7 1.5 collective-permute-start
  42.8 31.7 %copy-start.266 = (s32[256,1]{0,1:T(1,128)}, s32[256,1]{0,1:T(1,128)S(1)}, u32[]{:S(2)}) copy-start(s32[256,1]{0,1:T(1,128)S(1)} %compare_select_fusion.1) | copy-start | bytes 3076
  44.4 54.8 %copy-start.70 = (bf16[128,768]{1,0:T(8,128)(2,1)}, bf16[128,768]{1,0:T(8,128)(2,1)S(1)}, u32[]{:S(2)}) copy-start(bf16[128,768]{1,0:T(8,128)(2,1)S(1)} %get-tuple-element.196) | copy-start | bytes 589828
  47.4 22.7 %all-to-all-start.1 = ((bf16[16,32,768]{2,1,0:T(8,128)(2,1)}), bf16[16,32,768]{2,1,0:T(8,128)(2,1)S(1)}, u32[]{:S(2)}, u32[]{:S(2)}) async-start(bf16[16,32,768]{2,1,0:T(8,128)(2,1)} %bitcast.19), calls=%async_computation.1 | async-start | bytes 1572864 | tf_op jit(solution)/shard_map/all_to_all | solution.py:221
  55.5 19.1 %copy-start.3 = (bf16[1,768,384]{2,1,0:T(8,128)(2,1)S(1)}, bf16[1,768,384]{2,1,0:T(8,128)(2,1)}, u32[]{:S(2)}) copy-start(bf16[1,768,384]{2,1,0:T(8,128)(2,1)} %param.33) | copy-start | bytes 1769476
  55.7 43.1 %copy-start.242 = (f32[128,2]{0,1:T(2,128)}, f32[128,2]{0,1:T(2,128)S(1)}, u32[]{:S(2)}) copy-start(f32[128,2]{0,1:T(2,128)S(1)} %get-tuple-element.161) | copy-start | bytes 3076
  70.1 18.0 %all-to-all-start.19 = ((bf16[16,32,768]{2,1,0:T(8,128)(2,1)}), bf16[16,32,768]{2,1,0:T(8,128)(2,1)}, u32[]{:S(2)}, u32[]{:S(2)}) async-start(bf16[16,32,768]{2,1,0:T(8,128)(2,1)} %bitcast.632), calls=%async_computation.19 | async-start | bytes 1572864 | tf_op jit(solution)/shard_map/all_to_all | solution.py:331
  74.6 37.7 %copy-start.245 = (s32[1024]{0:T(1024)}, s32[1024]{0:T(1024)S(1)}, u32[]{:S(2)}) copy-start(s32[1024]{0:T(1024)S(1)} %pad_clamp_fusion.1) | copy-start | bytes 12292
  93.9 17.1 %all-to-all-start.2 = ((bf16[16,32,768]{2,1,0:T(8,128)(2,1)}), bf16[16,32,768]{2,1,0:T(8,128)(2,1)}, u32[]{:S(2)}, u32[]{:S(2)}) async-start(bf16[16,32,768]{2,1,0:T(8,128)(2,1)} %convolution_convert_fusion.2), calls=%async_computation.2 | async-start | bytes 1572864 | tf_op jit(solution)/shard_map/all_to_all | solution.py:231
  98.3 57.4 %all-gather.4.cloned.1.call-start = ((), (), s32[]{:S(2)}) async-start(), calls=%async_computation.27 | async-start | bytes 7077888 | tf_op jit(solution)/shard_map/all_gather | solution.py:34
  98.8 167.9 %copy-start.233 = (f32[2]{0:T(128)}, f32[2]{0:T(128)S(1)}, u32[]{:S(2)}) copy-start(f32[2]{0:T(128)S(1)} %compare_convert_fusion) | copy-start | bytes 28
  119.0 40.8 %copy-start.14 = (bf16[2,1,128,768]{3,2,1,0:T(8,128)(2,1)S(1)}, bf16[2,1,128,768]{3,2,1,0:T(8,128)(2,1)}, u32[]{:S(2)}) copy-start(bf16[2,1,128,768]{3,2,1,0:T(8,128)(2,1)} %param.18) | copy-start | bytes 1179652
  164.0 25.2 %copy-start.228 = (f32[3,128]{1,0:T(4,128)}, f32[3,128]{1,0:T(4,128)S(1)}, u32[]{:S(2)}) copy-start(f32[3,128]{1,0:T(4,128)S(1)} %log_add_fusion.1) | copy-start | bytes 4612
  164.2 25.0 %copy-start.163 = (bf16[3,64,128]{2,1,0:T(8,128)(2,1)}, bf16[3,64,128]{2,1,0:T(8,128)(2,1)S(1)}, u32[]{:S(2)}) copy-start(bf16[3,64,128]{2,1,0:T(8,128)(2,1)S(1)} %convolution_convert_fusion.7) | copy-start | bytes 147460
  191.1 1.5 collective-permute-start.1
  192.8 16.7 %copy-start.97 = (bf16[128,768]{1,0:T(8,128)(2,1)}, bf16[128,768]{1,0:T(8,128)(2,1)S(1)}, u32[]{:S(2)}) copy-start(bf16[128,768]{1,0:T(8,128)(2,1)S(1)} %get-tuple-element.195) | copy-start | bytes 589828
  192.8 56.4 %copy-start.72 = (bf16[128,768]{1,0:T(8,128)(2,1)}, bf16[128,768]{1,0:T(8,128)(2,1)S(1)}, u32[]{:S(2)}) copy-start(bf16[128,768]{1,0:T(8,128)(2,1)S(1)} %get-tuple-element.194) | copy-start | bytes 589828
  197.0 21.6 %all-to-all-start.4 = ((bf16[16,32,768]{2,1,0:T(8,128)(2,1)}), bf16[16,32,768]{2,1,0:T(8,128)(2,1)S(1)}, u32[]{:S(2)}, u32[]{:S(2)}) async-start(bf16[16,32,768]{2,1,0:T(8,128)(2,1)} %bitcast.628), calls=%async_computation.4 | async-start | bytes 1572864 | tf_op jit(solution)/shard_map/all_to_all | solution.py:221
  218.6 18.2 %all-to-all-start.14 = ((bf16[16,32,768]{2,1,0:T(8,128)(2,1)}), bf16[16,32,768]{2,1,0:T(8,128)(2,1)}, u32[]{:S(2)}, u32[]{:S(2)}) async-start(bf16[16,32,768]{2,1,0:T(8,128)(2,1)} %bitcast.631), calls=%async_computation.14 | async-start | bytes 1572864 | tf_op jit(solution)/shard_map/all_to_all | solution.py:331
  242.5 17.1 %all-to-all-start.5 = ((bf16[16,32,768]{2,1,0:T(8,128)(2,1)}), bf16[16,32,768]{2,1,0:T(8,128)(2,1)}, u32[]{:S(2)}, u32[]{:S(2)}) async-start(bf16[16,32,768]{2,1,0:T(8,128)(2,1)} %convolution_convert_fusion.1), calls=%async_computation.5 | async-start | bytes 1572864 | tf_op jit(solution)/shard_map/all_to_all | solution.py:231
  246.9 57.6 %all-gather.6.cloned.1.call-start = ((), (), s32[]{:S(2)}) async-start(), calls=%async_computation.28 | async-start | bytes 7077888 | tf_op jit(solution)/shard_map/all_gather | solution.py:34
  267.8 40.9 %copy-start.16 = (bf16[2,1,128,768]{3,2,1,0:T(8,128)(2,1)S(1)}, bf16[2,1,128,768]{3,2,1,0:T(8,128)(2,1)}, u32[]{:S(2)}) copy-start(bf16[2,1,128,768]{3,2,1,0:T(8,128)(2,1)} %param.18) | copy-start | bytes 1179652
  315.2 25.0 %all-to-all-start.6 = ((f32[4,128,768]{2,1,0:T(8,128)}), f32[4,128,768]{2,1,0:T(8,128)S(1)}, u32[]{:S(2)}, u32[]{:S(2)}) async-start(f32[4,128,768]{2,1,0:T(8,128)} %broadcast_in_dim.144), calls=%async_computation.6 | async-start | bytes 3145728 | tf_op jit(solution)/shard_map/all_to_all | solution.py:13
  342.9 1.5 collective-permute-start.2
  349.4 21.8 %all-to-all-start.7 = ((bf16[16,32,768]{2,1,0:T(8,128)(2,1)}), bf16[16,32,768]{2,1,0:T(8,128)(2,1)S(1)}, u32[]{:S(2)}, u32[]{:S(2)}) async-start(bf16[16,32,768]{2,1,0:T(8,128)(2,1)} %bitcast.629), calls=%async_computation.7 | async-start | bytes 1572864 | tf_op jit(solution)/shard_map/all_to_all | solution.py:221
  371.3 17.9 %all-to-all-start.9 = ((bf16[16,32,768]{2,1,0:T(8,128)(2,1)}), bf16[16,32,768]{2,1,0:T(8,128)(2,1)}, u32[]{:S(2)}, u32[]{:S(2)}) async-start(bf16[16,32,768]{2,1,0:T(8,128)(2,1)} %bitcast.630), calls=%async_computation.9 | async-start | bytes 1572864 | tf_op jit(solution)/shard_map/all_to_all | solution.py:331
  394.9 17.1 %all-to-all-start.10 = ((bf16[16,32,768]{2,1,0:T(8,128)(2,1)}), bf16[16,32,768]{2,1,0:T(8,128)(2,1)}, u32[]{:S(2)}, u32[]{:S(2)}) async-start(bf16[16,32,768]{2,1,0:T(8,128)(2,1)} %bitcast.633), calls=%async_computation.10 | async-start | bytes 1572864 | tf_op jit(solution)/shard_map/all_to_all | solution.py:349
  412.0 16.5 %all-to-all-start.8 = ((bf16[16,32,768]{2,1,0:T(8,128)(2,1)}), bf16[16,32,768]{2,1,0:T(8,128)(2,1)}, u32[]{:S(2)}, u32[]{:S(2)}) async-start(bf16[16,32,768]{2,1,0:T(8,128)(2,1)} %convolution_convert_fusion), calls=%async_computation.8 | async-start | bytes 1572864 | tf_op jit(solution)/shard_map/all_to_all | solution.py:231
  438.0 8.4 all-to-all-start.12
  448.4 42.4 %all-to-all-start.11 = ((bf16[8,2,128,768]{3,2,1,0:T(8,128)(2,1)}), bf16[8,2,128,768]{3,2,1,0:T(8,128)(2,1)}, u32[]{:S(2)}, u32[]{:S(2)}) async-start(bf16[8,2,128,768]{3,2,1,0:T(8,128)(2,1)} %broadcast_in_dim.147), calls=%async_computation.11 | async-start | bytes 6291456 | tf_op jit(solution)/shard_map/all_to_all | solution.py:13
  490.8 19.5 %all-to-all-start.15 = ((bf16[16,32,768]{2,1,0:T(8,128)(2,1)}), bf16[16,32,768]{2,1,0:T(8,128)(2,1)S(1)}, u32[]{:S(2)}, u32[]{:S(2)}) async-start(bf16[16,32,768]{2,1,0:T(8,128)(2,1)} %bitcast.88), calls=%async_computation.15 | async-start | bytes 1572864 | tf_op jit(solution)/shard_map/all_to_all | solution.py:349
  512.2 42.6 %all-to-all-start.13 = ((bf16[8,2,128,768]{3,2,1,0:T(8,128)(2,1)}), bf16[8,2,128,768]{3,2,1,0:T(8,128)(2,1)}, u32[]{:S(2)}, u32[]{:S(2)}) async-start(bf16[8,2,128,768]{3,2,1,0:T(8,128)(2,1)} %broadcast_in_dim.151), calls=%async_computation.13 | async-start | bytes 6291456 | tf_op jit(solution)/shard_map/all_to_all | solution.py:13
  554.9 18.5 %all-to-all-start.20 = ((bf16[16,32,768]{2,1,0:T(8,128)(2,1)}), bf16[16,32,768]{2,1,0:T(8,128)(2,1)S(1)}, u32[]{:S(2)}, u32[]{:S(2)}) async-start(bf16[16,32,768]{2,1,0:T(8,128)(2,1)} %bitcast.105), calls=%async_computation.20 | async-start | bytes 1572864 | tf_op jit(solution)/shard_map/all_to_all | solution.py:349
  561.0 19.5 %copy-start.98 = (f32[2,128,768]{2,1,0:T(8,128)}, f32[2,128,768]{2,1,0:T(8,128)S(1)}, u32[]{:S(2)}) copy-start(f32[2,128,768]{2,1,0:T(8,128)S(1)} %convert_reduce_fusion.4) | copy-start | bytes 2359300
  573.4 21.9 %copy-start.91 = (bf16[16,32,768]{2,1,0:T(8,128)(2,1)}, bf16[16,32,768]{2,1,0:T(8,128)(2,1)S(1)}, u32[]{:S(2)}) copy-start(bf16[16,32,768]{2,1,0:T(8,128)(2,1)S(1)} %all-to-all-done.20) | copy-start | bytes 2359300
  574.6 9.0 all-to-all-start.22
  584.9 8.4 all-to-all-start.17
  595.2 42.3 %all-to-all-start.16 = ((bf16[8,2,128,768]{3,2,1,0:T(8,128)(2,1)}), bf16[8,2,128,768]{3,2,1,0:T(8,128)(2,1)}, u32[]{:S(2)}, u32[]{:S(2)}) async-start(bf16[8,2,128,768]{3,2,1,0:T(8,128)(2,1)} %broadcast_in_dim.152), calls=%async_computation.16 | async-start | bytes 6291456 | tf_op jit(solution)/shard_map/all_to_all | solution.py:13
  623.2 16.8 %copy-start.30 = (f32[128,768]{1,0:T(8,128)S(1)}, f32[128,768]{1,0:T(8,128)}, u32[]{:S(2)}) copy-start(f32[128,768]{1,0:T(8,128)} %copy-done.29) | copy-start | bytes 1179652
  623.2 16.8 %copy-start.147 = (bf16[768,16]{0,1:T(8,128)(2,1)S(1)}, bf16[768,16]{0,1:T(8,128)(2,1)}, u32[]{:S(2)}) copy-start(bf16[768,16]{0,1:T(8,128)(2,1)} %param.32) | copy-start | bytes 73732
  623.2 16.8 %copy-start.222 = (f32[128,16]{0,1:T(8,128)S(1)}, f32[128,16]{0,1:T(8,128)}, u32[]{:S(2)}) copy-start(f32[128,16]{0,1:T(8,128)} %copy-done.221) | copy-start | bytes 24580
  623.2 16.8 %copy-start.255 = (f32[128]{0:T(128)S(1)}, f32[128]{0:T(128)}, u32[]{:S(2)}) copy-start(f32[128]{0:T(128)} %copy-done.254) | copy-start | bytes 1540
  623.2 17.9 %copy-start.280 = (f32[128]{0:T(128)S(1)}, f32[128]{0:T(128)}, u32[]{:S(2)}) copy-start(f32[128]{0:T(128)} %copy-done.279) | copy-start | bytes 1540
  623.2 17.9 %copy-start.99 = (f32[2,128,768]{2,1,0:T(8,128)S(1)}, f32[2,128,768]{2,1,0:T(8,128)}, u32[]{:S(2)}) copy-start(f32[2,128,768]{2,1,0:T(8,128)} %copy-done.98) | copy-start | bytes 2359300
  646.8 62.8 %all-to-all-start.18 = ((bf16[8,2,128,768]{3,2,1,0:T(8,128)(2,1)}), bf16[8,2,128,768]{3,2,1,0:T(8,128)(2,1)}, u32[]{:S(2)}, u32[]{:S(2)}) async-start(bf16[8,2,128,768]{3,2,1,0:T(8,128)(2,1)} %broadcast_in_dim.156), calls=%async_computation.18 | async-start | bytes 6291456 | tf_op jit(solution)/shard_map/all_to_all | solution.py:13
  651.4 156.6 %all-gather.8.cloned.1.call-start = ((), (), s32[]{:S(2)}) async-start(), calls=%async_computation.29 | async-start | bytes 7077888 | tf_op jit(solution)/shard_map/all_gather | solution.py:34
  668.4 43.6 %copy-start.153 = (f32[128,384]{1,0:T(8,128)S(1)}, f32[128,384]{1,0:T(8,128)}, u32[]{:S(2)}) copy-start(f32[128,384]{1,0:T(8,128)} %copy-done.152) | copy-start | bytes 589828
  668.4 43.6 %copy-start.205 = (f32[128,384]{1,0:T(8,128)S(1)}, f32[128,384]{1,0:T(8,128)}, u32[]{:S(2)}) copy-start(f32[128,384]{1,0:T(8,128)} %get-tuple-element.212) | copy-start | bytes 589828
  715.5 43.7 %all-to-all-start.21 = ((bf16[8,2,128,768]{3,2,1,0:T(8,128)(2,1)}), bf16[8,2,128,768]{3,2,1,0:T(8,128)(2,1)}, u32[]{:S(2)}, u32[]{:S(2)}) async-start(bf16[8,2,128,768]{3,2,1,0:T(8,128)(2,1)} %broadcast_in_dim.157), calls=%async_computation.21 | async-start | bytes 6291456 | tf_op jit(solution)/shard_map/all_to_all | solution.py:13
  731.8 29.9 %copy-start.23 = (f32[128,768]{1,0:T(8,128)S(1)}, f32[128,768]{1,0:T(8,128)}, u32[]{:S(2)}) copy-start(f32[128,768]{1,0:T(8,128)} %copy-done.22) | copy-start | bytes 1179652
  731.8 29.9 %copy-start.148 = (bf16[768,16]{0,1:T(8,128)(2,1)S(1)}, bf16[768,16]{0,1:T(8,128)(2,1)}, u32[]{:S(2)}) copy-start(bf16[768,16]{0,1:T(8,128)(2,1)} %param.32) | copy-start | bytes 73732
  731.8 29.9 %copy-start.220 = (f32[128,16]{0,1:T(8,128)S(1)}, f32[128,16]{0,1:T(8,128)}, u32[]{:S(2)}) copy-start(f32[128,16]{0,1:T(8,128)} %copy-done.219) | copy-start | bytes 24580
  731.8 29.9 %copy-start.253 = (f32[128]{0:T(128)S(1)}, f32[128]{0:T(128)}, u32[]{:S(2)}) copy-start(f32[128]{0:T(128)} %copy-done.252) | copy-start | bytes 1540
  731.8 31.0 %copy-start.276 = (f32[128]{0:T(128)S(1)}, f32[128]{0:T(128)}, u32[]{:S(2)}) copy-start(f32[128]{0:T(128)} %copy-done.275) | copy-start | bytes 1540
  765.8 8.6 all-to-all-start.26
  770.4 17.2 %copy-start.101 = (f32[192,768]{1,0:T(8,128)S(1)}, f32[192,768]{1,0:T(8,128)}, u32[]{:S(2)}) copy-start(f32[192,768]{1,0:T(8,128)} %convolution_add_fusion.17) | copy-start | bytes 1769476
  770.4 17.2 %copy-start.176 = (bf16[3,64,128]{2,1,0:T(8,128)(2,1)S(1)}, bf16[3,64,128]{2,1,0:T(8,128)(2,1)}, u32[]{:S(2)}) copy-start(bf16[3,64,128]{2,1,0:T(8,128)(2,1)} %copy-done.175) | copy-start | bytes 147460
  775.0 8.6 all-to-all-start.25
  784.2 8.6 all-to-all-start.24
  787.5 101.3 %all-reduce.4.cloned.1.call-start = ((), (), s32[]{:S(2)}) async-start(), calls=%async_computation.30 | async-start | bytes 5898240 | tf_op jit(solution)/shard_map/psum | solution.py:472
  794.8 90.6 %all-to-all-start.23 = ((bf16[8,2,128,768]{3,2,1,0:T(8,128)(2,1)}), bf16[8,2,128,768]{3,2,1,0:T(8,128)(2,1)}, u32[]{:S(2)}, u32[]{:S(2)}) async-start(bf16[8,2,128,768]{3,2,1,0:T(8,128)(2,1)} %broadcast_in_dim.161), calls=%async_computation.23 | async-start | bytes 6291456 | tf_op jit(solution)/shard_map/all_to_all | solution.py:13
  (256 other events, 818.8 us)
Sparse Core Ops, SparseCore 0:
  119.0 36.5 all-gather.3
  267.9 36.5 all-gather.5
  654.5 61.8 all-gather.7
  793.0 92.5 all-reduce.3
where the time goes:
time: 916 us; the launch traced here: 904 us
  waiting for transfers between devices  375 us (41%)
  starting transfers between devices  121 us (13%)
  matrix products  105 us (11%)
  other arithmetic  104 us (11%)
  blocking collectives  94.5 us (10%)
  local copies, waits for them, and re-layouts  86.6 us (9%)
  between operations  17.8 us (2%)
    all_to_all x14, waiting for transfers between devices, copy_for_each(): lax.all_to_all(jnp.broadcast_to(shard[None], (devices, *shard.shape)), ax...  197 us
    dot_general x93, matrix products, matrix_product(): return jnp.dot(left, right, preferred_element_type=jnp.float32)  92.5 us
    all_gather x3, waiting for transfers between devices, total_of_pieces(): return lax.all_gather(shard, axis).sum(0)  73.3 us
    psum x1, blocking collectives, shards(): lax.psum(for_sending(weight_grads), 'expert')  69.9 us
    all_to_all x14, starting transfers between devices, copy_for_each(): lax.all_to_all(jnp.broadcast_to(shard[None], (devices, *shard.shape)), ax...  57.6 us
    all_to_all x3, waiting for transfers between devices, shards(): lax.all_to_all(grad_send, 'expert', split_axis=0, concat_axis=0, tiled=True)  31.4 us
    all_to_all x3, waiting for transfers between devices, shards(): lax.all_to_all(received_gradient.astype(jnp.bfloat16), 'expert', split_ax...  26.8 us
    all_to_all x1, blocking collectives, copy_for_each(): lax.all_to_all(jnp.broadcast_to(shard[None], (devices, *shard.shape)), ax...  24.6 us
  transfers between devices with their start and end apart: 33, of which 30 were waited for; matrix products, arithmetic and copies ran while one was open for 19% of the time, Pallas kernels for 0%

commit v1 on v0

v1 whole, which is shorter than its diff:
```python
import jax
import jax.numpy as jnp
import numpy as np
from jax import lax
from jax.sharding import PartitionSpec as P

EPSILON = 1e-06
NEGATIVE = -1e30
GROUP = ("section", "mp")


def bucket_limits(count):
    exact = count // 2
    limits = []
    for level in range(1, count):
        if level < exact:
            limits.append(level)
        else:
            distance = exact
            while (
                min(
                    count - 1,
                    exact + int(np.floor(np.log(distance / exact) / np.log(128.0 / exact) * exact)),
                )
                < level
            ):
                distance += 1
            limits.append(distance)
    return limits


def bucket_hot(length, count):
    rows = lax.broadcasted_iota(jnp.int32, (length, length), 0)
    cols = lax.broadcasted_iota(jnp.int32, (length, length), 1)
    distance = rows - cols
    bucket = jnp.zeros((length, length), jnp.int32)
    for limit in bucket_limits(count):
        bucket = bucket + (distance >= limit).astype(jnp.int32)
    levels = lax.broadcasted_iota(jnp.int32, (length, length, count), 2)
    return (bucket[:, :, None] == levels).astype(jnp.float32)


def mm(left, right):
    return jnp.dot(left, right, preferred_element_type=jnp.float32)


def low(value):
    return value.astype(jnp.bfloat16)


def spread_sum(partial):
    devices = lax.axis_size(GROUP)
    rows, width = partial.shape
    pieces = low(partial).reshape(devices, rows // devices, width)
    pieces = lax.all_to_all(pieces, GROUP, 0, 0, tiled=True)
    return pieces.astype(jnp.float32).sum(axis=0)


def collect(rows):
    devices = lax.axis_size(GROUP)
    copies = jnp.broadcast_to(rows[None], (devices, *rows.shape))
    return lax.all_to_all(copies, GROUP, 0, 0, tiled=True).reshape(-1, rows.shape[1])


def inverse_rms(rows):
    return lax.rsqrt(jnp.mean(rows * rows, axis=-1, keepdims=True) + EPSILON)


def normed(rows, gain):
    return low(rows * inverse_rms(rows) * gain[None])


def normed_back(rows, gain, grad):
    rho = inverse_rms(rows)
    scaled = grad * gain[None]
    back = scaled * rho - rows * (rho * rho * rho) * jnp.mean(scaled * rows, axis=-1, keepdims=True)
    return back, jnp.sum(grad * rows * rho, axis=0)


def gelu_parts(a):
    inner = 0.7978845608028654 * (a + 0.044715 * a * a * a)
    t = jnp.tanh(inner)
    value = 0.5 * a * (1.0 + t)
    slope = 0.5 * (1.0 + t) + 0.5 * a * (1.0 - t * t) * 0.7978845608028654 * (1.0 + 3 * 0.044715 * a * a)
    return value, slope


def attention(rows_in, wq, wk, wv, wo, mask, bias, micro, heads):
    rows = rows_in.shape[0]
    size = wq.shape[1] // heads

    def split(w):
        return low(mm(rows_in, w)).reshape(micro, rows // micro, heads, size)

    q, k, v = split(wq), split(wk), split(wv)
    scores = jnp.einsum("mqhe,mkhe->mhqk", q, k, preferred_element_type=jnp.float32) * size**-0.5
    scores = jnp.where(mask[:, None], scores + bias[None], NEGATIVE)
    top = jnp.max(scores, axis=-1, keepdims=True)
    e = jnp.exp(scores - top)
    probs = e / jnp.sum(e, axis=-1, keepdims=True)
    o = jnp.einsum("mhqk,mkhe->mqhe", low(probs), v, preferred_element_type=jnp.float32)
    o = low(o).reshape(rows, -1)
    return mm(o, wo), (rows_in, q, k, v, probs, o)


def attention_back(state, grad, wq, wk, wv, wo, hot):
    rows_in, q, k, v, probs, o = state
    rows = rows_in.shape[0]
    size = q.shape[-1]
    g_out = mm(o.T, grad)
    do = low(mm(grad, wo.T)).reshape(q.shape)
    dv = low(jnp.einsum("mhqk,mqhe->mkhe", low(probs), do, preferred_element_type=jnp.float32))
    dp = jnp.einsum("mqhe,mkhe->mhqk", do, v, preferred_element_type=jnp.float32)
    ds = low(probs * (dp - jnp.sum(dp * probs, axis=-1, keepdims=True)))
    g_bias = jnp.einsum("hqk,qkb->bh", ds.astype(jnp.float32).sum(axis=0), hot, precision=lax.Precision.HIGHEST)
    dq = low(jnp.einsum("mhqk,mkhe->mqhe", ds, k, preferred_element_type=jnp.float32) * size**-0.5)
    dk = low(jnp.einsum("mhqk,mqhe->mkhe", ds, q, preferred_element_type=jnp.float32) * size**-0.5)
    dq, dk, dv = (t.reshape(rows, -1) for t in (dq, dk, dv))
    n_t = rows_in.T
    dn = mm(dq, wq.T) + mm(dk, wk.T) + mm(dv, wv.T)
    return dn, (mm(n_t, dq), mm(n_t, dk), mm(n_t, dv), g_out, g_bias)


def shards(
    block_input,
    segments,
    routes,
    cotangent,
    attn_gain,
    query_weight,
    key_weight,
    value_weight,
    out_weight,
    pos_bias,
    ffn_gain,
    dense_gate,
    dense_up,
    dense_down,
    router,
    expert_gate,
    expert_up,
    expert_down,
):
    section = lax.axis_index("section")
    first = section == 0
    place = section * lax.axis_size("mp") + lax.axis_index("mp")
    devices = lax.axis_size(GROUP)
    micro, _, length, width = block_input.shape
    experts = router.shape[1]
    cap = 4 * length // experts
    heads = pos_bias.shape[2]
    rows = micro * length
    part = rows // devices
    wq, wk, wv, wo = query_weight[0], key_weight[0], value_weight[0], out_weight[0]
    gate_w, up_w, down_w = expert_gate[0], expert_up[0], expert_down[0]

    def own_rows(whole):
        return lax.dynamic_slice_in_dim(whole, place * part, part, axis=0)

    x = block_input.reshape(rows, width)
    gy = cotangent.reshape(rows, width)
    gains = lax.all_gather(jnp.concatenate([attn_gain, ffn_gain]), "section")
    hot = bucket_hot(length, pos_bias.shape[1])
    bias = jnp.einsum("qkb,bh->hqk", hot, pos_bias[0], precision=lax.Precision.HIGHEST)
    docs = segments[:, 0]
    causal = lax.broadcasted_iota(jnp.int32, (length, length), 1) <= lax.broadcasted_iota(
        jnp.int32, (length, length), 0
    )
    mask = causal[None] & (docs[:, :, None] == docs[:, None, :])

    x_f = x.astype(jnp.float32)
    term, state_one = attention(normed(x_f, gains[0, 0]), wq, wk, wv, wo, mask, bias, micro, heads)
    h1 = own_rows(x_f) + spread_sum(jnp.where(first, term, 0.0))
    r1 = collect(normed(h1, gains[0, 1]))
    a1, u1 = mm(r1, dense_gate), mm(r1, dense_up)
    value1, slope1 = gelu_parts(a1)
    hid1 = low(value1 * u1)
    y1 = h1 + spread_sum(mm(hid1, dense_down))
    n2 = collect(normed(y1, gains[1, 0]))
    term, state_two = attention(n2, wq, wk, wv, wo, mask, bias, micro, heads)
    h2 = y1 + spread_sum(jnp.where(first, 0.0, term))
    r2_own = normed(h2, gains[1, 1])
    r2 = collect(r2_own)
    route = routes.reshape(micro, length, 2)
    ids = jnp.arange(experts, dtype=jnp.int32)
    route_hot = (route[..., None] == ids).astype(jnp.float32)
    logits = mm(r2, router).reshape(micro, length, experts)
    gates = jax.nn.softmax(jnp.sum(route_hot * logits[:, :, None], axis=-1), axis=-1)
    named = route_hot.sum(axis=2)
    rank = jnp.cumsum(named, axis=1) - named
    slots = jnp.arange(cap, dtype=jnp.float32)
    pick = (route_hot.transpose(0, 2, 3, 1)[:, :, :, None] > 0) & (
        rank.transpose(0, 2, 1)[:, None, :, None] == slots[:, None]
    )
    pick = low(pick)
    both = pick.sum(axis=1)
    gate_slot = jnp.einsum("mceki,mic->emk", pick.astype(jnp.float32), gates, precision=lax.Precision.HIGHEST)
    x_send = jnp.einsum("meki,mid->emkd", both, r2.reshape(micro, length, width))
    g_send = jnp.einsum(
        "meki,mid->emkd", both, gy.reshape(micro, length, width), preferred_element_type=jnp.float32
    )
    g_send = low(g_send * gate_slot[..., None])
    sent = jnp.concatenate([x_send, g_send], axis=-1).reshape(experts, micro * cap, 2 * width)
    arrived = lax.all_to_all(sent, "expert", 0, 0, tiled=True).reshape(-1, 2 * width)
    xr, dout = arrived[:, :width], arrived[:, width:]
    a, u = mm(xr, gate_w), mm(xr, up_w)
    value, slope = gelu_parts(a)
    hid = low(value * u)
    dhid = mm(dout, down_w.T)
    da, du = low(dhid * u * slope), low(dhid * value)
    e_out = low(mm(hid, down_w))
    d_x = low(mm(da, gate_w.T) + mm(du, up_w.T))
    back = jnp.concatenate([e_out, d_x], axis=-1).reshape(experts, micro * cap, 2 * width)
    back = lax.all_to_all(back, "expert", 0, 0, tiled=True).reshape(experts, micro, cap, 2 * width)
    g_expert = (mm(xr.T, da), mm(xr.T, du), mm(hid.T, dout))
    chosen = jnp.einsum(
        "mceki,emkd->cmid", pick, back[..., :width], preferred_element_type=jnp.float32
    ).reshape(2, rows, width)
    d_rows = jnp.einsum(
        "meki,emkd->mid", both, back[..., width:], preferred_element_type=jnp.float32
    ).reshape(rows, width)
    flat_gates = gates.reshape(rows, 2)
    moe = flat_gates[:, :1] * chosen[0] + flat_gates[:, 1:] * chosen[1]
    gate_terms = jnp.sum(chosen * gy.astype(jnp.float32)[None], axis=-1).T
    gate_terms = jnp.pad(gate_terms, ((0, 0), (0, 126)))
    summed = spread_sum(jnp.concatenate([moe, d_rows, gate_terms], axis=-1))
    out_own = h2 + summed[:, :width]
    block_output = collect(out_own)
    gate_own = own_rows(flat_gates)
    gate_grad = summed[:, 2 * width : 2 * width + 2]
    d_sel = gate_own * (gate_grad - jnp.sum(gate_own * gate_grad, axis=-1, keepdims=True))
    d_logits = jnp.sum(d_sel[:, :, None] * own_rows(route_hot.reshape(rows, 2, experts)), axis=1)
    g_router = jnp.dot(r2_own.astype(jnp.float32).T, d_logits, precision=lax.Precision.HIGHEST)
    dr2 = summed[:, width : 2 * width] + jnp.dot(
        d_logits, router.astype(jnp.float32).T, precision=lax.Precision.HIGHEST
    )
    back2, g_ffn2 = normed_back(h2, gains[1, 1], dr2)
    dh2 = own_rows(gy).astype(jnp.float32) + back2
    dn2, grads_two = attention_back(state_two, collect(low(dh2)), wq, wk, wv, wo, hot)
    back2, g_attn2 = normed_back(y1, gains[1, 0], spread_sum(jnp.where(first, 0.0, dn2)))
    gy1 = dh2 + back2
    dout1 = collect(low(gy1))
    dhid1 = mm(dout1, dense_down.T)
    da1, du1 = low(dhid1 * u1 * slope1), low(dhid1 * value1)
    dr1 = spread_sum(mm(da1, dense_gate.T) + mm(du1, dense_up.T))
    g_dense = (mm(r1.T, da1), mm(r1.T, du1), mm(hid1.T, dout1))
    back1, g_ffn1 = normed_back(h1, gains[0, 1], dr1)
    dh1 = gy1 + back1
    dn1, grads_one = attention_back(state_one, collect(low(dh1)), wq, wk, wv, wo, hot)
    back1, g_attn1 = normed_back(own_rows(x_f), gains[0, 0], spread_sum(jnp.where(first, dn1, 0.0)))
    input_grad = collect(low(dh1 + back1)).astype(jnp.float32)
    grads = jax.tree.map(lambda one, two: jnp.where(first, one, two), grads_one, grads_two)
    everyone = ("section", "expert", "mp")
    g_gains = jnp.stack([jnp.stack([g_attn1, g_attn2]), jnp.stack([g_ffn1, g_ffn2])])
    g_gains, g_router = lax.psum((g_gains, g_router), everyone)
    g_own = lax.dynamic_index_in_dim(g_gains, section, axis=1)
    grads, g_dense = jax.tree.map(
        lambda a: a.astype(jnp.float32), lax.psum(jax.tree.map(low, (grads, g_dense)), "expert")
    )
    return (
        block_output.reshape(block_input.shape),
        input_grad.reshape(block_input.shape),
        g_own[0],
        grads[0][None],
        grads[1][None],
        grads[2][None],
        grads[3][None],
        grads[4][None],
        g_own[1],
        *g_dense,
        g_router,
        *(g[None] for g in g_expert),
    )


def solution(mesh):
    placed = (
        P(None, "expert", None, None),
        P(None, "expert", None),
        P(None, "expert", None, None),
        P(None, "expert", None, None),
        P("section", None),
        P("section", None, "mp"),
        P("section", None, "mp"),
        P("section", None, "mp"),
        P("section", "mp", None),
        P("section", None, "mp"),
        P("section", None),
        P(None, ("section", "mp")),
        P(None, ("section", "mp")),
        P(("section", "mp"), None),
        P(),
        P("expert", None, ("section", "mp")),
        P("expert", None, ("section", "mp")),
        P("expert", ("section", "mp"), None),
    )
    return jax.shard_map(
        shards,
        mesh=mesh,
        in_specs=placed,
        out_specs=(
            P(None, "expert", None, None),
            P(None, "expert", None, None),
            P("section", None),
            P("section", None, "mp"),
            P("section", None, "mp"),
            P("section", None, "mp"),
            P("section", "mp", None),
            P("section", None, "mp"),
            P("section", None),
            P(None, ("section", "mp")),
            P(None, ("section", "mp")),
            P(("section", "mp"), None),
            P(),
            P("expert", None, ("section", "mp")),
            P("expert", None, ("section", "mp")),
            P("expert", ("section", "mp"), None),
        ),
        check_vma=False,
    )
```

time: 916 us -> 499 us (0.54)
  waiting for transfers between devices: 375 us -> 108 us
  blocking collectives: 94.5 us -> 218 us
  starting transfers between devices: 121 us -> 37.6 us
  other arithmetic: 104 us -> 33.5 us
  local copies, waits for them, and re-layouts: 86.6 us -> 23.8 us
  matrix products: 105 us -> 52.4 us
    all_to_all x26 -> x10, waiting for transfers between devices: 298 us -> 108 us  [the longest x1 43.9 us: shards(): lax.all_to_all(back, 'expert', 0, 0, tiled=True)]
    all_to_all x1 -> x7, blocking collectives: 24.6 us -> 115 us  [the longest x1 47.9 us: shards(): lax.all_to_all(sent, 'expert', 0, 0, tiled=True).reshape(-1, 2 * width)]
    all_to_all x26 -> x10, starting transfers between devices: 120 us -> 37.5 us  [the longest x5 17.9 us: collect(): lax.all_to_all(copies, GROUP, 0, 0, tiled=True).reshape(-1, rows.shape[1])]
    all_gather x3 -> x0, waiting for transfers between devices: 73.3 us -> none  [total_of_pieces(): return lax.all_gather(shard, axis).sum(0)]
    dot_general x121 -> x65, matrix products: 105 us -> 52.4 us  [the longest x43 38.4 us: mm(): return jnp.dot(left, right, preferred_element_type=jnp.float32)]
    reduce_sum x48 -> x21, other arithmetic: 53.1 us -> 7.19 us  [the longest x4 3.06 us: inverse_rms(): return lax.rsqrt(jnp.mean(rows * rows, axis=-1, keepdims=True) + EPSILON)]
    psum x1 -> x2, blocking collectives: 69.9 us -> 101 us  [the longest x1 64.9 us: shards(): g_gains, g_router = lax.psum((g_gains, g_router), everyone)]
    broadcast_in_dim x20 -> x8, local copies, waits for them, and re-layouts: 20.4 us -> 4.13 us  [collect(): copies = jnp.broadcast_to(rows[None], (devices, *rows.shape))]
  transfers between devices with their start and end apart: 33 -> 11, of which waited for: 30 -> 9; matrix products, arithmetic and copies ran while one was open for 19% -> 5% of each run, Pallas kernels for 0% -> 0%
where the time goes in v1:
time: 499 us; the launch traced here: 490 us
  blocking collectives  218 us (44%)
  waiting for transfers between devices  108 us (22%)
  matrix products  52.4 us (11%)
  starting transfers between devices  37.6 us (8%)
  other arithmetic  33.5 us (7%)
  local copies, waits for them, and re-layouts  23.8 us (5%)
  between operations  16.3 us (3%)
    psum x1, blocking collectives, shards(): g_gains, g_router = lax.psum((g_gains, g_router), everyone)  64.9 us
    all_to_all x1, blocking collectives, shards(): lax.all_to_all(sent, 'expert', 0, 0, tiled=True).reshape(-1, 2 * width)  47.9 us
    all_to_all x1, waiting for transfers between devices, shards(): lax.all_to_all(back, 'expert', 0, 0, tiled=True)  43.9 us
    dot_general x43, matrix products, mm(): return jnp.dot(left, right, preferred_element_type=jnp.float32)  38.4 us
    psum x1, blocking collectives, shards(): lax.psum(jax.tree.map(low, (grads, g_dense)), 'expert')  36.4 us
    all_to_all x3, blocking collectives, collect(): lax.all_to_all(copies, GROUP, 0, 0, tiled=True).reshape(-1, rows.shape[1])  33.8 us
    all_to_all x3, blocking collectives, spread_sum(): pieces = lax.all_to_all(pieces, GROUP, 0, 0, tiled=True)  33.7 us
    all_to_all x4, waiting for transfers between devices, spread_sum(): pieces = lax.all_to_all(pieces, GROUP, 0, 0, tiled=True)  32.9 us
  transfers between devices with their start and end apart: 11, of which 9 were waited for; matrix products, arithmetic and copies ran while one was open for 5% of the time, Pallas kernels for 0%

profile of v1, /device:TPU:0, one launch (start us, length us, event | category | flops | bytes accessed | tf_op | source)
XLA Modules:
  0.0 489.9 jit_solution(641128712403575138)
XLA Ops:
  7.4 1.2 multiply_reduce_fusion.1
  9.4 1.8 all-gather.1
  11.2 1.2 multiply_convert_fusion.2
  12.4 1.3 convolution_convert_fusion.10
  14.7 2.4 copy.349
  19.6 1.1 fusion.32
  20.7 4.4 all-to-all-start
  26.1 7.3 %all-to-all-done = bf16[8,32,768]{2,1,0:T(8,128)(2,1)S(1)} async-done(((bf16[8,32,768]{2,1,0:T(8,128)(2,1)}), bf16[8,32,768]{2,1,0:T(8,128)(2,1)S(1)}, u32[]{:S(2)}, u32[]{:S(2)}) %all-to-all-start) | async-done | bytes 393248 | tf_op jit(solution)/shard_map/all_to_all | solution.py:55
  33.5 1.6 multiply_reduce_fusion.15
  35.8 11.2 %all_to_all.85 = bf16[8,32,768]{2,1,0:T(8,128)(2,1)S(1)} all-to-all(bf16[8,32,768]{2,1,0:T(8,128)(2,1)S(1)} %broadcast_in_dim.74), channel_id=1, replica_groups=mesh['section'=2,'expert'=16,'mp'=4] {'section','mp'}, dimensions={0} | all-to-all | bytes 786432 | tf_op jit(solution)/shard_map/all_to_all | solution.py:62
  47.4 1.1 multiply_convert_fusion.6
  48.9 11.3 %all_to_all.86 = bf16[8,32,768]{2,1,0:T(8,128)(2,1)S(1)} all-to-all(bf16[8,32,768]{2,1,0:T(8,128)(2,1)S(1)} %bitcast.396), channel_id=1, replica_groups=mesh['section'=2,'expert'=16,'mp'=4] {'section','mp'}, dimensions={0} | all-to-all | bytes 786432 | tf_op jit(solution)/shard_map/all_to_all | solution.py:55
  61.1 11.2 %all_to_all.87 = bf16[8,32,768]{2,1,0:T(8,128)(2,1)S(1)} all-to-all(bf16[8,32,768]{2,1,0:T(8,128)(2,1)S(1)} %broadcast_in_dim.75), channel_id=1, replica_groups=mesh['section'=2,'expert'=16,'mp'=4] {'section','mp'}, dimensions={0} | all-to-all | bytes 786432 | tf_op jit(solution)/shard_map/all_to_all | solution.py:62
  75.2 11.2 %all_to_all.88 = bf16[8,32,768]{2,1,0:T(8,128)(2,1)S(1)} all-to-all(bf16[8,32,768]{2,1,0:T(8,128)(2,1)S(1)} %bitcast.410), channel_id=1, replica_groups=mesh['section'=2,'expert'=16,'mp'=4] {'section','mp'}, dimensions={0} | all-to-all | bytes 786432 | tf_op jit(solution)/shard_map/all_to_all | solution.py:55
  88.1 3.6 all-to-all-start.5
  91.7 8.2 %all-to-all-done.5 = bf16[8,32,768]{2,1,0:T(8,128)(2,1)S(1)} async-done(((bf16[8,32,768]{2,1,0:T(8,128)(2,1)}), bf16[8,32,768]{2,1,0:T(8,128)(2,1)S(1)}, u32[]{:S(2)}, u32[]{:S(2)}) %all-to-all-start.5) | async-done | bytes 393248 | tf_op jit(solution)/shard_map/all_to_all | solution.py:62
  101.5 1.1 fusion.5
  104.7 47.9 %all_to_all.89 = bf16[16,64,1536]{2,1,0:T(8,128)(2,1)S(1)} all-to-all(bf16[16,64,1536]{2,1,0:T(8,128)(2,1)S(1)} %bitcast.371), channel_id=1, replica_groups=mesh['section'=2,'expert'=16,'mp'=4] {'expert'}, dimensions={0} | all-to-all | bytes 6291456 | tf_op jit(solution)/shard_map/all_to_all | solution.py:204
  155.1 1.9 multiply_convert_fusion.1
  157.1 1.0 convolution_convert_fusion
  160.2 2.0 pad_maximum_fusion.1
  162.2 4.7 copy.363
  166.9 4.6 all-to-all-start.7
  172.6 43.9 %all-to-all-done.7 = bf16[16,64,1536]{2,1,0:T(8,128)(2,1)} async-done(((bf16[16,64,1536]{2,1,0:T(8,128)(2,1)}), bf16[16,64,1536]{2,1,0:T(8,128)(2,1)}, u32[]{:S(2)}, u32[]{:S(2)}) %all-to-all-start.7) | async-done | bytes 3145760 | tf_op jit(solution)/shard_map/all_to_all | solution.py:214
  216.5 2.2 fusion.214
  218.7 1.2 fusion.29
  222.9 3.7 all-to-all-start.8
  226.7 13.1 %all-to-all-done.8 = bf16[8,32,1664]{2,1,0:T(8,128)(2,1)S(1)} async-done(((bf16[8,32,1664]{2,1,0:T(8,128)(2,1)}), bf16[8,32,1664]{2,1,0:T(8,128)(2,1)S(1)}, u32[]{:S(2)}, u32[]{:S(2)}) %all-to-all-start.8) | async-done | bytes 852000 | tf_op jit(solution)/shard_map/all_to_all | solution.py:55
  241.2 1.5 fusion.213
  242.8 11.4 %all_to_all.90 = bf16[8,32,768]{2,1,0:T(8,128)(2,1)S(1)} all-to-all(bf16[8,32,768]{2,1,0:T(8,128)(2,1)S(1)} %broadcast_in_dim.78), channel_id=1, replica_groups=mesh['section'=2,'expert'=16,'mp'=4] {'section','mp'}, dimensions={0} | all-to-all | bytes 786432 | tf_op jit(solution)/shard_map/all_to_all | solution.py:62
  254.5 2.1 fusion.57
  259.8 11.2 %all_to_all.91 = bf16[8,32,768]{2,1,0:T(8,128)(2,1)S(1)} all-to-all(bf16[8,32,768]{2,1,0:T(8,128)(2,1)S(1)} %bitcast.395), channel_id=1, replica_groups=mesh['section'=2,'expert'=16,'mp'=4] {'section','mp'}, dimensions={0} | all-to-all | bytes 786432 | tf_op jit(solution)/shard_map/all_to_all | solution.py:55
  273.3 3.5 all-to-all-start.12
  276.8 8.2 %all-to-all-done.12 = bf16[8,32,768]{2,1,0:T(8,128)(2,1)S(1)} async-done(((bf16[8,32,768]{2,1,0:T(8,128)(2,1)}), bf16[8,32,768]{2,1,0:T(8,128)(2,1)S(1)}, u32[]{:S(2)}, u32[]{:S(2)}) %all-to-all-start.12) | async-done | bytes 393248 | tf_op jit(solution)/shard_map/all_to_all | solution.py:62
  285.8 2.0 multiply_convert_fusion.4
  289.0 1.1 fusion.34
  290.1 3.5 all-to-all-start.13
  294.1 2.1 convolution_convert_fusion.1
  296.2 5.6 %all-to-all-done.13 = bf16[8,32,768]{2,1,0:T(8,128)(2,1)S(1)} async-done(((bf16[8,32,768]{2,1,0:T(8,128)(2,1)}), bf16[8,32,768]{2,1,0:T(8,128)(2,1)S(1)}, u32[]{:S(2)}, u32[]{:S(2)}) %all-to-all-start.13) | async-done | bytes 393248 | tf_op jit(solution)/shard_map/all_to_all | solution.py:55
  304.4 3.6 all-to-all-start.14
  308.0 2.1 convolution_convert_fusion.2
  310.2 2.1 convolution_convert_fusion.3
  312.3 3.9 all-to-all-done.14
  316.8 1.4 fusion.58
  324.6 1.1 copy-done.117
  325.7 3.4 convolution_bitcast_fusion.1
  329.1 2.0 convolution_bitcast_fusion.3
  331.1 2.0 convolution_bitcast_fusion.2
  334.1 3.6 all-to-all-start.9
  338.3 1.1 fusion.28
  339.4 10.7 %all-to-all-done.9 = f32[8,32,768]{2,1,0:T(8,128)S(1)} async-done(((f32[8,32,768]{2,1,0:T(8,128)}), f32[8,32,768]{2,1,0:T(8,128)S(1)}, u32[]{:S(2)}, u32[]{:S(2)}) %all-to-all-start.9) | async-done | bytes 786464 | tf_op jit(solution)/shard_map/all_to_all | solution.py:62
  350.1 3.5 all-to-all-start.15
  353.8 1.1 convolution_bitcast_fusion.6
  354.9 6.9 %all-to-all-done.15 = bf16[8,32,768]{2,1,0:T(8,128)(2,1)S(1)} async-done(((bf16[8,32,768]{2,1,0:T(8,128)(2,1)}), bf16[8,32,768]{2,1,0:T(8,128)(2,1)S(1)}, u32[]{:S(2)}, u32[]{:S(2)}) %all-to-all-start.15) | async-done | bytes 393248 | tf_op jit(solution)/shard_map/all_to_all | solution.py:55
  361.9 1.1 multiply_reduce_fusion.7
  364.8 3.7 all-to-all-start.16
  368.5 1.1 fusion.65
  369.6 36.4 %psum.75 = bf16[1,32,3]{1,2,0:T(4,128)(2,1)S(1)} all-reduce(bf16[1,32,3]{1,2,0:T(4,128)(2,1)S(1)} %fusion.65), channel_id=1, replica_groups=mesh['section'=2,'expert'=16,'mp'=4] {'expert'}, use_global_device_ids=true, to_apply=%region_42.43 | all-reduce | flops 96 | bytes 384 | tf_op jit(solution)/shard_map/psum | solution.py:258
  406.6 64.9 %all-reduce.1 = (f32[2,2,768]{2,1,0:T(2,128)S(1)}, f32[768,16]{0,1:T(8,128)}) all-reduce(f32[2,2,768]{2,1,0:T(2,128)S(1)} %pad_maximum_fusion.3, f32[768,16]{0,1:T(8,128)S(1)} %fusion.220), channel_id=1, replica_groups=mesh['section'=2,'expert'=16,'mp'=4] {'section','expert','mp'}, use_global_device_ids=true, to_apply=%region_35.36 | all-reduce | flops 15360 | bytes 122880 | tf_op jit(solution)/shard_map/psum | solution.py:255
  473.0 1.9 broadcast_in_dim.83
  474.9 1.8 broadcast_in_dim.158
  478.5 1.1 convert_element_type.742
  479.6 1.1 convert_element_type.744
  480.7 1.1 convert_element_type.746
  (387 shorter events, 51.3 us)
Async XLA Ops:
  7.2 147.9 %copy-start = (bf16[1,768,384]{2,1,0:T(8,128)(2,1)S(1)}, bf16[1,768,384]{2,1,0:T(8,128)(2,1)}, u32[]{:S(2)}) copy-start(bf16[1,768,384]{2,1,0:T(8,128)(2,1)} %param.34) | copy-start | bytes 1769476
  7.2 6.5 %copy-start.2 = (bf16[1,768,192]{1,2,0:T(8,128)(2,1)S(1)}, bf16[1,768,192]{1,2,0:T(8,128)(2,1)}, u32[]{:S(2)}) copy-start(bf16[1,768,192]{1,2,0:T(8,128)(2,1)} %param.23) | copy-start | bytes 884740
  7.4 7.0 %copy-start.73 = (s32[128,128]{0,1:T(8,128)}, s32[128,128]{0,1:T(8,128)S(1)}, u32[]{:S(2)}) copy-start(s32[128,128]{0,1:T(8,128)S(1)} %convert_add_fusion) | copy-start | bytes 196612
  7.4 6.6 %copy-start.6 = (bf16[1,768,192]{1,2,0:T(8,128)(2,1)S(1)}, bf16[1,768,192]{1,2,0:T(8,128)(2,1)}, u32[]{:S(2)}) copy-start(bf16[1,768,192]{1,2,0:T(8,128)(2,1)} %param.25) | copy-start | bytes 884740
  11.2 24.5 %copy-start.83 = (f32[768]{0:T(1024)}, f32[768]{0:T(1024)S(1)}, u32[]{:S(2)}) copy-start(f32[768]{0:T(1024)S(1)} %get-tuple-element.154) | copy-start | bytes 9220
  11.2 49.7 %copy-start.85 = (f32[768]{0:T(1024)}, f32[768]{0:T(1024)S(1)}, u32[]{:S(2)}) copy-start(f32[768]{0:T(1024)S(1)} %get-tuple-element.153) | copy-start | bytes 9220
  14.4 4.8 copy-start.76
  19.2 5.8 %copy-start.8 = (bf16[2,1,128,768]{3,2,1,0:T(8,128)(2,1)S(1)}, bf16[2,1,128,768]{3,2,1,0:T(8,128)(2,1)}, u32[]{:S(2)}) copy-start(bf16[2,1,128,768]{3,2,1,0:T(8,128)(2,1)} %param.18) | copy-start | bytes 1179652
  19.6 5.5 %copy-start.62 = (bf16[2,128,3,64]{1,0,3,2:T(2,128)(2,1)}, bf16[2,128,3,64]{1,0,3,2:T(2,128)(2,1)S(1)}, u32[]{:S(2)}) copy-start(bf16[2,128,3,64]{1,0,3,2:T(2,128)(2,1)S(1)} %copy.353) | copy-start | bytes 294916
  20.7 12.7 %all-to-all-start = ((bf16[8,32,768]{2,1,0:T(8,128)(2,1)}), bf16[8,32,768]{2,1,0:T(8,128)(2,1)S(1)}, u32[]{:S(2)}, u32[]{:S(2)}) async-start(bf16[8,32,768]{2,1,0:T(8,128)(2,1)} %bitcast.10), calls=%async_computation | async-start | bytes 786432 | tf_op jit(solution)/shard_map/all_to_all | solution.py:55
  25.1 21.9 %copy-start.14 = (bf16[768,384]{1,0:T(8,128)(2,1)S(1)}, bf16[768,384]{1,0:T(8,128)(2,1)}, u32[]{:S(2)}) copy-start(bf16[768,384]{1,0:T(8,128)(2,1)} %param.29) | copy-start | bytes 1769476
  33.4 13.9 %copy-start.57 = (bf16[768,384]{1,0:T(8,128)(2,1)S(1)}, bf16[768,384]{1,0:T(8,128)(2,1)}, u32[]{:S(2)}) copy-start(bf16[768,384]{1,0:T(8,128)(2,1)} %param.30) | copy-start | bytes 1769476
  35.7 12.9 %copy-start.104 = (f32[32]{0:T(128)}, f32[32]{0:T(128)S(1)}, u32[]{:S(2)}) copy-start(f32[32]{0:T(128)S(1)} %get-tuple-element.201) | copy-start | bytes 388
  48.5 12.5 %copy-start.49 = (bf16[256,384]{1,0:T(8,128)(2,1)}, bf16[256,384]{1,0:T(8,128)(2,1)S(1)}, u32[]{:S(2)}) copy-start(bf16[256,384]{1,0:T(8,128)(2,1)S(1)} %get-tuple-element.208) | copy-start | bytes 589828
  48.9 23.3 %copy-start.4 = (bf16[1,768,192]{1,2,0:T(8,128)(2,1)S(1)}, bf16[1,768,192]{1,2,0:T(8,128)(2,1)}, u32[]{:S(2)}) copy-start(bf16[1,768,192]{1,2,0:T(8,128)(2,1)} %param.24) | copy-start | bytes 884740
  61.0 12.2 %copy-start.106 = (f32[32]{0:T(128)}, f32[32]{0:T(128)S(1)}, u32[]{:S(2)}) copy-start(f32[32]{0:T(128)S(1)} %get-tuple-element.203) | copy-start | bytes 388
  74.5 11.9 %copy-start.91 = (f32[2,3,128]{2,1,0:T(4,128)}, f32[2,3,128]{2,1,0:T(4,128)S(1)}, u32[]{:S(2)}) copy-start(f32[2,3,128]{2,1,0:T(4,128)S(1)} %get-tuple-element.210) | copy-start | bytes 9220
  74.8 13.2 %copy-start.67 = (bf16[2,128,3,64]{1,0,3,2:T(2,128)(2,1)}, bf16[2,128,3,64]{1,0,3,2:T(2,128)(2,1)S(1)}, u32[]{:S(2)}) copy-start(bf16[2,128,3,64]{1,0,3,2:T(2,128)(2,1)S(1)} %copy.358) | copy-start | bytes 294916
  75.2 16.5 %copy-start.98 = (s32[2,1,128,2]{2,3,1,0:T(2,128)S(1)}, s32[2,1,128,2]{2,3,1,0:T(2,128)}, u32[]{:S(2)}) copy-start(s32[2,1,128,2]{2,3,1,0:T(2,128)} %param.20) | copy-start | bytes 6148
  75.2 24.8 %copy-start.81 = (bf16[768,16]{0,1:T(8,128)(2,1)S(1)}, bf16[768,16]{0,1:T(8,128)(2,1)}, u32[]{:S(2)}) copy-start(bf16[768,16]{0,1:T(8,128)(2,1)} %param.32) | copy-start | bytes 73732
  86.6 15.0 %copy-start.19 = (f32[32,768]{1,0:T(8,128)}, f32[32,768]{1,0:T(8,128)S(1)}, u32[]{:S(2)}) copy-start(f32[32,768]{1,0:T(8,128)S(1)} %get-tuple-element.180) | copy-start | bytes 294916
  87.2 4.5 copy-start.102
  87.3 13.1 %copy-start.59 = (bf16[32,768]{1,0:T(8,128)(2,1)}, bf16[32,768]{1,0:T(8,128)(2,1)S(1)}, u32[]{:S(2)}) copy-start(bf16[32,768]{1,0:T(8,128)(2,1)S(1)} %multiply_convert_fusion.7) | copy-start | bytes 147460
  88.1 11.9 %all-to-all-start.5 = ((bf16[8,32,768]{2,1,0:T(8,128)(2,1)}), bf16[8,32,768]{2,1,0:T(8,128)(2,1)S(1)}, u32[]{:S(2)}, u32[]{:S(2)}) async-start(bf16[8,32,768]{2,1,0:T(8,128)(2,1)} %broadcast_in_dim.76), calls=%async_computation.5 | async-start | bytes 786432 | tf_op jit(solution)/shard_map/all_to_all | solution.py:62
  104.7 47.9 %copy-start.115 = (bf16[1,384,768]{2,1,0:T(8,128)(2,1)S(1)}, bf16[1,384,768]{2,1,0:T(8,128)(2,1)}, u32[]{:S(2)}) copy-start(bf16[1,384,768]{2,1,0:T(8,128)(2,1)} %param.35) | copy-start | bytes 1769476
  166.9 5.6 %copy-start.88 = (f32[2,128,2]{1,2,0:T(2,128)S(1)}, f32[2,128,2]{1,2,0:T(2,128)}, u32[]{:S(2)}) copy-start(f32[2,128,2]{1,2,0:T(2,128)} %copy-done.87) | copy-start | bytes 6148
  166.9 5.6 %copy-start.97 = (f32[2,128]{1,0:T(2,128)S(1)}, f32[2,128]{1,0:T(2,128)}, u32[]{:S(2)}) copy-start(f32[2,128]{1,0:T(2,128)} %copy-done.96) | copy-start | bytes 3076
  166.9 5.6 %copy-start.101 = (f32[2,128]{1,0:T(2,128)S(1)}, f32[2,128]{1,0:T(2,128)}, u32[]{:S(2)}) copy-start(f32[2,128]{1,0:T(2,128)} %copy-done.100) | copy-start | bytes 3076
  166.9 49.6 %all-to-all-start.7 = ((bf16[16,64,1536]{2,1,0:T(8,128)(2,1)}), bf16[16,64,1536]{2,1,0:T(8,128)(2,1)}, u32[]{:S(2)}, u32[]{:S(2)}) async-start(bf16[16,64,1536]{2,1,0:T(8,128)(2,1)} %bitcast.370), calls=%async_computation.7 | async-start | bytes 6291456 | tf_op jit(solution)/shard_map/all_to_all | solution.py:214
  221.9 4.7 copy-start.99
  222.9 17.3 %copy-start.20 = (f32[32,768]{1,0:T(8,128)S(1)}, f32[32,768]{1,0:T(8,128)}, u32[]{:S(2)}) copy-start(f32[32,768]{1,0:T(8,128)} %copy-done.19) | copy-start | bytes 294916
  222.9 17.3 %copy-start.82 = (bf16[768,16]{0,1:T(8,128)(2,1)S(1)}, bf16[768,16]{0,1:T(8,128)(2,1)}, u32[]{:S(2)}) copy-start(bf16[768,16]{0,1:T(8,128)(2,1)} %param.32) | copy-start | bytes 73732
  222.9 17.3 %copy-start.103 = (f32[32]{0:T(128)S(1)}, f32[32]{0:T(128)}, u32[]{:S(2)}) copy-start(f32[32]{0:T(128)} %copy-done.102) | copy-start | bytes 388
  222.9 18.3 %copy-start.113 = (f32[32]{0:T(128)S(1)}, f32[32]{0:T(128)}, u32[]{:S(2)}) copy-start(f32[32]{0:T(128)} %get-tuple-element.204) | copy-start | bytes 388
  222.9 16.9 %all-to-all-start.8 = ((bf16[8,32,1664]{2,1,0:T(8,128)(2,1)}), bf16[8,32,1664]{2,1,0:T(8,128)(2,1)S(1)}, u32[]{:S(2)}, u32[]{:S(2)}) async-start(bf16[8,32,1664]{2,1,0:T(8,128)(2,1)} %pad_maximum_fusion.2), calls=%async_computation.8 | async-start | bytes 1703936 | tf_op jit(solution)/shard_map/all_to_all | solution.py:55
  226.7 27.5 %copy-start.27 = (bf16[1,192,768]{2,1,0:T(8,128)(2,1)S(1)}, bf16[1,192,768]{2,1,0:T(8,128)(2,1)}, u32[]{:S(2)}) copy-start(bf16[1,192,768]{2,1,0:T(8,128)(2,1)} %param.26) | copy-start | bytes 884740
  240.2 14.3 %copy-start.92 = (f32[2,3,128]{2,1,0:T(4,128)S(1)}, f32[2,3,128]{2,1,0:T(4,128)}, u32[]{:S(2)}) copy-start(f32[2,3,128]{2,1,0:T(4,128)} %copy-done.91) | copy-start | bytes 9220
  259.2 11.9 %copy-start.86 = (f32[768]{0:T(1024)S(1)}, f32[768]{0:T(1024)}, u32[]{:S(2)}) copy-start(f32[768]{0:T(1024)} %copy-done.85) | copy-start | bytes 9220
  259.2 11.9 %copy-start.107 = (f32[32]{0:T(128)S(1)}, f32[32]{0:T(128)}, u32[]{:S(2)}) copy-start(f32[32]{0:T(128)} %copy-done.106) | copy-start | bytes 388
  259.2 12.6 %copy-start.64 = (f32[32,768]{1,0:T(8,128)S(1)}, f32[32,768]{1,0:T(8,128)}, u32[]{:S(2)}) copy-start(f32[32,768]{1,0:T(8,128)} %get-tuple-element.178) | copy-start | bytes 294916
  259.2 12.6 %copy-start.114 = (f32[32]{0:T(128)S(1)}, f32[32]{0:T(128)}, u32[]{:S(2)}) copy-start(f32[32]{0:T(128)} %get-tuple-element.202) | copy-start | bytes 388
  273.3 11.7 %all-to-all-start.12 = ((bf16[8,32,768]{2,1,0:T(8,128)(2,1)}), bf16[8,32,768]{2,1,0:T(8,128)(2,1)S(1)}, u32[]{:S(2)}, u32[]{:S(2)}) async-start(bf16[8,32,768]{2,1,0:T(8,128)(2,1)} %broadcast_in_dim.79), calls=%async_computation.12 | async-start | bytes 786432 | tf_op jit(solution)/shard_map/all_to_all | solution.py:62
  288.2 5.4 %copy-start.111 = (f32[32]{0:T(128)S(1)}, f32[32]{0:T(128)}, u32[]{:S(2)}) copy-start(f32[32]{0:T(128)} %get-tuple-element.192) | copy-start | bytes 388
  288.2 5.9 %copy-start.24 = (bf16[8,32,768]{2,1,0:T(8,128)(2,1)S(1)}, bf16[8,32,768]{2,1,0:T(8,128)(2,1)}, u32[]{:S(2)}) copy-start(bf16[8,32,768]{2,1,0:T(8,128)(2,1)} %copy-done.23) | copy-start | bytes 1179652
  290.1 11.8 %copy-start.84 = (f32[768]{0:T(1024)S(1)}, f32[768]{0:T(1024)}, u32[]{:S(2)}) copy-start(f32[768]{0:T(1024)} %copy-done.83) | copy-start | bytes 9220
  290.1 11.8 %copy-start.105 = (f32[32]{0:T(128)S(1)}, f32[32]{0:T(128)}, u32[]{:S(2)}) copy-start(f32[32]{0:T(128)} %copy-done.104) | copy-start | bytes 388
  290.1 11.7 %all-to-all-start.13 = ((bf16[8,32,768]{2,1,0:T(8,128)(2,1)}), bf16[8,32,768]{2,1,0:T(8,128)(2,1)S(1)}, u32[]{:S(2)}, u32[]{:S(2)}) async-start(bf16[8,32,768]{2,1,0:T(8,128)(2,1)} %bitcast.397), calls=%async_computation.13 | async-start | bytes 786432 | tf_op jit(solution)/shard_map/all_to_all | solution.py:55
  304.4 11.8 %copy-start.28 = (bf16[1,192,768]{2,1,0:T(8,128)(2,1)S(1)}, bf16[1,192,768]{2,1,0:T(8,128)(2,1)}, u32[]{:S(2)}) copy-start(bf16[1,192,768]{2,1,0:T(8,128)(2,1)} %param.26) | copy-start | bytes 884740
  304.4 11.8 %all-to-all-start.14 = ((bf16[8,32,768]{2,1,0:T(8,128)(2,1)}), bf16[8,32,768]{2,1,0:T(8,128)(2,1)S(1)}, u32[]{:S(2)}, u32[]{:S(2)}) async-start(bf16[8,32,768]{2,1,0:T(8,128)(2,1)} %broadcast_in_dim.80), calls=%async_computation.14 | async-start | bytes 786432 | tf_op jit(solution)/shard_map/all_to_all | solution.py:62
  308.0 8.6 %copy-start.63 = (bf16[2,128,3,64]{1,0,3,2:T(2,128)(2,1)S(1)}, bf16[2,128,3,64]{1,0,3,2:T(2,128)(2,1)}, u32[]{:S(2)}) copy-start(bf16[2,128,3,64]{1,0,3,2:T(2,128)(2,1)} %copy-done.62) | copy-start | bytes 294916
  308.0 165.0 %all-reduce.5.cloned.1.call-start = ((), (), s32[]{:S(2)}) async-start(), calls=%async_computation.17 | async-start | bytes 5898240 | tf_op jit(solution)/shard_map/psum | solution.py:258
  310.2 6.7 %copy-start.90 = (f32[2,3,128]{2,1,0:T(4,128)S(1)}, f32[2,3,128]{2,1,0:T(4,128)}, u32[]{:S(2)}) copy-start(f32[2,3,128]{2,1,0:T(4,128)} %copy-done.89) | copy-start | bytes 9220
  334.1 16.0 %all-to-all-start.9 = ((f32[8,32,768]{2,1,0:T(8,128)}), f32[8,32,768]{2,1,0:T(8,128)S(1)}, u32[]{:S(2)}, u32[]{:S(2)}) async-start(f32[8,32,768]{2,1,0:T(8,128)} %broadcast_in_dim.77), calls=%async_computation.9 | async-start | bytes 1572864 | tf_op jit(solution)/shard_map/all_to_all | solution.py:62
  338.3 15.3 %copy-start.60 = (bf16[32,768]{1,0:T(8,128)(2,1)S(1)}, bf16[32,768]{1,0:T(8,128)(2,1)}, u32[]{:S(2)}) copy-start(bf16[32,768]{1,0:T(8,128)(2,1)} %copy-done.59) | copy-start | bytes 147460
  338.3 15.5 %copy-start.94 = (f32[768]{0:T(1024)S(1)}, f32[768]{0:T(1024)}, u32[]{:S(2)}) copy-start(f32[768]{0:T(1024)} %get-tuple-element.146) | copy-start | bytes 9220
  338.3 15.5 %copy-start.95 = (f32[768]{0:T(1024)S(1)}, f32[768]{0:T(1024)}, u32[]{:S(2)}) copy-start(f32[768]{0:T(1024)} %get-tuple-element.148) | copy-start | bytes 9220
  338.3 15.5 %copy-start.74 = (s32[128,128]{0,1:T(8,128)S(1)}, s32[128,128]{0,1:T(8,128)}, u32[]{:S(2)}) copy-start(s32[128,128]{0,1:T(8,128)} %copy-done.73) | copy-start | bytes 196612
  338.3 23.6 %copy-start.110 = (f32[32]{0:T(128)S(1)}, f32[32]{0:T(128)}, u32[]{:S(2)}) copy-start(f32[32]{0:T(128)} %get-tuple-element.199) | copy-start | bytes 388
  339.4 23.6 %copy-start.112 = (f32[32]{0:T(128)S(1)}, f32[32]{0:T(128)}, u32[]{:S(2)}) copy-start(f32[32]{0:T(128)} %get-tuple-element.198) | copy-start | bytes 388
  350.1 11.7 %all-to-all-start.15 = ((bf16[8,32,768]{2,1,0:T(8,128)(2,1)}), bf16[8,32,768]{2,1,0:T(8,128)(2,1)S(1)}, u32[]{:S(2)}, u32[]{:S(2)}) async-start(bf16[8,32,768]{2,1,0:T(8,128)(2,1)} %bitcast.71), calls=%async_computation.15 | async-start | bytes 786432 | tf_op jit(solution)/shard_map/all_to_all | solution.py:55
  353.6 14.9 %copy-start.75 = (f32[3,128,128]{1,2,0:T(8,128)S(1)}, f32[3,128,128]{1,2,0:T(8,128)}, u32[]{:S(2)}) copy-start(f32[3,128,128]{1,2,0:T(8,128)} %get-tuple-element.169) | copy-start | bytes 589828
  364.8 107.3 %all-to-all-start.16 = ((bf16[8,32,768]{2,1,0:T(8,128)(2,1)}), bf16[8,32,768]{2,1,0:T(8,128)(2,1)S(1)}, u32[]{:S(2)}, u32[]{:S(2)}) async-start(bf16[8,32,768]{2,1,0:T(8,128)(2,1)} %broadcast_in_dim.81), calls=%async_computation.16 | async-start | bytes 786432 | tf_op jit(solution)/shard_map/all_to_all | solution.py:62
  473.0 4.6 copy-start.69
  473.0 5.4 %copy-start.55 = (bf16[768,384]{1,0:T(8,128)(2,1)S(1)}, bf16[768,384]{1,0:T(8,128)(2,1)}, u32[]{:S(2)}) copy-start(bf16[768,384]{1,0:T(8,128)(2,1)} %get-tuple-element.166) | copy-start | bytes 1769476
  (65 other events, 115.0 us)
Sparse Core Ops, SparseCore 0:
  324.7 92.3 all-reduce.4

commit v2 on v1

v2 whole, which is shorter than its diff:
```python
import functools

import jax
import jax.numpy as jnp
import numpy as np
from jax import lax
from jax.experimental import pallas as pl
from jax.experimental.pallas import tpu as pltpu
from jax.sharding import PartitionSpec as P

EPSILON = 1e-06
NEGATIVE = -1e30
BF16, F32 = jnp.bfloat16, jnp.float32
MESH = pl.DeviceIdType.MESH
HIGHEST = lax.Precision.HIGHEST

GAINS, TERM1, ROWS1, DENSE, ROWS2, TERM2, ROWS3, MOE, OUT, GRAD2, BACK2 = range(11)
GRAD1, BACK1, GRAD0, BACK0, INPUT, SMALL_A, SMALL_A2, SMALL_B, SMALL_B2 = range(11, 20)
DISPATCH, FORWARD, CORE, RETURN = 20, 24, 28, 32
DENSE_RS, DENSE_AG, ATTN_RS, ATTN_AG = 33, 34, 35, 36
SEMAPHORES = 37


def bucket_limits(count):
    exact = count // 2
    limits = []
    for level in range(1, count):
        if level < exact:
            limits.append(level)
        else:
            distance = exact
            while (
                min(
                    count - 1,
                    exact + int(np.floor(np.log(distance / exact) / np.log(128.0 / exact) * exact)),
                )
                < level
            ):
                distance += 1
            limits.append(distance)
    return limits


def dot(left, right, dims, precision=None):
    return lax.dot_general(
        left, right, (((dims[0],), (dims[1],)), ((), ())), precision=precision, preferred_element_type=F32
    )


def nn(left, right, precision=None):
    return dot(left, right, (1, 0), precision)


def nt(left, right, precision=None):
    return dot(left, right, (1, 1), precision)


def tn(left, right, precision=None):
    return dot(left, right, (0, 0), precision)


def low(value):
    return value.astype(BF16)


def full(value):
    return value.astype(F32)


def inverse_rms(rows):
    return lax.rsqrt(jnp.mean(rows * rows, axis=-1, keepdims=True) + EPSILON)


def normed(rows, gain):
    return low(rows * inverse_rms(rows) * gain)


def normed_back(rows, gain, grad):
    rho = inverse_rms(rows)
    scaled = grad * gain
    back = scaled * rho - rows * (rho * rho * rho) * jnp.mean(scaled * rows, axis=-1, keepdims=True)
    return back, jnp.sum(grad * rows * rho, axis=0, keepdims=True)


def gelu_parts(a):
    t = jnp.tanh(0.7978845608028654 * (a + 0.044715 * a * a * a))
    half = 0.5 * (1.0 + t)
    slope = half + 0.5 * a * (1.0 - t * t) * (0.7978845608028654 * (1.0 + 0.134145 * a * a))
    return a * half, slope


def kernel(
    c,
    x_ref,
    gy_ref,
    ints_ref,
    routes_ref,
    attn_gain_ref,
    ffn_gain_ref,
    table_ref,
    wq_ref,
    wk_ref,
    wv_ref,
    wo_ref,
    dense_gate_ref,
    dense_up_ref,
    dense_down_ref,
    router_ref,
    gate_ref,
    up_ref,
    down_ref,
    out_ref,
    input_ref,
    attn_ref,
    dense_ref,
    ge_gate_ref,
    ge_up_ref,
    ge_down_ref,
    small_ref,
    bias_grad_ref,
    send_sem,
    recv_sem,
    gains,
    bucket,
    bias,
    mask,
    n1,
    qkv,
    probs,
    o,
    do,
    dqkv,
    dsum,
    bias_rows,
    sends,
    recv4,
    recv8,
    rows1,
    rows2,
    rows3,
    grad2,
    grad1,
    grad0,
    chunk,
    hid1,
    gate1,
    up1,
    da1,
    du1,
    pick0,
    pick1,
    gate_slot,
    sx,
    rx,
    hid,
    da,
    du,
    cs,
    cr,
    rt,
    rb,
    moe_send,
    moe_recv,
    small,
    small_send,
    small_recv,
    small2_send,
    small2_recv,
    smallb_send,
    smallb_recv,
    smallb2_send,
    smallb2_recv,
    dense_own,
    dense_recv,
    attn_own,
    attn_recv,
):
    sections, experts, mps = c["section"], c["expert"], c["mp"]
    micro, length, heads, size, cap = c["micro"], c["length"], c["heads"], c["size"], c["cap"]
    width, ff = c["width"], c["ff"]
    group = sections * mps
    rows = micro * length
    part = rows // group
    half = width // sections
    local = heads * size
    scale = size**-0.5
    slots = micro * cap
    s, me, mp = lax.axis_index("section"), lax.axis_index("expert"), lax.axis_index("mp")
    place = s * mps + mp
    own = pl.ds(pl.multiple_of(place * part, part), part)
    mine = pl.ds(pl.multiple_of(s * half, 128), half)
    H2, Y1, H1, GRAD = 0, 1, 2, 3

    def on_expert(k):
        return {"expert": lax.rem(me + k, experts)}

    def in_group(p):
        return {"section": p // mps, "mp": lax.rem(p, mps)}

    def send(src, dst, phase, device, arrival=None):
        pltpu.make_async_remote_copy(
            src_ref=src,
            dst_ref=dst,
            send_sem=send_sem.at[phase],
            recv_sem=recv_sem.at[phase if arrival is None else arrival],
            device_id=device,
            device_id_type=MESH,
        ).start()

    def drain(sem, view):
        pltpu.make_async_copy(view, view, sem).wait()

    def arrived(phase, view):
        drain(recv_sem.at[phase], view)

    def left(phase, view):
        drain(send_sem.at[phase], view)

    barrier = pltpu.get_barrier_semaphore()
    for k in range(1, group):
        pl.semaphore_signal(barrier, inc=1, device_id=in_group(lax.rem(place + k, group)), device_id_type=MESH)
    for k in range(1, experts):
        pl.semaphore_signal(barrier, inc=1, device_id=on_expert(k), device_id_type=MESH)

    gains[s] = jnp.zeros((8, width), F32)
    gains[s, 0:1] = attn_gain_ref[...]
    gains[s, 1:2] = ffn_gain_ref[...]
    row_at = lax.broadcasted_iota(jnp.int32, (length, length), 0)
    col_at = lax.broadcasted_iota(jnp.int32, (length, length), 1)
    found = jnp.zeros((length, length), jnp.int32)
    for limit in bucket_limits(c["buckets"]):
        found = found + jnp.where(row_at - col_at >= limit, 1, 0)
    bucket[...] = found
    for h in range(heads):
        total = jnp.zeros((length, length), F32)
        for b in range(c["buckets"]):
            total = jnp.where(found == b, table_ref[b, h], total)
        bias[h] = total
    for m in range(micro):
        docs = jnp.broadcast_to(full(ints_ref[m : m + 1, :]), (length, length))
        same = (docs == jnp.transpose(docs)) & (col_at <= row_at)
        mask[m] = jnp.where(same, 1.0, 0.0)
    pl.semaphore_wait(barrier, group - 1 + experts - 1)
    send(gains.at[s], gains.at[s], GAINS, {"section": 1 - s})

    def gather_all(buf, phase):
        for k in range(1, group):
            send(buf.at[own], buf.at[own], phase, in_group(lax.rem(place + k, group)))

    def wait_all(buf, phase):
        arrived(phase, buf.at[pl.ds(0, (group - 1) * part)])

    def gather_to(target, buf, phase):
        for k in range(1, mps):
            send(buf.at[own], buf.at[own], phase, {"section": target, "mp": lax.rem(mp + k, mps)})

        @pl.when(s != target)
        def _():
            send(buf.at[own], buf.at[own], phase, {"section": 1 - s})

    def left_to(target, buf, phase):
        @pl.when(s != target)
        def _():
            left(phase, buf.at[pl.ds(0, mps * part)])

        @pl.when(s == target)
        def _():
            left(phase, buf.at[pl.ds(0, (mps - 1) * part)])

    def scatter(src, dst, phase):
        for k in range(1, group):
            p = lax.rem(place + k, group)
            send(src.at[pl.ds(pl.multiple_of(p * part, part), part)], dst.at[place], phase, in_group(p))
        dst[place] = src[own]

    def scatter_from(src, dst, phase):
        for k in range(1, group):
            p = lax.rem(place + k, group)
            send(src.at[pl.ds(pl.multiple_of(p * part, part), part)], dst.at[mp], phase, in_group(p))
        dst[mp] = src[own]

    def wait_from(source, dst, phase):
        @pl.when(s == source)
        def _():
            arrived(phase, dst.at[pl.ds(0, mps - 1)])

        @pl.when(s != source)
        def _():
            arrived(phase, dst)

    def total(ref, first=0, last=None):
        last = ref.shape[0] if last is None else last
        value = full(ref[first])
        for i in range(first + 1, last):
            value = value + full(ref[i])
        return value

    def attention(n_ref, out):
        for t, w in enumerate((wq_ref, wk_ref, wv_ref)):
            qkv[t] = low(nn(n_ref[...], w[...]))
        for m in range(micro):
            r = slice(m * length, (m + 1) * length)
            for h in range(heads):
                lanes = slice(h * size, (h + 1) * size)
                scores = nt(qkv[0, r, lanes], qkv[1, r, lanes]) * scale + bias[h]
                scores = jnp.where(mask[m] > 0, scores, NEGATIVE)
                e = jnp.exp(scores - jnp.max(scores, axis=-1, keepdims=True))
                p = e / jnp.sum(e, axis=-1, keepdims=True)
                probs[m * heads + h] = p
                o[r, lanes] = low(nn(low(p), qkv[2, r, lanes]))
        out[...] = low(nn(o[...], wo_ref[...]))

    def attention_back(g_ref, out):
        do[...] = low(nt(g_ref[...], wo_ref[...]))
        for m in range(micro):
            r = slice(m * length, (m + 1) * length)
            for h in range(heads):
                lanes = slice(h * size, (h + 1) * size)
                d, p = do[r, lanes], probs[m * heads + h]
                q, k, v = (qkv[t, r, lanes] for t in range(3))
                dp = nt(d, v)
                ds = low(p * (dp - jnp.sum(dp * p, axis=-1, keepdims=True)))
                dqkv[r, h * size : (h + 1) * size] = low(nn(ds, k) * scale)
                dqkv[r, local + h * size : local + (h + 1) * size] = low(tn(ds, q) * scale)
                dqkv[r, 2 * local + h * size : 2 * local + (h + 1) * size] = low(tn(low(p), d))
                dsum[h] = full(ds) if m == 0 else dsum[h] + full(ds)
        dn = nt(dqkv[:, 0:local], wq_ref[...]) + nt(dqkv[:, local : 2 * local], wk_ref[...])
        dn = dn + nt(dqkv[:, 2 * local : 3 * local], wv_ref[...])
        out[...] = low(dn)
        return dn

    def attention_weights(n_ref, g_ref):
        attn_own[:, 0 : 3 * local] = low(tn(n_ref[...], dqkv[...]))
        attn_own[:, 3 * local :] = low(tn(g_ref[...], o[...]))
        share(attn_own, attn_recv, ATTN_RS)
        found = bucket[...]
        for h in range(heads):
            held = dsum[h]
            for b in range(c["buckets"]):
                bias_rows[b : b + 1, :] = jnp.sum(jnp.where(found == b, held, 0.0), axis=0, keepdims=True)
            sums = nt(jnp.ones((8, length), F32), bias_rows[...], HIGHEST)
            smallb_send[1 + h : 2 + h, 0 : c["buckets"]] = sums[0:1]

    def piece(ref, p):
        step = width // experts
        at = pl.ds(pl.multiple_of(p * step, 16), step)
        return ref.at[:, at] if len(ref.shape) == 3 else ref.at[at]

    def share(src, dst, phase):
        for k in range(1, experts):
            p = lax.rem(me + k, experts)
            send(piece(src, p), dst.at[me], phase, on_expert(k))
        dst[me] = piece(src, me)[...]

    def hand_back(src, out, phase):
        piece(out, me)[...] = low(total(src))
        for k in range(1, experts):
            send(piece(out, me), piece(out, me), phase, on_expert(k))

    x = full(x_ref[...])
    @pl.when(s == 0)
    def _():
        n1[...] = normed(x, gains[0, 0:1])
        attention(n1, sends.at[0])
        scatter_from(sends.at[0], recv4.at[0], TERM1)

    arrived(GAINS, gains.at[1 - s])
    wait_from(0, recv4.at[0], TERM1)
    h1 = full(x_ref[own]) + total(recv4.at[0])
    chunk[H1] = h1
    rows1[own] = normed(h1, gains[0, 1:2])
    gather_all(rows1, ROWS1)
    wait_all(rows1, ROWS1)
    gate1[...] = nn(rows1[...], dense_gate_ref[...])
    up1[...] = nn(rows1[...], dense_up_ref[...])
    hid1[...] = low(gelu_parts(gate1[...])[0] * up1[...])
    sends[1] = low(nn(hid1[...], dense_down_ref[...]))
    scatter(sends.at[1], recv8.at[0], DENSE)
    arrived(DENSE, recv8.at[0, pl.ds(0, group - 1)])
    y1 = chunk[H1] + total(recv8.at[0])
    chunk[Y1] = y1
    rows2[own] = normed(y1, gains[1, 0:1])
    gather_to(1, rows2, ROWS2)

    @pl.when(s == 1)
    def _():
        wait_all(rows2, ROWS2)
        attention(rows2, sends.at[2])
        scatter_from(sends.at[2], recv4.at[1], TERM2)

    named = []
    before = low(jnp.where(row_at < col_at, 1.0, 0.0))
    expert_at = lax.broadcasted_iota(jnp.int32, (experts, length), 0)
    slot_at = full(lax.broadcasted_iota(jnp.int32, (cap, length), 0))
    for m in range(micro):
        hots = [
            jnp.where(expert_at == ints_ref[micro + 2 * m + ch : micro + 2 * m + ch + 1, :], 1.0, 0.0)
            for ch in range(2)
        ]
        rank = nn(low(hots[0] + hots[1]), before)
        for e in range(experts):
            fit = slot_at == rank[e : e + 1]
            at = slice(e * cap, (e + 1) * cap)
            pick0[m, at] = low(jnp.where(fit, hots[0][e : e + 1], 0.0))
            pick1[m, at] = low(jnp.where(fit, hots[1][e : e + 1], 0.0))
        named.append(hots)

    wait_from(1, recv4.at[1], TERM2)
    h2 = chunk[Y1] + total(recv4.at[1])
    chunk[H2] = h2
    rows3[own] = normed(h2, gains[1, 1:2])
    gather_all(rows3, ROWS3)
    wait_all(rows3, ROWS3)
    logits = nt(router_ref[...], rows3[...])
    for m in range(micro):
        hots = named[m]
        r = slice(m * length, (m + 1) * length)
        here = logits[:, r]
        l0 = jnp.sum(hots[0] * here, axis=0, keepdims=True)
        l1 = jnp.sum(hots[1] * here, axis=0, keepdims=True)
        top = jnp.maximum(l0, l1)
        e0, e1 = jnp.exp(l0 - top), jnp.exp(l1 - top)
        by_expert = (hots[0] * e0 + hots[1] * e1) / (e0 + e1)
        both = pick0[m] + pick1[m]
        for e in range(experts):
            at = slice(e * cap, (e + 1) * cap)
            gate = jnp.sum(full(both[at]) * by_expert[e : e + 1], axis=1, keepdims=True)
            gate_slot[m, at] = jnp.broadcast_to(gate, (cap, 128))
        place_rows = slice(m * cap, (m + 1) * cap)
        out_rows = low(nn(both, rows3[r, mine]))
        sx[:, place_rows, 0:half] = out_rows.reshape(experts, cap, half)
        out_rows = low(nn(both, gy_ref[r, mine]) * gate_slot[m][:, 0:1])
        sx[:, place_rows, half:] = out_rows.reshape(experts, cap, half)
    blocks = 4
    per = experts // blocks
    block = per * slots
    for k in range(1, experts):
        p = lax.rem(me + k, experts)
        send(sx.at[p], rx.at[s, pl.ds(k * slots, slots)], DISPATCH, {"expert": p}, DISPATCH + k // per)
    pltpu.make_async_copy(sx.at[me], rx.at[s, pl.ds(0, slots)], recv_sem.at[DISPATCH]).start()

    def forward(j):
        at = pl.ds(j * block, block)
        arrived(DISPATCH + j, rx.at[s, at])
        send(rx.at[s, at], rx.at[s, at], FORWARD + j, {"section": 1 - s})

    def give_back(j):
        at = pl.ds(j * block, block)
        arrived(CORE + j, cr.at[at])
        rt[at] = low(full(cs[s, at]) + full(cr[at]))
        for k in range(j * per, (j + 1) * per):
            src = rt.at[pl.ds(k * slots, slots)]
            if k == 0:
                pltpu.make_async_copy(src, rb.at[me], recv_sem.at[RETURN]).start()
            else:
                send(src, rb.at[me], RETURN, on_expert(experts - k))

    forward(0)
    for j in range(blocks):
        if j + 1 < blocks:
            forward(j + 1)
        at = pl.ds(j * block, block)
        arrived(FORWARD + j, rx.at[1 - s, at])
        x0, x1 = rx[0, at, 0:half], rx[1, at, 0:half]
        g0, g1 = rx[0, at, half:], rx[1, at, half:]
        a = nn(x0, gate_ref[0:half]) + nn(x1, gate_ref[half:])
        u = nn(x0, up_ref[0:half]) + nn(x1, up_ref[half:])
        d = nt(g0, down_ref[:, 0:half]) + nt(g1, down_ref[:, half:])
        value, slope = gelu_parts(a)
        hid[at] = low(value * u)
        da[at] = low(d * u * slope)
        du[at] = low(d * value)
        for side in range(sections):
            w = slice(side * half, (side + 1) * half)
            cs[side, at, 0:half] = low(nn(hid[at], down_ref[:, w]))
            cs[side, at, half:] = low(nt(da[at], gate_ref[w]) + nt(du[at], up_ref[w]))
        send(cs.at[1 - s, at], cr.at[at], CORE + j, {"section": 1 - s})
        if j > 0:
            give_back(j - 1)
    give_back(blocks - 1)
    for side in range(sections):
        w = slice(side * half, (side + 1) * half)
        ge_gate_ref[w] = low(tn(rx[side, :, 0:half], da[...]))
        ge_up_ref[w] = low(tn(rx[side, :, 0:half], du[...]))
        ge_down_ref[:, w] = low(tn(hid[...], rx[side, :, half:]))
    arrived(RETURN, rb)
    lane = lax.broadcasted_iota(jnp.int32, (length, 128), 1)
    for m in range(micro):
        r = slice(m * length, (m + 1) * length)
        held = rb[:, m * cap : (m + 1) * cap, :].reshape(experts * cap, width)
        scaled = low(full(held[:, 0:half]) * gate_slot[m][:, 0:1])
        first, second = tn(pick0[m], scaled), tn(pick1[m], scaled)
        gy = full(gy_ref[r, mine])
        t0 = jnp.sum(gy * first, axis=-1, keepdims=True)
        t1 = jnp.sum(gy * second, axis=-1, keepdims=True)
        moe_send[r, 0:half] = low(first + second)
        moe_send[r, half : 2 * half] = low(tn(pick0[m] + pick1[m], held[:, half:]))
        moe_send[r, 2 * half :] = low(jnp.where(lane == 0, t0, jnp.where(lane == 1, t1, 0.0)))
    scatter(moe_send, moe_recv, MOE)
    arrived(MOE, moe_recv.at[pl.ds(0, group - 1)])
    lower, upper = total(moe_recv, 0, mps), total(moe_recv, mps, group)
    h2 = chunk[H2]
    out_ref[own, 0:half] = low(h2[:, 0:half] + lower[:, 0:half])
    out_ref[own, half:] = low(h2[:, half:] + upper[:, 0:half])
    terms = lower[:, 2 * half :] + upper[:, 2 * half :]
    t0, t1 = terms[:, 0:1], terms[:, 1:2]
    here = routes_ref[own]
    expert_at = lax.broadcasted_iota(jnp.int32, (part, experts), 1)
    hot0 = jnp.where(expert_at == here[:, 0:1], 1.0, 0.0)
    hot1 = jnp.where(expert_at == here[:, 1:2], 1.0, 0.0)
    logits = nt(rows3[own], router_ref[...])
    l0 = jnp.sum(hot0 * logits, axis=-1, keepdims=True)
    l1 = jnp.sum(hot1 * logits, axis=-1, keepdims=True)
    top = jnp.maximum(l0, l1)
    e0, e1 = jnp.exp(l0 - top), jnp.exp(l1 - top)
    dlogits = hot0 * (t0 - e0 / (e0 + e1) * (t0 + t1)) + hot1 * (t1 - e1 / (e0 + e1) * (t0 + t1))
    dr = jnp.concatenate([lower[:, half : 2 * half], upper[:, half : 2 * half]], axis=1)
    dr = dr + nn(dlogits, full(router_ref[...]), HIGHEST)
    back, gain = normed_back(h2, gains[1, 1:2], dr)
    grad = full(gy_ref[own]) + back
    chunk[GRAD] = grad
    grad2[own] = low(grad)
    gather_to(1, grad2, GRAD2)
    small[...] = jnp.zeros_like(small)
    small[0:1] = gain
    small[8 : 8 + experts] = tn(dlogits, full(rows3[own]), HIGHEST)
    smallb_send[...] = jnp.zeros_like(smallb_send)
    gather_all(out_ref, OUT)

    @pl.when(s == 1)
    def _():
        wait_all(grad2, GRAD2)
        attention_back(grad2, sends.at[3])
        scatter_from(sends.at[3], recv4.at[2], BACK2)
        attention_weights(rows2, grad2)

    wait_from(1, recv4.at[2], BACK2)
    back, gain = normed_back(chunk[Y1], gains[1, 0:1], total(recv4.at[2]))
    small[1:2] = gain
    grad = chunk[GRAD] + back
    chunk[GRAD] = grad
    grad1[own] = low(grad)
    gather_all(grad1, GRAD1)
    wait_all(grad1, GRAD1)
    d = nt(grad1[...], dense_down_ref[...])
    value, slope = gelu_parts(gate1[...])
    da1[...] = low(d * up1[...] * slope)
    du1[...] = low(d * value)
    sends[4] = low(nt(da1[...], dense_gate_ref[...]) + nt(du1[...], dense_up_ref[...]))
    scatter(sends.at[4], recv8.at[1], BACK1)
    dense_own[0] = low(tn(rows1[...], da1[...]))
    dense_own[1] = low(tn(rows1[...], du1[...]))
    for side in range(sections):
        w = slice(side * half, (side + 1) * half)
        dense_own[2, side * ff : (side + 1) * ff] = low(tn(hid1[...], grad1[:, w]))
    share(dense_own, dense_recv, DENSE_RS)
    arrived(BACK1, recv8.at[1, pl.ds(0, group - 1)])
    back, gain = normed_back(chunk[H1], gains[0, 1:2], total(recv8.at[1]))
    small[2:3] = gain
    grad = chunk[GRAD] + back
    chunk[GRAD] = grad
    grad0[own] = low(grad)
    gather_to(0, grad0, GRAD0)
    small_send[...] = low(small[...])
    for k in range(1, group):
        send(small_send, small_recv.at[place], SMALL_A, in_group(lax.rem(place + k, group)))
    small_recv[place] = small_send[...]

    @pl.when(s == 0)
    def _():
        wait_all(grad0, GRAD0)
        dn = attention_back(grad0, sends.at[5])
        scatter_from(sends.at[5], recv4.at[3], BACK0)
        x = full(x_ref[...])
        smallb_send[0:1] = jnp.sum(dn * x * inverse_rms(x), axis=0, keepdims=True)
        attention_weights(n1, grad0)

    for k in range(1, experts):
        send(smallb_send, smallb_recv.at[me], SMALL_B, on_expert(k))
    smallb_recv[me] = smallb_send[...]
    arrived(SMALL_A, small_recv.at[pl.ds(0, group - 1)])
    small2_send[...] = low(total(small_recv))
    for k in range(1, experts):
        send(small2_send, small2_recv.at[me], SMALL_A2, on_expert(k))
    small2_recv[me] = small2_send[...]
    wait_from(0, recv4.at[3], BACK0)
    back, gain = normed_back(full(x_ref[own]), gains[0, 0:1], total(recv4.at[3]))
    input_ref[own] = low(chunk[GRAD] + back)
    gather_all(input_ref, INPUT)
    arrived(DENSE_RS, dense_recv.at[pl.ds(0, experts - 1)])
    hand_back(dense_recv, dense_ref, DENSE_AG)
    arrived(SMALL_B, smallb_recv.at[pl.ds(0, experts - 1)])
    smallb2_send[...] = total(smallb_recv)
    for k in range(1, mps):
        send(smallb2_send, smallb2_recv.at[mp], SMALL_B2, {"mp": lax.rem(mp + k, mps)})
    smallb2_recv[mp] = smallb2_send[...]
    arrived(ATTN_RS, attn_recv.at[pl.ds(0, experts - 1)])
    hand_back(attn_recv, attn_ref, ATTN_AG)
    arrived(SMALL_A2, small2_recv.at[pl.ds(0, experts - 1)])
    summed = total(small2_recv)
    bias_grad_ref[...] = smallb2_send[...]
    arrived(SMALL_B2, smallb2_recv.at[pl.ds(0, mps - 1)])
    gain0 = total(smallb2_recv)[0:1]
    small_ref[...] = summed
    small_ref[0:1] = jnp.where(s == 0, gain0, summed[1:2])
    small_ref[1:2] = jnp.where(s == 0, summed[2:3], summed[0:1])
    wait_all(out_ref, OUT)
    wait_all(input_ref, INPUT)
    others = pl.ds(0, width - width // experts)
    arrived(DENSE_AG, dense_ref.at[:, others])
    arrived(ATTN_AG, attn_ref.at[others])
    left(GAINS, gains.at[s])
    seven = pl.ds(0, (group - 1) * part)
    for phase, ref in ((ROWS1, rows1), (ROWS3, rows3), (OUT, out_ref), (GRAD1, grad1), (INPUT, input_ref)):
        left(phase, ref.at[seven])
    for phase, at in ((DENSE, 1), (BACK1, 4)):
        left(phase, sends.at[at, seven])
    left(MOE, moe_send.at[seven])
    left_to(1, rows2, ROWS2)
    left_to(1, grad2, GRAD2)
    left_to(0, grad0, GRAD0)

    @pl.when(s == 0)
    def _():
        left(TERM1, sends.at[0, seven])
        left(BACK0, sends.at[5, seven])

    @pl.when(s == 1)
    def _():
        left(TERM2, sends.at[2, seven])
        left(BACK2, sends.at[3, seven])

    left(DISPATCH, rx.at[0, pl.ds(0, (experts - 1) * slots)])
    for j in range(blocks):
        left(FORWARD + j, rx.at[0, pl.ds(0, block)])
        left(CORE + j, cr.at[pl.ds(0, block)])
    left(RETURN, rb.at[pl.ds(0, experts - 1)])
    left(SMALL_A, small_recv.at[pl.ds(0, group - 1)])
    left(SMALL_A2, small2_recv.at[pl.ds(0, experts - 1)])
    left(SMALL_B, smallb_recv.at[pl.ds(0, experts - 1)])
    left(SMALL_B2, smallb2_recv.at[pl.ds(0, mps - 1)])
    left(DENSE_RS, dense_recv.at[pl.ds(0, experts - 1)])
    left(DENSE_AG, dense_ref.at[:, others])
    left(ATTN_RS, attn_recv.at[pl.ds(0, experts - 1)])
    left(ATTN_AG, attn_ref.at[others])


def shards(
    block_input,
    segments,
    routes,
    cotangent,
    attn_gain,
    query_weight,
    key_weight,
    value_weight,
    out_weight,
    pos_bias,
    ffn_gain,
    dense_gate,
    dense_up,
    dense_down,
    router,
    expert_gate,
    expert_up,
    expert_down,
):
    micro, _, length, width = block_input.shape
    experts = router.shape[1]
    cap = 4 * length // experts
    buckets, heads = pos_bias.shape[1:]
    local = query_weight.shape[2]
    size = local // heads
    ff = dense_gate.shape[1]
    sections, mps = lax.axis_size("section"), lax.axis_size("mp")
    group = sections * mps
    rows = micro * length
    part = rows // group
    half = width // sections
    slots = micro * cap
    every = experts * slots
    step = width // experts
    c = dict(
        section=sections, expert=experts, mp=mps, micro=micro, length=length, heads=heads, size=size,
        cap=cap, width=width, ff=ff, buckets=buckets,
    )
    ints = jnp.concatenate(
        [segments[:, 0], routes[:, 0].transpose(0, 2, 1).reshape(2 * micro, length)], axis=0
    )
    ints = jnp.pad(ints, ((0, 8 - 3 * micro), (0, 0)))
    vmem = pl.BlockSpec(memory_space=pltpu.VMEM)
    smem = pl.BlockSpec(memory_space=pltpu.SMEM)

    def held(*shape):
        return pltpu.VMEM(shape, BF16)

    def exact(*shape):
        return pltpu.VMEM(shape, F32)

    scratch = [
        pltpu.SemaphoreType.DMA((SEMAPHORES,)),
        pltpu.SemaphoreType.DMA((SEMAPHORES,)),
        exact(sections, 8, width),
        pltpu.VMEM((length, length), jnp.int32),
        exact(heads, length, length),
        exact(micro, length, length),
        held(rows, width),
        held(3, rows, local),
        exact(micro * heads, length, length),
        held(rows, local),
        held(rows, local),
        held(rows, 3 * local),
        exact(heads, length, length),
        exact(buckets, length),
        held(6, rows, width),
        held(4, mps, part, width),
        held(2, group, part, width),
        held(rows, width),
        held(rows, width),
        held(rows, width),
        held(rows, width),
        held(rows, width),
        held(rows, width),
        exact(4, part, width),
        held(rows, ff),
        exact(rows, ff),
        exact(rows, ff),
        held(rows, ff),
        held(rows, ff),
        held(micro, experts * cap, length),
        held(micro, experts * cap, length),
        exact(micro, experts * cap, 128),
        held(experts, slots, 2 * half),
        held(sections, every, 2 * half),
        held(every, ff),
        held(every, ff),
        held(every, ff),
        held(sections, every, 2 * half),
        held(every, 2 * half),
        held(every, 2 * half),
        held(experts, slots, 2 * half),
        held(rows, 2 * half + 128),
        held(group, part, 2 * half + 128),
        exact(32, width),
        held(32, width),
        held(group, 32, width),
        held(32, width),
        held(experts, 32, width),
        exact(8, width),
        exact(experts, 8, width),
        exact(8, width),
        exact(mps, 8, width),
        held(3, width, ff),
        held(experts, 3, step, ff),
        held(width, 4 * local),
        held(experts, step, 4 * local),
    ]
    shape = jax.ShapeDtypeStruct
    block_output, input_grad, attn, dense, ge_gate, ge_up, ge_down, small, bias_grad = pl.pallas_call(
        functools.partial(kernel, c),
        out_shape=(
            shape((rows, width), BF16),
            shape((rows, width), BF16),
            shape((width, 4 * local), BF16),
            shape((3, width, ff), BF16),
            shape((width, ff), BF16),
            shape((width, ff), BF16),
            shape((ff, width), BF16),
            shape((32, width), F32),
            shape((8, width), F32),
        ),
        in_specs=[vmem] * 6 + [smem] + [vmem] * 11,
        out_specs=(vmem,) * 9,
        scratch_shapes=scratch,
        compiler_params=pltpu.CompilerParams(
            collective_id=0, has_side_effects=True, vmem_limit_bytes=60 * 1024 * 1024
        ),
    )(
        block_input.reshape(rows, width),
        cotangent.reshape(rows, width),
        ints,
        routes.reshape(rows, 2),
        attn_gain,
        ffn_gain,
        pos_bias[0],
        query_weight[0],
        key_weight[0],
        value_weight[0],
        out_weight[0],
        dense_gate,
        dense_up,
        dense_down,
        router.T,
        expert_gate[0],
        expert_up[0],
        expert_down[0],
    )
    attn, dense = attn.astype(F32), dense.astype(F32)
    return (
        block_output.astype(F32).reshape(block_input.shape),
        input_grad.astype(F32).reshape(block_input.shape),
        small[0:1],
        attn[None, :, 0:local],
        attn[None, :, local : 2 * local],
        attn[None, :, 2 * local : 3 * local],
        attn[:, 3 * local :].T[None],
        bias_grad[None, 1 : 1 + heads, 0:buckets].transpose(0, 2, 1),
        small[1:2],
        dense[0],
        dense[1],
        jnp.concatenate([dense[2, 0:ff], dense[2, ff:]], axis=1),
        small[8 : 8 + experts].T,
        ge_gate.astype(F32)[None],
        ge_up.astype(F32)[None],
        ge_down.astype(F32)[None],
    )


def solution(mesh):
    placed = (
        P(None, "expert", None, None),
        P(None, "expert", None),
        P(None, "expert", None, None),
        P(None, "expert", None, None),
        P("section", None),
        P("section", None, "mp"),
        P("section", None, "mp"),
        P("section", None, "mp"),
        P("section", "mp", None),
        P("section", None, "mp"),
        P("section", None),
        P(None, ("section", "mp")),
        P(None, ("section", "mp")),
        P(("section", "mp"), None),
        P(),
        P("expert", None, ("section", "mp")),
        P("expert", None, ("section", "mp")),
        P("expert", ("section", "mp"), None),
    )
    return jax.shard_map(
        shards,
        mesh=mesh,
        in_specs=placed,
        out_specs=(
            P(None, "expert", None, None),
            P(None, "expert", None, None),
            P("section", None),
            P("section", None, "mp"),
            P("section", None, "mp"),
            P("section", None, "mp"),
            P("section", "mp", None),
            P("section", None, "mp"),
            P("section", None),
            P(None, ("section", "mp")),
            P(None, ("section", "mp")),
            P(("section", "mp"), None),
            P(),
            P("expert", None, ("section", "mp")),
            P("expert", None, ("section", "mp")),
            P("expert", ("section", "mp"), None),
        ),
        check_vma=False,
    )
```

time: 499 us -> 234 us (0.47); the launches traced: 490 us -> 232 us
  blocking collectives: 218 us -> 0 us
  Pallas kernels: 0 us -> 207 us
  waiting for transfers between devices: 108 us -> 0 us
  matrix products: 52.4 us -> 0 us
  starting transfers between devices: 37.6 us -> 0 us
  other arithmetic: 33.5 us -> 7.87 us
  between operations: 16.3 us -> 0.74 us
  local copies, waits for them, and re-layouts: 23.8 us -> 17 us
    pallas_call x0 -> x1, Pallas kernels: none -> 207 us  [shards(): pl.pallas_call(functools.partial(kernel, c), out_shape=(shape((rows, widt...]
    all_to_all x7 -> x0, blocking collectives: 115 us -> none  [the longest x1 47.9 us: shards(): lax.all_to_all(sent, 'expert', 0, 0, tiled=True).reshape(-1, 2 * width)]
    all_to_all x10 -> x0, waiting for transfers between devices: 108 us -> none  [the longest x1 43.9 us: shards(): lax.all_to_all(back, 'expert', 0, 0, tiled=True)]
    psum x2 -> x0, blocking collectives: 101 us -> none  [the longest x1 64.9 us: shards(): g_gains, g_router = lax.psum((g_gains, g_router), everyone)]
    dot_general x65 -> x0, matrix products: 52.4 us -> none  [the longest x43 38.4 us: mm(): return jnp.dot(left, right, preferred_element_type=jnp.float32)]
    all_to_all x10 -> x0, starting transfers between devices: 37.5 us -> none  [the longest x5 17.9 us: collect(): lax.all_to_all(copies, GROUP, 0, 0, tiled=True).reshape(-1, rows.shape[1])]
    convert_element_type x14 -> x2, other arithmetic: 11.7 us -> 0.4 us  [shards(): attn, dense = (attn.astype(F32), dense.astype(F32))]
    reduce_sum x21 -> x0, other arithmetic: 7.19 us -> none  [the longest x4 3.06 us: inverse_rms(): return lax.rsqrt(jnp.mean(rows * rows, axis=-1, keepdims=True) + EPSILON)]
  transfers between devices with their start and end apart: 11 -> 0, of which waited for: 9 -> 0; matrix products, arithmetic and copies ran while one was open for 5% -> 0% of each run, Pallas kernels for 0% -> 0%
where the time goes in v2:
time: 234 us; the launch traced here: 232 us
  Pallas kernels  207 us (88%)
  local copies, waits for them, and re-layouts  17 us (7%)
  other arithmetic  7.87 us (3%)
    pallas_call x1, Pallas kernels, shards(): pl.pallas_call(functools.partial(kernel, c), out_shape=(shape((rows, widt...  207 us
    unnamed x25, local copies, waits for them, and re-layouts  11 us

profile of v2, /device:TPU:0, one launch (start us, length us, event | category | flops | bytes accessed | tf_op | source)
XLA Modules:
  0.0 232.3 jit_solution(10365453192684431615)
XLA Ops:
  0.6 0.0 copy-start.6
  0.7 0.7 pad_add_fusion
  1.4 0.6 pad.4.ints_ref
  2.0 1.5 copy.34
  3.5 1.4 copy.46
  4.8 1.9 copy.35
  6.7 1.9 copy.36
  8.6 0.0 copy-done.6
  8.6 0.9 copy.37
  9.5 206.7 %shard_map.297 = (bf16[256,768]{1,0:T(8,128)(2,1)}, bf16[256,768]{1,0:T(8,128)(2,1)}, bf16[768,768]{1,0:T(8,128)(2,1)}, bf16[3,768,384]{2,1,0:T(8,128)(2,1)}, bf...) custom-call(bf16[256,768]{1,0:T(8,128)(2,1)} %bitcast.70, ...), custom_call_target="tpu_custom_call" | custom-call | tf_op jit(solution)/shard_map/pallas_call | solution.py:759
  216.2 0.0 copy-start.5
  216.2 0.0 copy-start.7
  216.2 0.0 copy-start.1
  216.3 2.0 convert.6
  218.3 0.0 copy-done.5
  218.3 0.9 convert.8
  219.2 0.0 copy-done.7
  219.2 0.6 fusion
  219.8 0.0 copy-done.1
  219.8 0.2 convert_element_type.4
  220.0 0.5 slice_bitcast_fusion.2
  220.5 1.1 copy.41
  221.6 1.1 copy.42
  222.7 0.0 copy-start
  222.7 1.1 copy.43
  223.7 1.1 copy.44
  224.8 0.7 slice_bitcast_fusion.9
  225.5 0.6 copy.45
  226.0 0.0 copy-done
  226.0 0.2 convert_element_type.5
  226.3 1.6 slice_bitcast_fusion
  227.8 0.1 slice_bitcast_fusion.7
  227.9 0.0 copy-start.3
  227.9 0.0 copy-start.4
  227.9 1.1 pad_maximum_fusion
  229.0 0.6 slice_bitcast_fusion.8
  229.7 0.0 copy-done.3
  229.7 0.0 copy-done.4
  229.7 0.0 copy-start.2
  229.7 1.6 bitcast_convert_fusion.1
  231.2 0.0 copy-done.2
  231.2 1.1 bitcast_convert_fusion
Async XLA Ops:
  0.6 8.0 %copy-start.6 = (bf16[1,768,192]{1,2,0:T(8,128)(2,1)S(1)}, bf16[1,768,192]{1,2,0:T(8,128)(2,1)}, u32[]{:S(2)}) copy-start(bf16[1,768,192]{1,2,0:T(8,128)(2,1)} %param.25) | copy-start | bytes 884740
  216.2 2.1 copy-start.5
  216.2 3.0 %copy-start.7 = (f32[32,768]{1,0:T(8,128)S(1)}, f32[32,768]{1,0:T(8,128)}, u32[]{:S(2)}) copy-start(f32[32,768]{1,0:T(8,128)} %get-tuple-element.27) | copy-start | bytes 294916
  216.2 3.6 %copy-start.1 = (bf16[768,768]{1,0:T(8,128)(2,1)S(1)}, bf16[768,768]{1,0:T(8,128)(2,1)}, u32[]{:S(2)}) copy-start(bf16[768,768]{1,0:T(8,128)(2,1)} %get-tuple-element.28) | copy-start | bytes 3538948
  222.7 3.4 %copy-start = (bf16[3,768,384]{2,1,0:T(8,128)(2,1)S(1)}, bf16[3,768,384]{2,1,0:T(8,128)(2,1)}, u32[]{:S(2)}) copy-start(bf16[3,768,384]{2,1,0:T(8,128)(2,1)} %get-tuple-element.30) | copy-start | bytes 5308420
  227.9 1.7 copy-start.3
  227.9 1.7 copy-start.4
  229.7 1.6 copy-start.2

commit v3 on v2

--- a/solution.py
+++ b/solution.py
@@ -1,3 +1,4 @@
+import contextlib
 import functools
 
 import jax
@@ -17,8 +18,8 @@
 GAINS, TERM1, ROWS1, DENSE, ROWS2, TERM2, ROWS3, MOE, OUT, GRAD2, BACK2 = range(11)
 GRAD1, BACK1, GRAD0, BACK0, INPUT, SMALL_A, SMALL_A2, SMALL_B, SMALL_B2 = range(11, 20)
 DISPATCH, FORWARD, CORE, RETURN = 20, 24, 28, 32
-DENSE_RS, DENSE_AG, ATTN_RS, ATTN_AG = 33, 34, 35, 36
-SEMAPHORES = 37
+DENSE_SUM, ATTN_SUM = 33, 41
+SEMAPHORES = 49
 
 
 def bucket_limits(count):
@@ -93,7 +94,7 @@
     c,
     x_ref,
     gy_ref,
-    ints_ref,
+    docs_ref,
     routes_ref,
     attn_gain_ref,
     ffn_gain_ref,
@@ -102,20 +103,20 @@
     wk_ref,
     wv_ref,
     wo_ref,
-    dense_gate_ref,
-    dense_up_ref,
-    dense_down_ref,
     router_ref,
-    gate_ref,
-    up_ref,
-    down_ref,
+    dense_gate_hbm,
+    dense_up_hbm,
+    dense_down_hbm,
+    gate_hbm,
+    up_hbm,
+    down_hbm,
     out_ref,
     input_ref,
     attn_ref,
     dense_ref,
-    ge_gate_ref,
-    ge_up_ref,
-    ge_down_ref,
+    ge_gate_hbm,
+    ge_up_hbm,
+    ge_down_hbm,
     small_ref,
     bias_grad_ref,
     send_sem,
@@ -171,9 +172,29 @@
     smallb2_send,
     smallb2_recv,
     dense_own,
-    dense_recv,
+    dense_a1,
+    dense_b1,
+    dense_am,
+    dense_bm,
+    dense_a2,
+    dense_b2,
     attn_own,
-    attn_recv,
+    attn_a1,
+    attn_b1,
+    attn_am,
+    attn_bm,
+    attn_a2,
+    attn_b2,
+    dense_gate_ref,
+    dense_up_ref,
+    dense_down_ref,
+    gate_ref,
+    up_ref,
+    down_ref,
+    ge_gate_ref,
+    ge_up_ref,
+    ge_down_ref,
+    stage_sem,
 ):
     sections, experts, mps = c["section"], c["expert"], c["mp"]
     micro, length, heads, size, cap = c["micro"], c["length"], c["heads"], c["size"], c["cap"]
@@ -190,6 +211,39 @@
     own = pl.ds(pl.multiple_of(place * part, part), part)
     mine = pl.ds(pl.multiple_of(s * half, 128), half)
     H2, Y1, H1, GRAD = 0, 1, 2, 3
+    staged = [
+        pltpu.make_async_copy(src, dst, stage_sem.at[i])
+        for i, (src, dst) in enumerate(
+            (
+                (dense_gate_hbm, dense_gate_ref),
+                (dense_up_hbm, dense_up_ref),
+                (dense_down_hbm, dense_down_ref),
+                (gate_hbm, gate_ref),
+                (up_hbm, up_ref),
+                (down_hbm, down_ref),
+                (ge_gate_ref, ge_gate_hbm),
+                (ge_up_ref, ge_up_hbm),
+                (ge_down_ref, ge_down_hbm),
+            )
+        )
+    ]
+    for copy in staged[0:6]:
+        copy.start()
+    blocks = 4
+    per = experts // blocks
+    block = per * slots
+    side_size = c["side"]
+    slow, fast = me // side_size, lax.rem(me, side_size)
+
+    def at_offset(dz, dy):
+        z, y = lax.rem(slow + dz, side_size), lax.rem(fast + dy, side_size)
+        return z * side_size + y
+
+    scopes = contextlib.ExitStack()
+
+    def phase(name):
+        scopes.close()
+        scopes.enter_context(jax.named_scope(name))
 
     def on_expert(k):
         return {"expert": lax.rem(me + k, experts)}
@@ -197,12 +251,12 @@
     def in_group(p):
         return {"section": p // mps, "mp": lax.rem(p, mps)}
 
-    def send(src, dst, phase, device, arrival=None):
+    def send(src, dst, which, device, arrival=None):
         pltpu.make_async_remote_copy(
             src_ref=src,
             dst_ref=dst,
-            send_sem=send_sem.at[phase],
-            recv_sem=recv_sem.at[phase if arrival is None else arrival],
+            send_sem=send_sem.at[which],
+            recv_sem=recv_sem.at[which if arrival is None else arrival],
             device_id=device,
             device_id_type=MESH,
         ).start()
@@ -216,12 +270,14 @@
     def left(phase, view):
         drain(send_sem.at[phase], view)
 
+    phase("signals")
     barrier = pltpu.get_barrier_semaphore()
     for k in range(1, group):
         pl.semaphore_signal(barrier, inc=1, device_id=in_group(lax.rem(place + k, group)), device_id_type=MESH)
     for k in range(1, experts):
         pl.semaphore_signal(barrier, inc=1, device_id=on_expert(k), device_id_type=MESH)
 
+    phase("tables")
     gains[s] = jnp.zeros((8, width), F32)
     gains[s, 0:1] = attn_gain_ref[...]
     gains[s, 1:2] = ffn_gain_ref[...]
@@ -234,12 +290,13 @@
     for h in range(heads):
         total = jnp.zeros((length, length), F32)
         for b in range(c["buckets"]):
-            total = jnp.where(found == b, table_ref[b, h], total)
+            total = jnp.where(found == b, table_ref[h][:, b : b + 1], total)
         bias[h] = total
     for m in range(micro):
-        docs = jnp.broadcast_to(full(ints_ref[m : m + 1, :]), (length, length))
+        docs = jnp.broadcast_to(full(docs_ref[m : m + 1, :]), (length, length))
         same = (docs == jnp.transpose(docs)) & (col_at <= row_at)
         mask[m] = jnp.where(same, 1.0, 0.0)
+    phase("barrier")
     pl.semaphore_wait(barrier, group - 1 + experts - 1)
     send(gains.at[s], gains.at[s], GAINS, {"section": 1 - s})
 
@@ -295,44 +352,64 @@
             value = value + full(ref[i])
         return value
 
+    pairs = [
+        (m, h, slice(m * length, (m + 1) * length), slice(h * size, (h + 1) * size))
+        for m in range(micro)
+        for h in range(heads)
+    ]
+
     def attention(n_ref, out):
         for t, w in enumerate((wq_ref, wk_ref, wv_ref)):
-            qkv[t] = low(nn(n_ref[...], w[...]))
-        for m in range(micro):
-            r = slice(m * length, (m + 1) * length)
-            for h in range(heads):
-                lanes = slice(h * size, (h + 1) * size)
-                scores = nt(qkv[0, r, lanes], qkv[1, r, lanes]) * scale + bias[h]
-                scores = jnp.where(mask[m] > 0, scores, NEGATIVE)
-                e = jnp.exp(scores - jnp.max(scores, axis=-1, keepdims=True))
-                p = e / jnp.sum(e, axis=-1, keepdims=True)
-                probs[m * heads + h] = p
-                o[r, lanes] = low(nn(low(p), qkv[2, r, lanes]))
+            qkv[t] = low(nt(n_ref[...], w[...]))
+        tops, scores = [], []
+        for m, h, r, lanes in pairs:
+            raw = nt(qkv[0, r, lanes], qkv[1, r, lanes]) * scale + bias[h]
+            scores.append(jnp.where(mask[m] > 0, raw, NEGATIVE))
+        tops = [jnp.max(raw, axis=-1, keepdims=True) for raw in scores]
+        powers = [jnp.exp(raw - top) for raw, top in zip(scores, tops)]
+        sums = [jnp.sum(e, axis=-1, keepdims=True) for e in powers]
+        lows = []
+        for i, (m, h, r, lanes) in enumerate(pairs):
+            p = powers[i] / sums[i]
+            probs[m * heads + h] = p
+            lows.append(low(p))
+        for i, (m, h, r, lanes) in enumerate(pairs):
+            o[r, lanes] = low(nn(lows[i], qkv[2, r, lanes]))
         out[...] = low(nn(o[...], wo_ref[...]))
 
     def attention_back(g_ref, out):
         do[...] = low(nt(g_ref[...], wo_ref[...]))
-        for m in range(micro):
-            r = slice(m * length, (m + 1) * length)
-            for h in range(heads):
-                lanes = slice(h * size, (h + 1) * size)
-                d, p = do[r, lanes], probs[m * heads + h]
-                q, k, v = (qkv[t, r, lanes] for t in range(3))
-                dp = nt(d, v)
-                ds = low(p * (dp - jnp.sum(dp * p, axis=-1, keepdims=True)))
-                dqkv[r, h * size : (h + 1) * size] = low(nn(ds, k) * scale)
-                dqkv[r, local + h * size : local + (h + 1) * size] = low(tn(ds, q) * scale)
-                dqkv[r, 2 * local + h * size : 2 * local + (h + 1) * size] = low(tn(low(p), d))
-                dsum[h] = full(ds) if m == 0 else dsum[h] + full(ds)
-        dn = nt(dqkv[:, 0:local], wq_ref[...]) + nt(dqkv[:, local : 2 * local], wk_ref[...])
-        dn = dn + nt(dqkv[:, 2 * local : 3 * local], wv_ref[...])
+        dps = [nt(do[r, lanes], qkv[2, r, lanes]) for m, h, r, lanes in pairs]
+        for m, h, r, lanes in pairs:
+            dv = tn(low(probs[m * heads + h]), do[r, lanes])
+            dqkv[r, 2 * local + h * size : 2 * local + (h + 1) * size] = low(dv)
+        sums = [
+            jnp.sum(dp * probs[m * heads + h], axis=-1, keepdims=True)
+            for dp, (m, h, r, lanes) in zip(dps, pairs)
+        ]
+        grads = [
+            low(probs[m * heads + h] * (dp - total_row))
+            for dp, total_row, (m, h, r, lanes) in zip(dps, sums, pairs)
+        ]
+        for ds, (m, h, r, lanes) in zip(grads, pairs):
+            dqkv[r, h * size : (h + 1) * size] = low(nn(ds, qkv[1, r, lanes]) * scale)
+        for ds, (m, h, r, lanes) in zip(grads, pairs):
+            dqkv[r, local + h * size : local + (h + 1) * size] = low(tn(ds, qkv[0, r, lanes]) * scale)
+        for h in range(heads):
+            dsum[h] = sum(full(grads[m * heads + h]) for m in range(micro))
+        dn = nn(dqkv[:, 0:local], wq_ref[...]) + nn(dqkv[:, local : 2 * local], wk_ref[...])
+        dn = dn + nn(dqkv[:, 2 * local : 3 * local], wv_ref[...])
         out[...] = low(dn)
         return dn
 
     def attention_weights(n_ref, g_ref):
-        attn_own[:, 0 : 3 * local] = low(tn(n_ref[...], dqkv[...]))
-        attn_own[:, 3 * local :] = low(tn(g_ref[...], o[...]))
-        share(attn_own, attn_recv, ATTN_RS)
+        grads = low(tn(dqkv[...], n_ref[...]))
+        last = low(tn(o[...], g_ref[...]))
+        for t in range(width // 128):
+            lanes = slice(t * 128, (t + 1) * 128)
+            attn_own[t, 0 : 3 * local] = grads[:, lanes]
+            attn_own[t, 3 * local :] = last[:, lanes]
+        attn_sum[0]()
         found = bucket[...]
         for h in range(heads):
             held = dsum[h]
@@ -341,21 +418,77 @@
             sums = nt(jnp.ones((8, length), F32), bias_rows[...], HIGHEST)
             smallb_send[1 + h : 2 + h, 0 : c["buckets"]] = sums[0:1]
 
-    def piece(ref, p):
-        step = width // experts
-        at = pl.ds(pl.multiple_of(p * step, 16), step)
-        return ref.at[:, at] if len(ref.shape) == 3 else ref.at[at]
-
-    def share(src, dst, phase):
-        for k in range(1, experts):
-            p = lax.rem(me + k, experts)
-            send(piece(src, p), dst.at[me], phase, on_expert(k))
-        dst[me] = piece(src, me)[...]
-
-    def hand_back(src, out, phase):
-        piece(out, me)[...] = low(total(src))
-        for k in range(1, experts):
-            send(piece(out, me), piece(out, me), phase, on_expert(k))
+    def reducer(own, out, base, split, first_recv, middles, second_recv):
+        n = side_size
+        quarter, step = width // n, width // (n * n)
+        tiles = own.shape[0]
+
+        def half_of(i):
+            f, g = (fast, slow) if i == 0 else (slow, fast)
+            to_f = (lambda p: slow * n + p) if i == 0 else (lambda p: p * n + fast)
+            to_g = (lambda p: p * n + fast) if i == 0 else (lambda p: slow * n + p)
+            lanes = pl.ds(0, split) if i == 0 else pl.ds(split, tiles - split)
+            return f, g, to_f, to_g, lanes, base + i
+
+        def many(p, size):
+            return pl.ds(pl.multiple_of(p * size, 16), size)
+
+        def one():
+            for i in range(2):
+                f, g, to_f, to_g, lanes, which = half_of(i)
+                for k in range(1, n):
+                    p = lax.rem(f + k, n)
+                    src = own.at[lanes, many(p, quarter)]
+                    send(src, first_recv[i].at[f], which, {"expert": to_f(p)})
+                first_recv[i][f] = own[lanes, many(f, quarter)]
+
+        def two():
+            for i in range(2):
+                f, g, to_f, to_g, lanes, which = half_of(i)
+                arrived(which, first_recv[i].at[pl.ds(0, n - 1)])
+                middles[i][...] = low(total(first_recv[i]))
+                for k in range(1, n):
+                    p = lax.rem(g + k, n)
+                    src = middles[i].at[:, many(p, step)]
+                    send(src, second_recv[i].at[g], which + 2, {"expert": to_g(p)})
+                second_recv[i][g] = middles[i][:, many(g, step)]
+
+        def three():
+            for i in range(2):
+                f, g, to_f, to_g, lanes, which = half_of(i)
+                arrived(which + 2, second_recv[i].at[pl.ds(0, n - 1)])
+                at = out.at[lanes, many(f * n + g, step)]
+                at[...] = low(total(second_recv[i]))
+                for k in range(1, n):
+                    send(at, at, which + 4, {"expert": to_g(lax.rem(g + k, n))})
+
+        def four():
+            for i in range(2):
+                f, g, to_f, to_g, lanes, which = half_of(i)
+                arrived(which + 4, second_recv[i].at[pl.ds(0, n - 1)])
+                at = out.at[lanes, many(f, quarter)]
+                for k in range(1, n):
+                    send(at, at, which + 6, {"expert": to_f(lax.rem(f + k, n))})
+
+        def five():
+            for i in range(2):
+                arrived(base + i + 6, first_recv[i].at[pl.ds(0, n - 1)])
+
+        def done():
+            for i in range(2):
+                for stage in range(4):
+                    ref = (first_recv, second_recv, second_recv, first_recv)[stage][i]
+                    left(base + i + 2 * stage, ref.at[pl.ds(0, n - 1)])
+
+        return one, two, three, four, five, done
+
+    phase("attention1")
+    dense_sum = reducer(
+        dense_own, dense_ref, DENSE_SUM, 5, (dense_a1, dense_b1), (dense_am, dense_bm), (dense_a2, dense_b2)
+    )
+    attn_sum = reducer(
+        attn_own, attn_ref, ATTN_SUM, 3, (attn_a1, attn_b1), (attn_am, attn_bm), (attn_a2, attn_b2)
+    )
 
     x = full(x_ref[...])
     @pl.when(s == 0)
@@ -364,37 +497,47 @@
         attention(n1, sends.at[0])
         scatter_from(sends.at[0], recv4.at[0], TERM1)
 
+    phase("term1_wait")
     arrived(GAINS, gains.at[1 - s])
     wait_from(0, recv4.at[0], TERM1)
+    phase("norm1")
     h1 = full(x_ref[own]) + total(recv4.at[0])
     chunk[H1] = h1
     rows1[own] = normed(h1, gains[0, 1:2])
     gather_all(rows1, ROWS1)
+    phase("rows1_wait")
     wait_all(rows1, ROWS1)
+    phase("dense")
+    for copy in staged[0:3]:
+        copy.wait()
     gate1[...] = nn(rows1[...], dense_gate_ref[...])
     up1[...] = nn(rows1[...], dense_up_ref[...])
     hid1[...] = low(gelu_parts(gate1[...])[0] * up1[...])
     sends[1] = low(nn(hid1[...], dense_down_ref[...]))
     scatter(sends.at[1], recv8.at[0], DENSE)
+    phase("dense_wait")
     arrived(DENSE, recv8.at[0, pl.ds(0, group - 1)])
+    phase("norm2")
     y1 = chunk[H1] + total(recv8.at[0])
     chunk[Y1] = y1
     rows2[own] = normed(y1, gains[1, 0:1])
     gather_to(1, rows2, ROWS2)
 
+    phase("attention2")
     @pl.when(s == 1)
     def _():
         wait_all(rows2, ROWS2)
         attention(rows2, sends.at[2])
         scatter_from(sends.at[2], recv4.at[1], TERM2)
 
+    phase("routing")
     named = []
     before = low(jnp.where(row_at < col_at, 1.0, 0.0))
     expert_at = lax.broadcasted_iota(jnp.int32, (experts, length), 0)
     slot_at = full(lax.broadcasted_iota(jnp.int32, (cap, length), 0))
     for m in range(micro):
         hots = [
-            jnp.where(expert_at == ints_ref[micro + 2 * m + ch : micro + 2 * m + ch + 1, :], 1.0, 0.0)
+            jnp.where(expert_at == routes_ref[2 * m + ch : 2 * m + ch + 1, :], 1.0, 0.0)
             for ch in range(2)
         ]
         rank = nn(low(hots[0] + hots[1]), before)
@@ -405,12 +548,16 @@
             pick1[m, at] = low(jnp.where(fit, hots[1][e : e + 1], 0.0))
         named.append(hots)
 
+    phase("term2_wait")
     wait_from(1, recv4.at[1], TERM2)
+    phase("norm3")
     h2 = chunk[Y1] + total(recv4.at[1])
     chunk[H2] = h2
     rows3[own] = normed(h2, gains[1, 1:2])
     gather_all(rows3, ROWS3)
+    phase("rows3_wait")
     wait_all(rows3, ROWS3)
+    phase("slots")
     logits = nt(router_ref[...], rows3[...])
     for m in range(micro):
         hots = named[m]
@@ -431,13 +578,25 @@
         sx[:, place_rows, 0:half] = out_rows.reshape(experts, cap, half)
         out_rows = low(nn(both, gy_ref[r, mine]) * gate_slot[m][:, 0:1])
         sx[:, place_rows, half:] = out_rows.reshape(experts, cap, half)
-    blocks = 4
-    per = experts // blocks
-    block = per * slots
-    for k in range(1, experts):
-        p = lax.rem(me + k, experts)
-        send(sx.at[p], rx.at[s, pl.ds(k * slots, slots)], DISPATCH, {"expert": p}, DISPATCH + k // per)
-    pltpu.make_async_copy(sx.at[me], rx.at[s, pl.ds(0, slots)], recv_sem.at[DISPATCH]).start()
+    if side_size == 4:
+        offsets = [(0, 1), (0, 3), (1, 0), (3, 0), (1, 1), (3, 3), (1, 3), (3, 1)]
+        offsets += [(2, 1), (2, 3), (1, 2), (3, 2), (0, 0), (0, 2), (2, 0), (2, 2)]
+    else:
+        offsets = [(a, b) for a in range(side_size) for b in range(side_size)]
+
+    def dispatch(j):
+        for k in range(j * per, (j + 1) * per):
+            to = rx.at[s, pl.ds(k * slots, slots)]
+            if offsets[k] == (0, 0):
+                pltpu.make_async_copy(sx.at[me], to, recv_sem.at[DISPATCH + j]).start()
+            else:
+                p = at_offset(*offsets[k])
+                send(sx.at[p], to, DISPATCH + j, {"expert": p})
+
+    def dispatched(j):
+        count = sum(offsets[k] != (0, 0) for k in range(j * per, (j + 1) * per))
+        if count:
+            left(DISPATCH + j, rx.at[0, pl.ds(0, count * slots)])
 
     def forward(j):
         at = pl.ds(j * block, block)
@@ -450,17 +609,25 @@
         rt[at] = low(full(cs[s, at]) + full(cr[at]))
         for k in range(j * per, (j + 1) * per):
             src = rt.at[pl.ds(k * slots, slots)]
-            if k == 0:
+            if offsets[k] == (0, 0):
                 pltpu.make_async_copy(src, rb.at[me], recv_sem.at[RETURN]).start()
             else:
-                send(src, rb.at[me], RETURN, on_expert(experts - k))
-
+                dz, dy = offsets[k]
+                send(src, rb.at[me], RETURN, {"expert": at_offset(side_size - dz, side_size - dy)})
+
+    phase("dispatch_wait")
+    dispatch(0)
+    dispatch(1)
     forward(0)
+    dispatched(0)
+    dispatch(2)
+    for copy in staged[3:6]:
+        copy.wait()
     for j in range(blocks):
-        if j + 1 < blocks:
-            forward(j + 1)
         at = pl.ds(j * block, block)
+        phase("forward_wait%d" % j)
         arrived(FORWARD + j, rx.at[1 - s, at])
+        phase("expert%d" % j)
         x0, x1 = rx[0, at, 0:half], rx[1, at, 0:half]
         g0, g1 = rx[0, at, half:], rx[1, at, half:]
         a = nn(x0, gate_ref[0:half]) + nn(x1, gate_ref[half:])
@@ -475,15 +642,26 @@
             cs[side, at, 0:half] = low(nn(hid[at], down_ref[:, w]))
             cs[side, at, half:] = low(nt(da[at], gate_ref[w]) + nt(du[at], up_ref[w]))
         send(cs.at[1 - s, at], cr.at[at], CORE + j, {"section": 1 - s})
+        phase("give_back%d" % j)
+        if j + 1 < blocks:
+            forward(j + 1)
+            dispatched(j + 1)
+            if j + 3 < blocks:
+                dispatch(j + 3)
         if j > 0:
             give_back(j - 1)
     give_back(blocks - 1)
+    phase("expert_weights")
     for side in range(sections):
         w = slice(side * half, (side + 1) * half)
         ge_gate_ref[w] = low(tn(rx[side, :, 0:half], da[...]))
         ge_up_ref[w] = low(tn(rx[side, :, 0:half], du[...]))
         ge_down_ref[:, w] = low(tn(hid[...], rx[side, :, half:]))
+    for copy in staged[6:]:
+        copy.start()
+    phase("return_wait")
     arrived(RETURN, rb)
+    phase("combine")
     lane = lax.broadcasted_iota(jnp.int32, (length, 128), 1)
     for m in range(micro):
         r = slice(m * length, (m + 1) * length)
@@ -497,17 +675,21 @@
         moe_send[r, half : 2 * half] = low(tn(pick0[m] + pick1[m], held[:, half:]))
         moe_send[r, 2 * half :] = low(jnp.where(lane == 0, t0, jnp.where(lane == 1, t1, 0.0)))
     scatter(moe_send, moe_recv, MOE)
+    phase("moe_wait")
     arrived(MOE, moe_recv.at[pl.ds(0, group - 1)])
+    phase("norm3_back")
     lower, upper = total(moe_recv, 0, mps), total(moe_recv, mps, group)
     h2 = chunk[H2]
     out_ref[own, 0:half] = low(h2[:, 0:half] + lower[:, 0:half])
     out_ref[own, half:] = low(h2[:, half:] + upper[:, 0:half])
     terms = lower[:, 2 * half :] + upper[:, 2 * half :]
     t0, t1 = terms[:, 0:1], terms[:, 1:2]
-    here = routes_ref[own]
-    expert_at = lax.broadcasted_iota(jnp.int32, (part, experts), 1)
-    hot0 = jnp.where(expert_at == here[:, 0:1], 1.0, 0.0)
-    hot1 = jnp.where(expert_at == here[:, 1:2], 1.0, 0.0)
+    ahead = lax.rem(place * part, length)
+    token = lax.broadcasted_iota(jnp.int32, (part, length), 1)
+    is_own = low(jnp.where(token == lax.broadcasted_iota(jnp.int32, (part, length), 0) + ahead, 1.0, 0.0))
+    hot0, hot1 = (
+        nt(is_own, low(jnp.where(place * part < length, named[0][ch], named[1][ch]))) for ch in range(2)
+    )
     logits = nt(rows3[own], router_ref[...])
     l0 = jnp.sum(hot0 * logits, axis=-1, keepdims=True)
     l1 = jnp.sum(hot1 * logits, axis=-1, keepdims=True)
@@ -527,6 +709,7 @@
     smallb_send[...] = jnp.zeros_like(smallb_send)
     gather_all(out_ref, OUT)
 
+    phase("attention2_back")
     @pl.when(s == 1)
     def _():
         wait_all(grad2, GRAD2)
@@ -534,27 +717,39 @@
         scatter_from(sends.at[3], recv4.at[2], BACK2)
         attention_weights(rows2, grad2)
 
+    phase("back2_wait")
     wait_from(1, recv4.at[2], BACK2)
+    phase("norm2_back")
     back, gain = normed_back(chunk[Y1], gains[1, 0:1], total(recv4.at[2]))
     small[1:2] = gain
     grad = chunk[GRAD] + back
     chunk[GRAD] = grad
     grad1[own] = low(grad)
     gather_all(grad1, GRAD1)
+    phase("grad1_wait")
     wait_all(grad1, GRAD1)
+    phase("dense_back")
     d = nt(grad1[...], dense_down_ref[...])
     value, slope = gelu_parts(gate1[...])
     da1[...] = low(d * up1[...] * slope)
     du1[...] = low(d * value)
     sends[4] = low(nt(da1[...], dense_gate_ref[...]) + nt(du1[...], dense_up_ref[...]))
     scatter(sends.at[4], recv8.at[1], BACK1)
-    dense_own[0] = low(tn(rows1[...], da1[...]))
-    dense_own[1] = low(tn(rows1[...], du1[...]))
-    for side in range(sections):
-        w = slice(side * half, (side + 1) * half)
-        dense_own[2, side * ff : (side + 1) * ff] = low(tn(hid1[...], grad1[:, w]))
-    share(dense_own, dense_recv, DENSE_RS)
+    phase("dense_weights")
+    gate_grad = low(tn(rows1[...], da1[...]))
+    up_grad = low(tn(rows1[...], du1[...]))
+    for t in range(ff // 128):
+        lanes = slice(t * 128, (t + 1) * 128)
+        dense_own[t] = gate_grad[:, lanes]
+        dense_own[ff // 128 + t] = up_grad[:, lanes]
+    down_grad = low(tn(hid1[...], grad1[...]))
+    for t in range(width // 128):
+        at = slice(t % 2 * ff, t % 2 * ff + ff)
+        dense_own[2 * (ff // 128) + t // 2, at] = down_grad[:, t * 128 : (t + 1) * 128]
+    dense_sum[0]()
+    phase("back1_wait")
     arrived(BACK1, recv8.at[1, pl.ds(0, group - 1)])
+    phase("norm1_back")
     back, gain = normed_back(chunk[H1], gains[0, 1:2], total(recv8.at[1]))
     small[2:3] = gain
     grad = chunk[GRAD] + back
@@ -566,6 +761,7 @@
         send(small_send, small_recv.at[place], SMALL_A, in_group(lax.rem(place + k, group)))
     small_recv[place] = small_send[...]
 
+    phase("attention1_back")
     @pl.when(s == 0)
     def _():
         wait_all(grad0, GRAD0)
@@ -573,42 +769,82 @@
         scatter_from(sends.at[5], recv4.at[3], BACK0)
         x = full(x_ref[...])
         smallb_send[0:1] = jnp.sum(dn * x * inverse_rms(x), axis=0, keepdims=True)
+
+    @pl.when(s == 1)
+    def _():
+        for stage in attn_sum[1:]:
+            stage()
+
+    phase("dense_two")
+    dense_sum[1]()
+
+    phase("attn_one")
+    @pl.when(s == 0)
+    def _():
         attention_weights(n1, grad0)
 
+    phase("dense_three")
+    dense_sum[2]()
     for k in range(1, experts):
         send(smallb_send, smallb_recv.at[me], SMALL_B, on_expert(k))
     smallb_recv[me] = smallb_send[...]
+    phase("back0_wait")
+    wait_from(0, recv4.at[3], BACK0)
+    phase("norm0_back")
+    back, gain = normed_back(full(x_ref[own]), gains[0, 0:1], total(recv4.at[3]))
+    input_ref[own] = low(chunk[GRAD] + back)
+    gather_all(input_ref, INPUT)
+    phase("attn_two")
+    @pl.when(s == 0)
+    def _():
+        attn_sum[1]()
+
+    phase("dense_four")
+    dense_sum[3]()
+    phase("small_a")
     arrived(SMALL_A, small_recv.at[pl.ds(0, group - 1)])
     small2_send[...] = low(total(small_recv))
     for k in range(1, experts):
         send(small2_send, small2_recv.at[me], SMALL_A2, on_expert(k))
     small2_recv[me] = small2_send[...]
-    wait_from(0, recv4.at[3], BACK0)
-    back, gain = normed_back(full(x_ref[own]), gains[0, 0:1], total(recv4.at[3]))
-    input_ref[own] = low(chunk[GRAD] + back)
-    gather_all(input_ref, INPUT)
-    arrived(DENSE_RS, dense_recv.at[pl.ds(0, experts - 1)])
-    hand_back(dense_recv, dense_ref, DENSE_AG)
+    phase("attn_three")
+    @pl.when(s == 0)
+    def _():
+        attn_sum[2]()
+
+    phase("small_b")
     arrived(SMALL_B, smallb_recv.at[pl.ds(0, experts - 1)])
     smallb2_send[...] = total(smallb_recv)
     for k in range(1, mps):
         send(smallb2_send, smallb2_recv.at[mp], SMALL_B2, {"mp": lax.rem(mp + k, mps)})
     smallb2_recv[mp] = smallb2_send[...]
-    arrived(ATTN_RS, attn_recv.at[pl.ds(0, experts - 1)])
-    hand_back(attn_recv, attn_ref, ATTN_AG)
+    phase("attn_four")
+    @pl.when(s == 0)
+    def _():
+        attn_sum[3]()
+
     arrived(SMALL_A2, small2_recv.at[pl.ds(0, experts - 1)])
     summed = total(small2_recv)
-    bias_grad_ref[...] = smallb2_send[...]
+    for h in range(heads):
+        bias_grad_ref[h] = smallb2_send[1 + h : 2 + h, 0 : c["buckets"]]
     arrived(SMALL_B2, smallb2_recv.at[pl.ds(0, mps - 1)])
     gain0 = total(smallb2_recv)[0:1]
     small_ref[...] = summed
     small_ref[0:1] = jnp.where(s == 0, gain0, summed[1:2])
     small_ref[1:2] = jnp.where(s == 0, summed[2:3], summed[0:1])
+    phase("last_waits")
     wait_all(out_ref, OUT)
     wait_all(input_ref, INPUT)
-    others = pl.ds(0, width - width // experts)
-    arrived(DENSE_AG, dense_ref.at[:, others])
-    arrived(ATTN_AG, attn_ref.at[others])
+    dense_sum[4]()
+
+    @pl.when(s == 0)
+    def _():
+        attn_sum[4]()
+        attn_sum[5]()
+
+    for copy in staged[6:]:
+        copy.wait()
+    dense_sum[5]()
     left(GAINS, gains.at[s])
     seven = pl.ds(0, (group - 1) * part)
     for phase, ref in ((ROWS1, rows1), (ROWS3, rows3), (OUT, out_ref), (GRAD1, grad1), (INPUT, input_ref)):
@@ -630,7 +866,6 @@
         left(TERM2, sends.at[2, seven])
         left(BACK2, sends.at[3, seven])
 
-    left(DISPATCH, rx.at[0, pl.ds(0, (experts - 1) * slots)])
     for j in range(blocks):
         left(FORWARD + j, rx.at[0, pl.ds(0, block)])
         left(CORE + j, cr.at[pl.ds(0, block)])
@@ -639,10 +874,28 @@
     left(SMALL_A2, small2_recv.at[pl.ds(0, experts - 1)])
     left(SMALL_B, smallb_recv.at[pl.ds(0, experts - 1)])
     left(SMALL_B2, smallb2_recv.at[pl.ds(0, mps - 1)])
-    left(DENSE_RS, dense_recv.at[pl.ds(0, experts - 1)])
-    left(DENSE_AG, dense_ref.at[:, others])
-    left(ATTN_RS, attn_recv.at[pl.ds(0, experts - 1)])
-    left(ATTN_AG, attn_ref.at[others])
+    scopes.close()
+
+
+def widen(tiles, experts, out, back, attn, gate, up, down, e_gate, e_up, e_down, small, bias, *to):
+    to[0][...] = full(out[...])
+    to[1][...] = full(back[...])
+    for t in range(2 * tiles):
+        lanes = slice(t * 128, (t + 1) * 128)
+        for which in range(4):
+            to[2 + which][:, lanes] = full(attn[t, which])
+        to[8][:, lanes] = full(down[t // 2, t % 2])
+    for t in range(tiles):
+        lanes = slice(t * 128, (t + 1) * 128)
+        to[6][:, lanes] = full(gate[t])
+        to[7][:, lanes] = full(up[t])
+    to[9][...] = full(e_gate[...])
+    to[10][...] = full(e_up[...])
+    to[11][...] = full(e_down[...])
+    to[12][...] = small[0:1]
+    to[13][...] = small[1:2]
+    to[14][...] = small[8 : 8 + experts]
+    to[15][...] = bias[...]
 
 
 def shards(
@@ -680,16 +933,14 @@
     slots = micro * cap
     every = experts * slots
     step = width // experts
+    side = int(np.sqrt(experts))
     c = dict(
+        side=side,
         section=sections, expert=experts, mp=mps, micro=micro, length=length, heads=heads, size=size,
         cap=cap, width=width, ff=ff, buckets=buckets,
     )
-    ints = jnp.concatenate(
-        [segments[:, 0], routes[:, 0].transpose(0, 2, 1).reshape(2 * micro, length)], axis=0
-    )
-    ints = jnp.pad(ints, ((0, 8 - 3 * micro), (0, 0)))
     vmem = pl.BlockSpec(memory_space=pltpu.VMEM)
-    smem = pl.BlockSpec(memory_space=pltpu.SMEM)
+    hbm = pl.BlockSpec(memory_space=pl.ANY)
 
     def held(*shape):
         return pltpu.VMEM(shape, BF16)
@@ -750,10 +1001,30 @@
         exact(experts, 8, width),
         exact(8, width),
         exact(mps, 8, width),
-        held(3, width, ff),
-        held(experts, 3, step, ff),
-        held(width, 4 * local),
-        held(experts, step, 4 * local),
+        held(9, width, 128),
+        held(side, 5, width // side, 128),
+        held(side, 4, width // side, 128),
+        held(5, width // side, 128),
+        held(4, width // side, 128),
+        held(side, 5, step, 128),
+        held(side, 4, step, 128),
+        held(6, width, 128),
+        held(side, 3, width // side, 128),
+        held(side, 3, width // side, 128),
+        held(3, width // side, 128),
+        held(3, width // side, 128),
+        held(side, 3, step, 128),
+        held(side, 3, step, 128),
+        held(width, ff),
+        held(width, ff),
+        held(ff, width),
+        held(width, ff),
+        held(width, ff),
+        held(ff, width),
+        held(width, ff),
+        held(width, ff),
+        held(ff, width),
+        pltpu.SemaphoreType.DMA((9,)),
     ]
     shape = jax.ShapeDtypeStruct
     block_output, input_grad, attn, dense, ge_gate, ge_up, ge_down, small, bias_grad = pl.pallas_call(
@@ -761,16 +1032,16 @@
         out_shape=(
             shape((rows, width), BF16),
             shape((rows, width), BF16),
-            shape((width, 4 * local), BF16),
-            shape((3, width, ff), BF16),
+            shape((6, 4 * local, 128), BF16),
+            shape((9, width, 128), BF16),
             shape((width, ff), BF16),
             shape((width, ff), BF16),
             shape((ff, width), BF16),
             shape((32, width), F32),
-            shape((8, width), F32),
+            shape((heads, 1, buckets), F32),
         ),
-        in_specs=[vmem] * 6 + [smem] + [vmem] * 11,
-        out_specs=(vmem,) * 9,
+        in_specs=[vmem] * 12 + [hbm] * 6,
+        out_specs=(vmem,) * 4 + (hbm,) * 3 + (vmem,) * 2,
         scratch_shapes=scratch,
         compiler_params=pltpu.CompilerParams(
             collective_id=0, has_side_effects=True, vmem_limit_bytes=60 * 1024 * 1024
@@ -778,41 +1049,110 @@
     )(
         block_input.reshape(rows, width),
         cotangent.reshape(rows, width),
-        ints,
-        routes.reshape(rows, 2),
+        segments.reshape(micro, length),
+        routes[:, 0].transpose(0, 2, 1).reshape(2 * micro, length),
         attn_gain,
         ffn_gain,
-        pos_bias[0],
-        query_weight[0],
-        key_weight[0],
-        value_weight[0],
+        pos_bias.transpose(2, 0, 1),
+        query_weight[0].T,
+        key_weight[0].T,
+        value_weight[0].T,
         out_weight[0],
+        router.T,
         dense_gate,
         dense_up,
         dense_down,
-        router.T,
         expert_gate[0],
         expert_up[0],
         expert_down[0],
     )
-    attn, dense = attn.astype(F32), dense.astype(F32)
+    steps = 4
+
+    def rows_of(rows, width):
+        return pl.BlockSpec((rows // steps, width), lambda i: (i, 0))
+
+    def whole(*dims):
+        return pl.BlockSpec(dims, lambda i: (0,) * len(dims))
+
+    tiles = ff // 128
+    attn_shape = shape((local, width), F32)
+    results = pl.pallas_call(
+        functools.partial(widen, tiles, experts),
+        grid=(steps,),
+        out_shape=(
+            shape((rows, width), F32),
+            shape((rows, width), F32),
+            *[attn_shape] * 4,
+            shape((width, ff), F32),
+            shape((width, ff), F32),
+            shape((ff, width), F32),
+            shape((width, ff), F32),
+            shape((width, ff), F32),
+            shape((ff, width), F32),
+            shape((1, width), F32),
+            shape((1, width), F32),
+            shape((experts, width), F32),
+            shape((heads, 1, buckets), F32),
+        ),
+        in_specs=[
+            rows_of(rows, width),
+            rows_of(rows, width),
+            pl.BlockSpec((2 * tiles, 4, local // steps, 128), lambda i: (0, 0, i, 0)),
+            pl.BlockSpec((tiles, width // steps, 128), lambda i: (0, i, 0)),
+            pl.BlockSpec((tiles, width // steps, 128), lambda i: (1, i, 0)),
+            pl.BlockSpec((tiles, 2, ff // steps, 128), lambda i: (2, 0, i, 0)),
+            rows_of(width, ff),
+            rows_of(width, ff),
+            rows_of(ff, width),
+            whole(32, width),
+            whole(heads, 1, buckets),
+        ],
+        out_specs=(
+            rows_of(rows, width),
+            rows_of(rows, width),
+            *[rows_of(local, width)] * 4,
+            rows_of(width, ff),
+            rows_of(width, ff),
+            rows_of(ff, width),
+            rows_of(width, ff),
+            rows_of(width, ff),
+            rows_of(ff, width),
+            whole(1, width),
+            whole(1, width),
+            whole(experts, width),
+            whole(heads, 1, buckets),
+        ),
+        compiler_params=pltpu.CompilerParams(vmem_limit_bytes=63 * 1024 * 1024),
+    )(
+        block_output,
+        input_grad,
+        attn.reshape(2 * tiles, 4, local, 128),
+        dense,
+        dense,
+        dense.reshape(3 * tiles, 2, ff, 128),
+        ge_gate,
+        ge_up,
+        ge_down,
+        small,
+        bias_grad,
+    )
     return (
-        block_output.astype(F32).reshape(block_input.shape),
-        input_grad.astype(F32).reshape(block_input.shape),
-        small[0:1],
-        attn[None, :, 0:local],
-        attn[None, :, local : 2 * local],
-        attn[None, :, 2 * local : 3 * local],
-        attn[:, 3 * local :].T[None],
-        bias_grad[None, 1 : 1 + heads, 0:buckets].transpose(0, 2, 1),
-        small[1:2],
-        dense[0],
-        dense[1],
-        jnp.concatenate([dense[2, 0:ff], dense[2, ff:]], axis=1),
-        small[8 : 8 + experts].T,
-        ge_gate.astype(F32)[None],
-        ge_up.astype(F32)[None],
-        ge_down.astype(F32)[None],
+        results[0].reshape(block_input.shape),
+        results[1].reshape(block_input.shape),
+        results[12],
+        results[2].T[None],
+        results[3].T[None],
+        results[4].T[None],
+        results[5][None],
+        results[15].transpose(1, 2, 0),
+        results[13],
+        results[6],
+        results[7],
+        results[8],
+        results[14].T,
+        results[9][None],
+        results[10][None],
+        results[11][None],
     )
 
 

time: 234 us -> 192 us (0.82)
  Pallas kernels: 207 us -> 190 us
  local copies, waits for them, and re-layouts: 17 us -> 0 us
  other arithmetic: 7.87 us -> 0 us
    pallas_call x1, Pallas kernels: 207 us -> 183 us  [shards(): pl.pallas_call(functools.partial(kernel, c), out_shape=(shape((rows, widt...]
    unnamed x25 -> x0, local copies, waits for them, and re-layouts: 11 us -> none
    pallas_call x0 -> x1, Pallas kernels: none -> 7.15 us  [shards(): pl.pallas_call(functools.partial(widen, tiles, experts), grid=(steps,), o...]
    squeeze x3 -> x0, local copies, waits for them, and re-layouts: 3 us -> none  [the longest x1 1.55 us: shards(): dense[1]]
    unnamed x2 -> x0, other arithmetic: 2.98 us -> none
    broadcast_in_dim x2 -> x0, other arithmetic: 2.65 us -> none  [the longest x1 1.56 us: shards(): ge_up.astype(F32)[None]]
where the time goes in v3:
time: 192 us; the launch traced here: 191 us
  Pallas kernels  190 us (99%)
    pallas_call x1, Pallas kernels, shards(): pl.pallas_call(functools.partial(kernel, c), out_shape=(shape((rows, widt...  183 us
    pallas_call x1, Pallas kernels, shards(): pl.pallas_call(functools.partial(widen, tiles, experts), grid=(steps,), o...  7.15 us

profile of v3, /device:TPU:0, one launch (start us, length us, event | category | flops | bytes accessed | tf_op | source)
XLA Modules:
  0.0 191.3 jit_solution(16308550187862828438)
XLA Ops:
  0.7 183.3 %shard_map.297 = (bf16[256,768]{1,0:T(8,128)(2,1)}, bf16[256,768]{1,0:T(8,128)(2,1)}, bf16[6,768,128]{2,1,0:T(8,128)(2,1)}, bf16[9,768,128]{2,1,0:T(8,128)(2,1)}...) custom-call(bf16[256,768]{1,0:T(8,128)(2,1)} %bitcast.51, ...), custom_call_target="tpu_custom_call" | custom-call | tf_op jit(solution)/shard_map/pallas_call | solution.py:1030
  184.0 7.2 %shard_map.298 = (f32[256,768]{1,0:T(8,128)}, f32[256,768]{1,0:T(8,128)}, f32[192,768]{1,0:T(8,128)}, f32[192,768]{1,0:T(8,128)}, f32[192,768]{1,0:T(8,128)}, /*...) custom-call(bf16[256,768]{1,0:T(8,128)(2,1)} %get-tuple-element.41.o, ...), custom_call_target="tpu_custom_call" | custom-call | tf_op jit(solution)/shard_map/pallas_call | solution.py:1079

commit v4 on v3

--- a/solution.py
+++ b/solution.py
@@ -19,7 +19,8 @@
 GRAD1, BACK1, GRAD0, BACK0, INPUT, SMALL_A, SMALL_A2, SMALL_B, SMALL_B2 = range(11, 20)
 DISPATCH, FORWARD, CORE, RETURN = 20, 24, 28, 32
 DENSE_SUM, ATTN_SUM = 33, 41
-SEMAPHORES = 49
+EARLY, EARLY_FORWARD, CORE2, RETURN2, MOE2 = range(49, 54)
+SEMAPHORES = 54
 
 
 def bucket_limits(count):
@@ -150,18 +151,27 @@
     du1,
     pick0,
     pick1,
-    gate_slot,
+    ex,
+    ey,
     sx,
     rx,
     hid,
     da,
     du,
+    dout,
+    gates,
     cs,
     cr,
     rt,
     rb,
+    cs2,
+    cr2,
+    rt2,
+    rb2,
     moe_send,
     moe_recv,
+    out_send,
+    out_recv,
     small,
     small_send,
     small_recv,
@@ -195,6 +205,7 @@
     ge_up_ref,
     ge_down_ref,
     stage_sem,
+    wide_router,
 ):
     sections, experts, mps = c["section"], c["expert"], c["mp"]
     micro, length, heads, size, cap = c["micro"], c["length"], c["heads"], c["size"], c["cap"]
@@ -287,6 +298,8 @@
     for limit in bucket_limits(c["buckets"]):
         found = found + jnp.where(row_at - col_at >= limit, 1, 0)
     bucket[...] = found
+    wide_router[...] = jnp.zeros_like(wide_router)
+    wide_router[0:experts] = router_ref[...]
     for h in range(heads):
         total = jnp.zeros((length, length), F32)
         for b in range(c["buckets"]):
@@ -497,6 +510,53 @@
         attention(n1, sends.at[0])
         scatter_from(sends.at[0], recv4.at[0], TERM1)
 
+    phase("early")
+    named = []
+    before = low(jnp.where(row_at < col_at, 1.0, 0.0))
+    expert_at = lax.broadcasted_iota(jnp.int32, (length, length), 0)
+    slot_at = full(lax.broadcasted_iota(jnp.int32, (cap, length), 0))
+    for m in range(micro):
+        r = slice(m * length, (m + 1) * length)
+        wide = [
+            jnp.where(expert_at == routes_ref[2 * m + ch : 2 * m + ch + 1, :], 1.0, 0.0)
+            for ch in range(2)
+        ]
+        hots = [hot[0:experts] for hot in wide]
+        rank = nn(low(hots[0] + hots[1]), before)
+        for e in range(experts):
+            fit = slot_at == rank[e : e + 1]
+            at = slice(e * cap, (e + 1) * cap)
+            pick0[m, at] = low(jnp.where(fit, hots[0][e : e + 1], 0.0))
+            pick1[m, at] = low(jnp.where(fit, hots[1][e : e + 1], 0.0))
+        named.append(hots)
+        place_rows = slice(m * cap, (m + 1) * cap)
+        out_rows = low(nn(pick0[m] + pick1[m], gy_ref[r, mine]))
+        ex[:, place_rows, 0:half] = out_rows.reshape(experts, cap, half)
+        other = low(nt(pick0[m], low(wide[1])) + nt(pick1[m], low(wide[0])))
+        ex[:, place_rows, half:] = other.reshape(experts, cap, 128)
+    if side_size == 4:
+        offsets = [(0, 1), (0, 3), (1, 0), (3, 0), (1, 1), (3, 3), (1, 3), (3, 1)]
+        offsets += [(2, 1), (2, 3), (1, 2), (3, 2), (0, 0), (0, 2), (2, 0), (2, 2)]
+    else:
+        offsets = [(a, b) for a in range(side_size) for b in range(side_size)]
+
+    def to_slot(src, dst, k, which):
+        if offsets[k] == (0, 0):
+            pltpu.make_async_copy(src.at[me], dst.at[s, pl.ds(k * slots, slots)], recv_sem.at[which]).start()
+        else:
+            p = at_offset(*offsets[k])
+            send(src.at[p], dst.at[s, pl.ds(k * slots, slots)], which, {"expert": p})
+
+    def to_token(src, dst, k, which):
+        src = src.at[pl.ds(k * slots, slots)]
+        if offsets[k] == (0, 0):
+            pltpu.make_async_copy(src, dst.at[me], recv_sem.at[which]).start()
+        else:
+            dz, dy = offsets[k]
+            send(src, dst.at[me], which, {"expert": at_offset(side_size - dz, side_size - dy)})
+
+    for k in range(experts):
+        to_slot(ex, ey, k, EARLY)
     phase("term1_wait")
     arrived(GAINS, gains.at[1 - s])
     wait_from(0, recv4.at[0], TERM1)
@@ -530,23 +590,9 @@
         attention(rows2, sends.at[2])
         scatter_from(sends.at[2], recv4.at[1], TERM2)
 
-    phase("routing")
-    named = []
-    before = low(jnp.where(row_at < col_at, 1.0, 0.0))
-    expert_at = lax.broadcasted_iota(jnp.int32, (experts, length), 0)
-    slot_at = full(lax.broadcasted_iota(jnp.int32, (cap, length), 0))
-    for m in range(micro):
-        hots = [
-            jnp.where(expert_at == routes_ref[2 * m + ch : 2 * m + ch + 1, :], 1.0, 0.0)
-            for ch in range(2)
-        ]
-        rank = nn(low(hots[0] + hots[1]), before)
-        for e in range(experts):
-            fit = slot_at == rank[e : e + 1]
-            at = slice(e * cap, (e + 1) * cap)
-            pick0[m, at] = low(jnp.where(fit, hots[0][e : e + 1], 0.0))
-            pick1[m, at] = low(jnp.where(fit, hots[1][e : e + 1], 0.0))
-        named.append(hots)
+    phase("early_forward")
+    arrived(EARLY, ey.at[s])
+    send(ey.at[s], ey.at[s], EARLY_FORWARD, {"section": 1 - s})
 
     phase("term2_wait")
     wait_from(1, recv4.at[1], TERM2)
@@ -558,40 +604,14 @@
     phase("rows3_wait")
     wait_all(rows3, ROWS3)
     phase("slots")
-    logits = nt(router_ref[...], rows3[...])
     for m in range(micro):
-        hots = named[m]
         r = slice(m * length, (m + 1) * length)
-        here = logits[:, r]
-        l0 = jnp.sum(hots[0] * here, axis=0, keepdims=True)
-        l1 = jnp.sum(hots[1] * here, axis=0, keepdims=True)
-        top = jnp.maximum(l0, l1)
-        e0, e1 = jnp.exp(l0 - top), jnp.exp(l1 - top)
-        by_expert = (hots[0] * e0 + hots[1] * e1) / (e0 + e1)
-        both = pick0[m] + pick1[m]
-        for e in range(experts):
-            at = slice(e * cap, (e + 1) * cap)
-            gate = jnp.sum(full(both[at]) * by_expert[e : e + 1], axis=1, keepdims=True)
-            gate_slot[m, at] = jnp.broadcast_to(gate, (cap, 128))
-        place_rows = slice(m * cap, (m + 1) * cap)
-        out_rows = low(nn(both, rows3[r, mine]))
-        sx[:, place_rows, 0:half] = out_rows.reshape(experts, cap, half)
-        out_rows = low(nn(both, gy_ref[r, mine]) * gate_slot[m][:, 0:1])
-        sx[:, place_rows, half:] = out_rows.reshape(experts, cap, half)
-    if side_size == 4:
-        offsets = [(0, 1), (0, 3), (1, 0), (3, 0), (1, 1), (3, 3), (1, 3), (3, 1)]
-        offsets += [(2, 1), (2, 3), (1, 2), (3, 2), (0, 0), (0, 2), (2, 0), (2, 2)]
-    else:
-        offsets = [(a, b) for a in range(side_size) for b in range(side_size)]
+        out_rows = low(nn(pick0[m] + pick1[m], rows3[r, mine]))
+        sx[:, m * cap : (m + 1) * cap, :] = out_rows.reshape(experts, cap, half)
 
     def dispatch(j):
         for k in range(j * per, (j + 1) * per):
-            to = rx.at[s, pl.ds(k * slots, slots)]
-            if offsets[k] == (0, 0):
-                pltpu.make_async_copy(sx.at[me], to, recv_sem.at[DISPATCH + j]).start()
-            else:
-                p = at_offset(*offsets[k])
-                send(sx.at[p], to, DISPATCH + j, {"expert": p})
+            to_slot(sx, rx, k, DISPATCH + j)
 
     def dispatched(j):
         count = sum(offsets[k] != (0, 0) for k in range(j * per, (j + 1) * per))
@@ -606,14 +626,9 @@
     def give_back(j):
         at = pl.ds(j * block, block)
         arrived(CORE + j, cr.at[at])
-        rt[at] = low(full(cs[s, at]) + full(cr[at]))
+        rt[at, 0:half] = low(full(cs[s, at]) + full(cr[at]))
         for k in range(j * per, (j + 1) * per):
-            src = rt.at[pl.ds(k * slots, slots)]
-            if offsets[k] == (0, 0):
-                pltpu.make_async_copy(src, rb.at[me], recv_sem.at[RETURN]).start()
-            else:
-                dz, dy = offsets[k]
-                send(src, rb.at[me], RETURN, {"expert": at_offset(side_size - dz, side_size - dy)})
+            to_token(rt, rb, k, RETURN)
 
     phase("dispatch_wait")
     dispatch(0)
@@ -623,24 +638,37 @@
     dispatch(2)
     for copy in staged[3:6]:
         copy.wait()
+    arrived(EARLY_FORWARD, ey.at[1 - s])
+    named_here = lax.broadcasted_iota(jnp.int32, (block, 128), 1)
     for j in range(blocks):
         at = pl.ds(j * block, block)
         phase("forward_wait%d" % j)
         arrived(FORWARD + j, rx.at[1 - s, at])
         phase("expert%d" % j)
         x0, x1 = rx[0, at, 0:half], rx[1, at, 0:half]
-        g0, g1 = rx[0, at, half:], rx[1, at, half:]
+        logits = nt(x0, wide_router[:, 0:half]) + nt(x1, wide_router[:, half:])
+        this = jnp.sum(jnp.where(named_here == me, logits, 0.0), axis=-1, keepdims=True)
+        other = jnp.sum(full(ey[0, at, half:]) * logits, axis=-1, keepdims=True)
+        top = jnp.maximum(this, other)
+        e0, e1 = jnp.exp(this - top), jnp.exp(other - top)
+        gate = e0 / (e0 + e1)
+        gates[at] = jnp.broadcast_to(gate, (block, 128))
+        g0, g1 = low(gate * full(ey[0, at, 0:half])), low(gate * full(ey[1, at, 0:half]))
+        dout[at, 0:half] = g0
+        dout[at, half:] = g1
         a = nn(x0, gate_ref[0:half]) + nn(x1, gate_ref[half:])
         u = nn(x0, up_ref[0:half]) + nn(x1, up_ref[half:])
         d = nt(g0, down_ref[:, 0:half]) + nt(g1, down_ref[:, half:])
         value, slope = gelu_parts(a)
-        hid[at] = low(value * u)
+        held = low(value * u)
+        hid[at] = held
+        term = jnp.sum(d * full(held), axis=-1, keepdims=True)
+        rt[at, half:] = low(jnp.where(named_here == 0, term, 0.0))
         da[at] = low(d * u * slope)
         du[at] = low(d * value)
         for side in range(sections):
             w = slice(side * half, (side + 1) * half)
-            cs[side, at, 0:half] = low(nn(hid[at], down_ref[:, w]))
-            cs[side, at, half:] = low(nt(da[at], gate_ref[w]) + nt(du[at], up_ref[w]))
+            cs[side, at] = low(nt(da[at], gate_ref[w]) + nt(du[at], up_ref[w]))
         send(cs.at[1 - s, at], cr.at[at], CORE + j, {"section": 1 - s})
         phase("give_back%d" % j)
         if j + 1 < blocks:
@@ -651,38 +679,44 @@
         if j > 0:
             give_back(j - 1)
     give_back(blocks - 1)
+    phase("outputs")
+    for j in range(blocks):
+        at = pl.ds(j * block, block)
+        for side in range(sections):
+            w = slice(side * half, (side + 1) * half)
+            cs2[side, at] = low(nn(hid[at], down_ref[:, w]) * gates[at][:, 0:1])
+        send(cs2.at[1 - s, at], cr2.at[at], CORE2, {"section": 1 - s})
     phase("expert_weights")
     for side in range(sections):
         w = slice(side * half, (side + 1) * half)
-        ge_gate_ref[w] = low(tn(rx[side, :, 0:half], da[...]))
-        ge_up_ref[w] = low(tn(rx[side, :, 0:half], du[...]))
-        ge_down_ref[:, w] = low(tn(hid[...], rx[side, :, half:]))
+        ge_gate_ref[w] = low(tn(rx[side], da[...]))
+        ge_up_ref[w] = low(tn(rx[side], du[...]))
+        ge_down_ref[:, w] = low(tn(hid[...], dout[:, w]))
     for copy in staged[6:]:
         copy.start()
+    arrived(CORE2, cr2)
+    for j in range(blocks):
+        at = pl.ds(j * block, block)
+        rt2[at] = low(full(cs2[s, at]) + full(cr2[at]))
+        for k in range(j * per, (j + 1) * per):
+            to_token(rt2, rb2, k, RETURN2)
     phase("return_wait")
     arrived(RETURN, rb)
     phase("combine")
     lane = lax.broadcasted_iota(jnp.int32, (length, 128), 1)
     for m in range(micro):
         r = slice(m * length, (m + 1) * length)
-        held = rb[:, m * cap : (m + 1) * cap, :].reshape(experts * cap, width)
-        scaled = low(full(held[:, 0:half]) * gate_slot[m][:, 0:1])
-        first, second = tn(pick0[m], scaled), tn(pick1[m], scaled)
-        gy = full(gy_ref[r, mine])
-        t0 = jnp.sum(gy * first, axis=-1, keepdims=True)
-        t1 = jnp.sum(gy * second, axis=-1, keepdims=True)
-        moe_send[r, 0:half] = low(first + second)
-        moe_send[r, half : 2 * half] = low(tn(pick0[m] + pick1[m], held[:, half:]))
-        moe_send[r, 2 * half :] = low(jnp.where(lane == 0, t0, jnp.where(lane == 1, t1, 0.0)))
+        held = rb[:, m * cap : (m + 1) * cap, :].reshape(experts * cap, half + 128)
+        moe_send[r, 0:half] = low(tn(pick0[m] + pick1[m], held[:, 0:half]))
+        t0, t1 = tn(pick0[m], held[:, half:]), tn(pick1[m], held[:, half:])
+        moe_send[r, half:] = low(jnp.where(lane == 0, t0, jnp.where(lane == 1, t1[:, 0:1], 0.0)))
     scatter(moe_send, moe_recv, MOE)
     phase("moe_wait")
     arrived(MOE, moe_recv.at[pl.ds(0, group - 1)])
     phase("norm3_back")
     lower, upper = total(moe_recv, 0, mps), total(moe_recv, mps, group)
     h2 = chunk[H2]
-    out_ref[own, 0:half] = low(h2[:, 0:half] + lower[:, 0:half])
-    out_ref[own, half:] = low(h2[:, half:] + upper[:, 0:half])
-    terms = lower[:, 2 * half :] + upper[:, 2 * half :]
+    terms = lower[:, half:] + upper[:, half:]
     t0, t1 = terms[:, 0:1], terms[:, 1:2]
     ahead = lax.rem(place * part, length)
     token = lax.broadcasted_iota(jnp.int32, (part, length), 1)
@@ -696,7 +730,7 @@
     top = jnp.maximum(l0, l1)
     e0, e1 = jnp.exp(l0 - top), jnp.exp(l1 - top)
     dlogits = hot0 * (t0 - e0 / (e0 + e1) * (t0 + t1)) + hot1 * (t1 - e1 / (e0 + e1) * (t0 + t1))
-    dr = jnp.concatenate([lower[:, half : 2 * half], upper[:, half : 2 * half]], axis=1)
+    dr = jnp.concatenate([lower[:, 0:half], upper[:, 0:half]], axis=1)
     dr = dr + nn(dlogits, full(router_ref[...]), HIGHEST)
     back, gain = normed_back(h2, gains[1, 1:2], dr)
     grad = full(gy_ref[own]) + back
@@ -707,7 +741,6 @@
     small[0:1] = gain
     small[8 : 8 + experts] = tn(dlogits, full(rows3[own]), HIGHEST)
     smallb_send[...] = jnp.zeros_like(smallb_send)
-    gather_all(out_ref, OUT)
 
     phase("attention2_back")
     @pl.when(s == 1)
@@ -717,6 +750,12 @@
         scatter_from(sends.at[3], recv4.at[2], BACK2)
         attention_weights(rows2, grad2)
 
+    phase("output")
+    arrived(RETURN2, rb2)
+    for m in range(micro):
+        held = rb2[:, m * cap : (m + 1) * cap, :].reshape(experts * cap, half)
+        out_send[m * length : (m + 1) * length] = low(tn(pick0[m] + pick1[m], held))
+    scatter(out_send, out_recv, MOE2)
     phase("back2_wait")
     wait_from(1, recv4.at[2], BACK2)
     phase("norm2_back")
@@ -761,6 +800,14 @@
         send(small_send, small_recv.at[place], SMALL_A, in_group(lax.rem(place + k, group)))
     small_recv[place] = small_send[...]
 
+    phase("out")
+    arrived(MOE2, out_recv.at[pl.ds(0, group - 1)])
+    out_ref[own, 0:half] = low(chunk[H2][:, 0:half] + total(out_recv, 0, mps))
+    out_ref[own, half:] = low(chunk[H2][:, half:] + total(out_recv, mps, group))
+    gather_all(out_ref, OUT)
+    phase("dense_two")
+    dense_sum[1]()
+
     phase("attention1_back")
     @pl.when(s == 0)
     def _():
@@ -775,16 +822,15 @@
         for stage in attn_sum[1:]:
             stage()
 
-    phase("dense_two")
-    dense_sum[1]()
-
+    phase("dense_three")
+    dense_sum[2]()
     phase("attn_one")
     @pl.when(s == 0)
     def _():
         attention_weights(n1, grad0)
 
-    phase("dense_three")
-    dense_sum[2]()
+    phase("dense_four")
+    dense_sum[3]()
     for k in range(1, experts):
         send(smallb_send, smallb_recv.at[me], SMALL_B, on_expert(k))
     smallb_recv[me] = smallb_send[...]
@@ -799,8 +845,6 @@
     def _():
         attn_sum[1]()
 
-    phase("dense_four")
-    dense_sum[3]()
     phase("small_a")
     arrived(SMALL_A, small_recv.at[pl.ds(0, group - 1)])
     small2_send[...] = low(total(small_recv))
@@ -852,6 +896,11 @@
     for phase, at in ((DENSE, 1), (BACK1, 4)):
         left(phase, sends.at[at, seven])
     left(MOE, moe_send.at[seven])
+    left(MOE2, out_send.at[seven])
+    left(EARLY, ey.at[0, pl.ds(0, (experts - 1) * slots)])
+    left(EARLY_FORWARD, ey.at[0])
+    left(CORE2, cr2)
+    left(RETURN2, rb2.at[pl.ds(0, experts - 1)])
     left_to(1, rows2, ROWS2)
     left_to(1, grad2, GRAD2)
     left_to(0, grad0, GRAD0)
@@ -980,18 +1029,27 @@
         held(rows, ff),
         held(micro, experts * cap, length),
         held(micro, experts * cap, length),
-        exact(micro, experts * cap, 128),
-        held(experts, slots, 2 * half),
-        held(sections, every, 2 * half),
+        held(experts, slots, half + 128),
+        held(sections, every, half + 128),
+        held(experts, slots, half),
+        held(sections, every, half),
         held(every, ff),
         held(every, ff),
         held(every, ff),
-        held(sections, every, 2 * half),
-        held(every, 2 * half),
-        held(every, 2 * half),
-        held(experts, slots, 2 * half),
-        held(rows, 2 * half + 128),
-        held(group, part, 2 * half + 128),
+        held(every, width),
+        exact(every, 128),
+        held(sections, every, half),
+        held(every, half),
+        held(every, half + 128),
+        held(experts, slots, half + 128),
+        held(sections, every, half),
+        held(every, half),
+        held(every, half),
+        held(experts, slots, half),
+        held(rows, half + 128),
+        held(group, part, half + 128),
+        held(rows, half),
+        held(group, part, half),
         exact(32, width),
         held(32, width),
         held(group, 32, width),
@@ -1025,6 +1083,7 @@
         held(width, ff),
         held(ff, width),
         pltpu.SemaphoreType.DMA((9,)),
+        held(128, width),
     ]
     shape = jax.ShapeDtypeStruct
     block_output, input_grad, attn, dense, ge_gate, ge_up, ge_down, small, bias_grad = pl.pallas_call(

time: 192 us -> 173 us (0.901)
  Pallas kernels: 190 us -> 171 us
    pallas_call x1, Pallas kernels: 183 us -> 164 us  [shards(): pl.pallas_call(functools.partial(kernel, c), out_shape=(shape((rows, widt...]
where the time goes in v4:
time: 173 us; the launch traced here: 172 us
  Pallas kernels  171 us (99%)
    pallas_call x1, Pallas kernels, shards(): pl.pallas_call(functools.partial(kernel, c), out_shape=(shape((rows, widt...  164 us
    pallas_call x1, Pallas kernels, shards(): pl.pallas_call(functools.partial(widen, tiles, experts), grid=(steps,), o...  7.15 us

profile of v4, /device:TPU:0, one launch (start us, length us, event | category | flops | bytes accessed | tf_op | source)
XLA Modules:
  0.0 171.7 jit_solution(10678626195748821374)
XLA Ops:
  0.7 163.7 %shard_map.297 = (bf16[256,768]{1,0:T(8,128)(2,1)}, bf16[256,768]{1,0:T(8,128)(2,1)}, bf16[6,768,128]{2,1,0:T(8,128)(2,1)}, bf16[9,768,128]{2,1,0:T(8,128)(2,1)}...) custom-call(bf16[256,768]{1,0:T(8,128)(2,1)} %bitcast.51, ...), custom_call_target="tpu_custom_call" | custom-call | tf_op jit(solution)/shard_map/pallas_call | solution.py:1089
  164.4 7.2 %shard_map.298 = (f32[256,768]{1,0:T(8,128)}, f32[256,768]{1,0:T(8,128)}, f32[192,768]{1,0:T(8,128)}, f32[192,768]{1,0:T(8,128)}, f32[192,768]{1,0:T(8,128)}, /*...) custom-call(bf16[256,768]{1,0:T(8,128)(2,1)} %get-tuple-element.41.o, ...), custom_call_target="tpu_custom_call" | custom-call | tf_op jit(solution)/shard_map/pallas_call | solution.py:1138

commit v5 on v4

--- a/solution.py
+++ b/solution.py
@@ -20,7 +20,8 @@
 DISPATCH, FORWARD, CORE, RETURN = 20, 24, 28, 32
 DENSE_SUM, ATTN_SUM = 33, 41
 EARLY, EARLY_FORWARD, CORE2, RETURN2, MOE2 = range(49, 54)
-SEMAPHORES = 54
+SMALL_A3, SMALL_B3 = 54, 55
+SEMAPHORES = 56
 
 
 def bucket_limits(count):
@@ -93,28 +94,28 @@
 
 def kernel(
     c,
-    x_ref,
-    gy_ref,
+    x_hbm,
+    gy_hbm,
     docs_ref,
     routes_ref,
     attn_gain_ref,
     ffn_gain_ref,
     table_ref,
-    wq_ref,
-    wk_ref,
-    wv_ref,
-    wo_ref,
-    router_ref,
+    wq_hbm,
+    wk_hbm,
+    wv_hbm,
+    wo_hbm,
+    router_hbm,
     dense_gate_hbm,
     dense_up_hbm,
     dense_down_hbm,
     gate_hbm,
     up_hbm,
     down_hbm,
-    out_ref,
-    input_ref,
-    attn_ref,
-    dense_ref,
+    out_hbm,
+    input_hbm,
+    attn_hbm,
+    dense_hbm,
     ge_gate_hbm,
     ge_up_hbm,
     ge_down_hbm,
@@ -177,8 +178,12 @@
     small_recv,
     small2_send,
     small2_recv,
+    small3_send,
+    small3_recv,
     smallb_send,
     smallb_recv,
+    smallb3_send,
+    smallb3_recv,
     smallb2_send,
     smallb2_recv,
     dense_own,
@@ -206,6 +211,18 @@
     ge_down_ref,
     stage_sem,
     wide_router,
+    x_ref,
+    gy_ref,
+    wq_ref,
+    wk_ref,
+    wv_ref,
+    wo_ref,
+    router_ref,
+    out_ref,
+    input_ref,
+    attn_ref,
+    dense_ref,
+    d0,
 ):
     sections, experts, mps = c["section"], c["expert"], c["mp"]
     micro, length, heads, size, cap = c["micro"], c["length"], c["heads"], c["size"], c["cap"]
@@ -235,10 +252,21 @@
                 (ge_gate_ref, ge_gate_hbm),
                 (ge_up_ref, ge_up_hbm),
                 (ge_down_ref, ge_down_hbm),
+                (x_hbm, x_ref),
+                (wq_hbm, wq_ref),
+                (wk_hbm, wk_ref),
+                (wv_hbm, wv_ref),
+                (wo_hbm, wo_ref),
+                (router_hbm, router_ref),
+                (gy_hbm, gy_ref),
+                (out_ref, out_hbm),
+                (input_ref, input_hbm),
+                (dense_ref, dense_hbm),
+                (attn_ref, attn_hbm),
             )
         )
     ]
-    for copy in staged[0:6]:
+    for copy in staged[9:16] + staged[0:6]:
         copy.start()
     blocks = 4
     per = experts // blocks
@@ -299,7 +327,6 @@
         found = found + jnp.where(row_at - col_at >= limit, 1, 0)
     bucket[...] = found
     wide_router[...] = jnp.zeros_like(wide_router)
-    wide_router[0:experts] = router_ref[...]
     for h in range(heads):
         total = jnp.zeros((length, length), F32)
         for b in range(c["buckets"]):
@@ -390,7 +417,7 @@
             o[r, lanes] = low(nn(lows[i], qkv[2, r, lanes]))
         out[...] = low(nn(o[...], wo_ref[...]))
 
-    def attention_back(g_ref, out):
+    def attention_back(g_ref, out, between=None):
         do[...] = low(nt(g_ref[...], wo_ref[...]))
         dps = [nt(do[r, lanes], qkv[2, r, lanes]) for m, h, r, lanes in pairs]
         for m, h, r, lanes in pairs:
@@ -404,6 +431,8 @@
             low(probs[m * heads + h] * (dp - total_row))
             for dp, total_row, (m, h, r, lanes) in zip(dps, sums, pairs)
         ]
+        if between is not None:
+            between()
         for ds, (m, h, r, lanes) in zip(grads, pairs):
             dqkv[r, h * size : (h + 1) * size] = low(nn(ds, qkv[1, r, lanes]) * scale)
         for ds, (m, h, r, lanes) in zip(grads, pairs):
@@ -423,6 +452,8 @@
             attn_own[t, 0 : 3 * local] = grads[:, lanes]
             attn_own[t, 3 * local :] = last[:, lanes]
         attn_sum[0]()
+
+    def bias_sums():
         found = bucket[...]
         for h in range(heads):
             held = dsum[h]
@@ -503,6 +534,9 @@
         attn_own, attn_ref, ATTN_SUM, 3, (attn_a1, attn_b1), (attn_am, attn_bm), (attn_a2, attn_b2)
     )
 
+    for copy in staged[9:16]:
+        copy.wait()
+    wide_router[0:experts] = router_ref[...]
     x = full(x_ref[...])
     @pl.when(s == 0)
     def _():
@@ -583,6 +617,9 @@
     rows2[own] = normed(y1, gains[1, 0:1])
     gather_to(1, rows2, ROWS2)
 
+    phase("early_forward")
+    arrived(EARLY, ey.at[s])
+    send(ey.at[s], ey.at[s], EARLY_FORWARD, {"section": 1 - s})
     phase("attention2")
     @pl.when(s == 1)
     def _():
@@ -590,9 +627,12 @@
         attention(rows2, sends.at[2])
         scatter_from(sends.at[2], recv4.at[1], TERM2)
 
-    phase("early_forward")
-    arrived(EARLY, ey.at[s])
-    send(ey.at[s], ey.at[s], EARLY_FORWARD, {"section": 1 - s})
+    phase("early_hidden")
+    staged[5].wait()
+    arrived(EARLY_FORWARD, ey.at[1 - s])
+    for j in range(blocks):
+        at = pl.ds(j * block, block)
+        d0[at] = nt(ey[0, at, 0:half], down_ref[:, 0:half]) + nt(ey[1, at, 0:half], down_ref[:, half:])
 
     phase("term2_wait")
     wait_from(1, recv4.at[1], TERM2)
@@ -600,9 +640,12 @@
     h2 = chunk[Y1] + total(recv4.at[1])
     chunk[H2] = h2
     rows3[own] = normed(h2, gains[1, 1:2])
-    gather_all(rows3, ROWS3)
+    for k in range(1, group):
+        p = in_group(lax.rem(place + k, group))
+        src = rows3.at[own, pl.ds(pl.multiple_of(p["section"] * half, 128), half)]
+        send(src, src, ROWS3, p)
     phase("rows3_wait")
-    wait_all(rows3, ROWS3)
+    arrived(ROWS3, rows3.at[pl.ds(0, (group - 1) * part), pl.ds(0, half)])
     phase("slots")
     for m in range(micro):
         r = slice(m * length, (m + 1) * length)
@@ -636,9 +679,8 @@
     forward(0)
     dispatched(0)
     dispatch(2)
-    for copy in staged[3:6]:
+    for copy in staged[3:5]:
         copy.wait()
-    arrived(EARLY_FORWARD, ey.at[1 - s])
     named_here = lax.broadcasted_iota(jnp.int32, (block, 128), 1)
     for j in range(blocks):
         at = pl.ds(j * block, block)
@@ -653,12 +695,9 @@
         e0, e1 = jnp.exp(this - top), jnp.exp(other - top)
         gate = e0 / (e0 + e1)
         gates[at] = jnp.broadcast_to(gate, (block, 128))
-        g0, g1 = low(gate * full(ey[0, at, 0:half])), low(gate * full(ey[1, at, 0:half]))
-        dout[at, 0:half] = g0
-        dout[at, half:] = g1
         a = nn(x0, gate_ref[0:half]) + nn(x1, gate_ref[half:])
         u = nn(x0, up_ref[0:half]) + nn(x1, up_ref[half:])
-        d = nt(g0, down_ref[:, 0:half]) + nt(g1, down_ref[:, half:])
+        d = gate * d0[at]
         value, slope = gelu_parts(a)
         held = low(value * u)
         hid[at] = held
@@ -687,12 +726,17 @@
             cs2[side, at] = low(nn(hid[at], down_ref[:, w]) * gates[at][:, 0:1])
         send(cs2.at[1 - s, at], cr2.at[at], CORE2, {"section": 1 - s})
     phase("expert_weights")
+    for j in range(blocks):
+        at = pl.ds(j * block, block)
+        for side in range(sections):
+            w = slice(side * half, (side + 1) * half)
+            dout[at, w] = low(gates[at][:, 0:1] * full(ey[side, at, 0:half]))
     for side in range(sections):
         w = slice(side * half, (side + 1) * half)
         ge_gate_ref[w] = low(tn(rx[side], da[...]))
         ge_up_ref[w] = low(tn(rx[side], du[...]))
         ge_down_ref[:, w] = low(tn(hid[...], dout[:, w]))
-    for copy in staged[6:]:
+    for copy in staged[6:9]:
         copy.start()
     arrived(CORE2, cr2)
     for j in range(blocks):
@@ -749,6 +793,7 @@
         attention_back(grad2, sends.at[3])
         scatter_from(sends.at[3], recv4.at[2], BACK2)
         attention_weights(rows2, grad2)
+        bias_sums()
 
     phase("output")
     arrived(RETURN2, rb2)
@@ -805,35 +850,43 @@
     out_ref[own, 0:half] = low(chunk[H2][:, 0:half] + total(out_recv, 0, mps))
     out_ref[own, half:] = low(chunk[H2][:, half:] + total(out_recv, mps, group))
     gather_all(out_ref, OUT)
-    phase("dense_two")
-    dense_sum[1]()
-
     phase("attention1_back")
     @pl.when(s == 0)
     def _():
         wait_all(grad0, GRAD0)
-        dn = attention_back(grad0, sends.at[5])
+        dn = attention_back(grad0, sends.at[5], dense_sum[1])
         scatter_from(sends.at[5], recv4.at[3], BACK0)
+        dense_sum[2]()
+        attention_weights(n1, grad0)
         x = full(x_ref[...])
         smallb_send[0:1] = jnp.sum(dn * x * inverse_rms(x), axis=0, keepdims=True)
 
     @pl.when(s == 1)
     def _():
-        for stage in attn_sum[1:]:
+        for stage in attn_sum[1:3]:
             stage()
-
-    phase("dense_three")
-    dense_sum[2]()
-    phase("attn_one")
+        dense_sum[1]()
+        attn_sum[3]()
+        dense_sum[2]()
+
+    def along(src, dst, which, fast_side):
+        for k in range(1, side_size):
+            p = at_offset(0, k) if fast_side else at_offset(k, 0)
+            send(src, dst.at[fast if fast_side else slow], which, {"expert": p})
+        dst[fast if fast_side else slow] = src[...]
+
+    phase("small_a")
+    arrived(SMALL_A, small_recv.at[pl.ds(0, group - 1)])
+    small2_send[...] = low(total(small_recv))
+    along(small2_send, small2_recv, SMALL_A2, True)
+    phase("dense_four")
+    dense_sum[3]()
+    phase("bias")
     @pl.when(s == 0)
     def _():
-        attention_weights(n1, grad0)
-
-    phase("dense_four")
-    dense_sum[3]()
-    for k in range(1, experts):
-        send(smallb_send, smallb_recv.at[me], SMALL_B, on_expert(k))
-    smallb_recv[me] = smallb_send[...]
+        bias_sums()
+
+    along(smallb_send, smallb_recv, SMALL_B, True)
     phase("back0_wait")
     wait_from(0, recv4.at[3], BACK0)
     phase("norm0_back")
@@ -845,20 +898,21 @@
     def _():
         attn_sum[1]()
 
-    phase("small_a")
-    arrived(SMALL_A, small_recv.at[pl.ds(0, group - 1)])
-    small2_send[...] = low(total(small_recv))
-    for k in range(1, experts):
-        send(small2_send, small2_recv.at[me], SMALL_A2, on_expert(k))
-    small2_recv[me] = small2_send[...]
+    phase("small_two")
+    arrived(SMALL_A2, small2_recv.at[pl.ds(0, side_size - 1)])
+    small3_send[...] = low(total(small2_recv))
+    along(small3_send, small3_recv, SMALL_A3, False)
+    arrived(SMALL_B, smallb_recv.at[pl.ds(0, side_size - 1)])
+    smallb3_send[...] = total(smallb_recv)
+    along(smallb3_send, smallb3_recv, SMALL_B3, False)
     phase("attn_three")
     @pl.when(s == 0)
     def _():
         attn_sum[2]()
 
-    phase("small_b")
-    arrived(SMALL_B, smallb_recv.at[pl.ds(0, experts - 1)])
-    smallb2_send[...] = total(smallb_recv)
+    phase("small_three")
+    arrived(SMALL_B3, smallb3_recv.at[pl.ds(0, side_size - 1)])
+    smallb2_send[...] = total(smallb3_recv)
     for k in range(1, mps):
         send(smallb2_send, smallb2_recv.at[mp], SMALL_B2, {"mp": lax.rem(mp + k, mps)})
     smallb2_recv[mp] = smallb2_send[...]
@@ -867,8 +921,8 @@
     def _():
         attn_sum[3]()
 
-    arrived(SMALL_A2, small2_recv.at[pl.ds(0, experts - 1)])
-    summed = total(small2_recv)
+    arrived(SMALL_A3, small3_recv.at[pl.ds(0, side_size - 1)])
+    summed = total(small3_recv)
     for h in range(heads):
         bias_grad_ref[h] = smallb2_send[1 + h : 2 + h, 0 : c["buckets"]]
     arrived(SMALL_B2, smallb2_recv.at[pl.ds(0, mps - 1)])
@@ -878,20 +932,19 @@
     small_ref[1:2] = jnp.where(s == 0, summed[2:3], summed[0:1])
     phase("last_waits")
     wait_all(out_ref, OUT)
+    staged[16].start()
     wait_all(input_ref, INPUT)
+    staged[17].start()
     dense_sum[4]()
-
-    @pl.when(s == 0)
-    def _():
-        attn_sum[4]()
-        attn_sum[5]()
-
-    for copy in staged[6:]:
-        copy.wait()
+    staged[18].start()
+    attn_sum[4]()
+    staged[19].start()
+    attn_sum[5]()
     dense_sum[5]()
     left(GAINS, gains.at[s])
     seven = pl.ds(0, (group - 1) * part)
-    for phase, ref in ((ROWS1, rows1), (ROWS3, rows3), (OUT, out_ref), (GRAD1, grad1), (INPUT, input_ref)):
+    left(ROWS3, rows3.at[seven, pl.ds(0, half)])
+    for phase, ref in ((ROWS1, rows1), (OUT, out_ref), (GRAD1, grad1), (INPUT, input_ref)):
         left(phase, ref.at[seven])
     for phase, at in ((DENSE, 1), (BACK1, 4)):
         left(phase, sends.at[at, seven])
@@ -920,9 +973,14 @@
         left(CORE + j, cr.at[pl.ds(0, block)])
     left(RETURN, rb.at[pl.ds(0, experts - 1)])
     left(SMALL_A, small_recv.at[pl.ds(0, group - 1)])
-    left(SMALL_A2, small2_recv.at[pl.ds(0, experts - 1)])
-    left(SMALL_B, smallb_recv.at[pl.ds(0, experts - 1)])
+    three = pl.ds(0, side_size - 1)
+    left(SMALL_A2, small2_recv.at[three])
+    left(SMALL_A3, small3_recv.at[three])
+    left(SMALL_B, smallb_recv.at[three])
+    left(SMALL_B3, smallb3_recv.at[three])
     left(SMALL_B2, smallb2_recv.at[pl.ds(0, mps - 1)])
+    for copy in staged[6:9] + staged[16:]:
+        copy.wait()
     scopes.close()
 
 
@@ -1054,9 +1112,13 @@
         held(32, width),
         held(group, 32, width),
         held(32, width),
-        held(experts, 32, width),
+        held(side, 32, width),
+        held(32, width),
+        held(side, 32, width),
         exact(8, width),
-        exact(experts, 8, width),
+        exact(side, 8, width),
+        exact(8, width),
+        exact(side, 8, width),
         exact(8, width),
         exact(mps, 8, width),
         held(9, width, 128),
@@ -1082,8 +1144,20 @@
         held(width, ff),
         held(width, ff),
         held(ff, width),
-        pltpu.SemaphoreType.DMA((9,)),
+        pltpu.SemaphoreType.DMA((20,)),
         held(128, width),
+        held(rows, width),
+        held(rows, width),
+        held(local, width),
+        held(local, width),
+        held(local, width),
+        held(local, width),
+        held(experts, width),
+        held(rows, width),
+        held(rows, width),
+        held(6, 4 * local, 128),
+        held(9, width, 128),
+        exact(every, ff),
     ]
     shape = jax.ShapeDtypeStruct
     block_output, input_grad, attn, dense, ge_gate, ge_up, ge_down, small, bias_grad = pl.pallas_call(
@@ -1099,8 +1173,8 @@
             shape((32, width), F32),
             shape((heads, 1, buckets), F32),
         ),
-        in_specs=[vmem] * 12 + [hbm] * 6,
-        out_specs=(vmem,) * 4 + (hbm,) * 3 + (vmem,) * 2,
+        in_specs=[hbm] * 2 + [vmem] * 5 + [hbm] * 11,
+        out_specs=(hbm,) * 7 + (vmem,) * 2,
         scratch_shapes=scratch,
         compiler_params=pltpu.CompilerParams(
             collective_id=0, has_side_effects=True, vmem_limit_bytes=60 * 1024 * 1024

time: 173 us -> 164 us (0.948)
  Pallas kernels: 171 us -> 163 us
    pallas_call x1, Pallas kernels: 164 us -> 156 us  [shards(): pl.pallas_call(functools.partial(kernel, c), out_shape=(shape((rows, widt...]
where the time goes in v5:
time: 164 us
  Pallas kernels  163 us (99%)
    pallas_call x1, Pallas kernels, shards(): pl.pallas_call(functools.partial(kernel, c), out_shape=(shape((rows, widt...  156 us
    pallas_call x1, Pallas kernels, shards(): pl.pallas_call(functools.partial(widen, tiles, experts), grid=(steps,), o...  7.15 us

profile of v5, /device:TPU:0, one launch (start us, length us, event | category | flops | bytes accessed | tf_op | source)
XLA Modules:
  0.0 163.6 jit_solution(16011070724482651616)
XLA Ops:
  0.7 155.6 %shard_map.297 = (bf16[256,768]{1,0:T(8,128)(2,1)}, bf16[256,768]{1,0:T(8,128)(2,1)}, bf16[6,768,128]{2,1,0:T(8,128)(2,1)}, bf16[9,768,128]{2,1,0:T(8,128)(2,1)}...) custom-call(bf16[256,768]{1,0:T(8,128)(2,1)} %bitcast.51, ...), custom_call_target="tpu_custom_call" | custom-call | tf_op jit(solution)/shard_map/pallas_call | solution.py:1163
  156.3 7.2 %shard_map.298 = (f32[256,768]{1,0:T(8,128)}, f32[256,768]{1,0:T(8,128)}, f32[192,768]{1,0:T(8,128)}, f32[192,768]{1,0:T(8,128)}, f32[192,768]{1,0:T(8,128)}, /*...) custom-call(bf16[256,768]{1,0:T(8,128)(2,1)} %get-tuple-element.41.o, ...), custom_call_target="tpu_custom_call" | custom-call | tf_op jit(solution)/shard_map/pallas_call | solution.py:1212

commit v6 on v5

--- a/solution.py
+++ b/solution.py
@@ -793,14 +793,19 @@
         attention_back(grad2, sends.at[3])
         scatter_from(sends.at[3], recv4.at[2], BACK2)
         attention_weights(rows2, grad2)
-        bias_sums()
+
+    def output():
+        arrived(RETURN2, rb2)
+        for m in range(micro):
+            held = rb2[:, m * cap : (m + 1) * cap, :].reshape(experts * cap, half)
+            out_send[m * length : (m + 1) * length] = low(tn(pick0[m] + pick1[m], held))
+        scatter(out_send, out_recv, MOE2)
 
     phase("output")
-    arrived(RETURN2, rb2)
-    for m in range(micro):
-        held = rb2[:, m * cap : (m + 1) * cap, :].reshape(experts * cap, half)
-        out_send[m * length : (m + 1) * length] = low(tn(pick0[m] + pick1[m], held))
-    scatter(out_send, out_recv, MOE2)
+    @pl.when(s == 0)
+    def _():
+        output()
+
     phase("back2_wait")
     wait_from(1, recv4.at[2], BACK2)
     phase("norm2_back")
@@ -810,6 +815,11 @@
     chunk[GRAD] = grad
     grad1[own] = low(grad)
     gather_all(grad1, GRAD1)
+    phase("output1")
+    @pl.when(s == 1)
+    def _():
+        output()
+
     phase("grad1_wait")
     wait_all(grad1, GRAD1)
     phase("dense_back")
@@ -845,11 +855,6 @@
         send(small_send, small_recv.at[place], SMALL_A, in_group(lax.rem(place + k, group)))
     small_recv[place] = small_send[...]
 
-    phase("out")
-    arrived(MOE2, out_recv.at[pl.ds(0, group - 1)])
-    out_ref[own, 0:half] = low(chunk[H2][:, 0:half] + total(out_recv, 0, mps))
-    out_ref[own, half:] = low(chunk[H2][:, half:] + total(out_recv, mps, group))
-    gather_all(out_ref, OUT)
     phase("attention1_back")
     @pl.when(s == 0)
     def _():
@@ -882,9 +887,7 @@
     phase("dense_four")
     dense_sum[3]()
     phase("bias")
-    @pl.when(s == 0)
-    def _():
-        bias_sums()
+    bias_sums()
 
     along(smallb_send, smallb_recv, SMALL_B, True)
     phase("back0_wait")
@@ -893,6 +896,11 @@
     back, gain = normed_back(full(x_ref[own]), gains[0, 0:1], total(recv4.at[3]))
     input_ref[own] = low(chunk[GRAD] + back)
     gather_all(input_ref, INPUT)
+    phase("out")
+    arrived(MOE2, out_recv.at[pl.ds(0, group - 1)])
+    out_ref[own, 0:half] = low(chunk[H2][:, 0:half] + total(out_recv, 0, mps))
+    out_ref[own, half:] = low(chunk[H2][:, half:] + total(out_recv, mps, group))
+    gather_all(out_ref, OUT)
     phase("attn_two")
     @pl.when(s == 0)
     def _():
@@ -1199,7 +1207,7 @@
         expert_up[0],
         expert_down[0],
     )
-    steps = 4
+    steps = 2
 
     def rows_of(rows, width):
         return pl.BlockSpec((rows // steps, width), lambda i: (i, 0))

time: 164 us -> 162 us (0.988)
  Pallas kernels: 163 us -> 161 us
where the time goes in v6:
time: 162 us; the launch traced here: 161 us
  Pallas kernels  161 us (99%)
    pallas_call x1, Pallas kernels, shards(): pl.pallas_call(functools.partial(kernel, c), out_shape=(shape((rows, widt...  154 us
    pallas_call x1, Pallas kernels, shards(): pl.pallas_call(functools.partial(widen, tiles, experts), grid=(steps,), o...  6.21 us

profile of v6, /device:TPU:0, one launch (start us, length us, event | category | flops | bytes accessed | tf_op | source)
XLA Modules:
  0.0 161.4 jit_solution(16266081579263771620)
XLA Ops:
  0.7 154.4 %shard_map.297 = (bf16[256,768]{1,0:T(8,128)(2,1)}, bf16[256,768]{1,0:T(8,128)(2,1)}, bf16[6,768,128]{2,1,0:T(8,128)(2,1)}, bf16[9,768,128]{2,1,0:T(8,128)(2,1)}...) custom-call(bf16[256,768]{1,0:T(8,128)(2,1)} %bitcast.51, ...), custom_call_target="tpu_custom_call" | custom-call | tf_op jit(solution)/shard_map/pallas_call | solution.py:1171
  155.0 6.2 %shard_map.298 = (f32[256,768]{1,0:T(8,128)}, f32[256,768]{1,0:T(8,128)}, f32[192,768]{1,0:T(8,128)}, f32[192,768]{1,0:T(8,128)}, f32[192,768]{1,0:T(8,128)}, /*...) custom-call(bf16[256,768]{1,0:T(8,128)(2,1)} %get-tuple-element.41.o, ...), custom_call_target="tpu_custom_call" | custom-call | tf_op jit(solution)/shard_map/pallas_call | solution.py:1220
